TPU v7x, 128 devices: a whole 4x4x4 slice. The times are simulated.
128 devices in a mesh: dp: 32 (over x, z_hi, y), seq: 4 (over z_lo, core).
Axes of the slice: x: 4, y: 4, z: 4 (z_hi: 2, z_lo: 2; z = z_hi * 2 + z_lo), core: 2. Of those that a mesh axis runs over, the one named last changes fastest.
Arguments:
- hidden: bfloat16 [32768, 5120], P(('dp', 'seq')), may hold values from -24 to 24
- query_base: bfloat16 [32768, 2560], P(('dp', 'seq')), may hold values from -6 to 6
- key_base: bfloat16 [32768, 2560], P(('dp', 'seq')), may hold values from -6 to 6
- value_base: bfloat16 [32768, 2560], P(('dp', 'seq')), may hold values from -6 to 6
- cotangent: bfloat16 [32768, 2560], P(('dp', 'seq')), may hold values from -0.375 to 0.375
- down_query: bfloat16 [5120, 128], replicated, may hold values from -0.078125 to 0.078125
- down_value: bfloat16 [5120, 128], replicated, may hold values from -0.078125 to 0.078125
- up_query: bfloat16 [128, 2560], replicated, may hold values from -0.5 to 0.5
- up_value: bfloat16 [128, 2560], replicated, may hold values from -0.5 to 0.5
- key_blocks: int32 [20, 8, 5], P('seq'), may hold values from 0 to 7, as said below
- block_counts: int32 [20, 8], P('seq'), may hold values from 1 to 5
Outputs:
- attended: bfloat16 [32768, 2560], P(('dp', 'seq'))
- grad_down: float32 [5120, 2, 128], P(('dp', 'seq'))
- grad_up: float32 [128, 2, 2560], P('dp', None, 'seq')
Inputs may be any that keep to these rules, and one draw needn't show every extreme that they name: For head h and query block i the first block_counts[h, i] entries of key_blocks[h, i] are distinct key blocks in rising order; the later entries are valid block numbers and are not attended to.
All inputs are finite; a program needn't handle non-finite values.
Results may differ from a plain program's by a relative error of at most 0.033.
Values may be sent and summed in bfloat16 or wider, within the bound.
No kernel may reach another device: no remote copies, remote signals or barrier semaphores. Data moves between devices by JAX's collectives and lax.ppermute only.
A program may use at most 128 MiB of HBM per device.

v0:
```python
import math

import jax
import jax.numpy as jnp
from jax import lax
from jax.sharding import PartitionSpec as P

HEADS = 20
HD = 128


def head_pass(queries, key_rows, values, upstream, blocks, counts):
    block_total, slot_count = blocks.shape
    head_width = queries.shape[1]
    length = queries.shape[0] // block_total
    score_scale = 1.0 / math.sqrt(head_width)
    query_tiles = queries.reshape(block_total, length, head_width)
    key_tiles = key_rows.reshape(block_total, length, head_width)[blocks].reshape(
        block_total, slot_count * length, head_width
    )
    value_tiles = values.reshape(block_total, length, head_width)[blocks].reshape(
        block_total, slot_count * length, head_width
    )
    upstream_tiles = upstream.reshape(block_total, length, head_width)
    listed = jnp.arange(slot_count)[None, :] < counts[:, None]
    spread_mask = jnp.repeat(listed, length, axis=1)
    scores = (
        jnp.einsum("nqd,nkd->nqk", query_tiles, key_tiles, preferred_element_type=jnp.float32)
        * score_scale
    )
    scores = jnp.where(spread_mask[:, None, :], scores, -1e30)
    row_max = jnp.max(scores, axis=-1, keepdims=True)
    powers = jnp.exp(scores - row_max)
    probability = powers / jnp.sum(powers, axis=-1, keepdims=True)
    weights = probability.astype(jnp.bfloat16)
    attended = jnp.einsum(
        "nqk,nkd->nqd", weights, value_tiles, preferred_element_type=jnp.float32
    ).astype(jnp.bfloat16)
    grad_probs = jnp.einsum(
        "nqd,nkd->nqk", upstream_tiles, value_tiles, preferred_element_type=jnp.float32
    )
    centred = grad_probs - jnp.sum(probability * grad_probs, axis=-1, keepdims=True)
    shifted = (probability * centred).astype(jnp.bfloat16)
    grad_query = (
        jnp.einsum("nqk,nkd->nqd", shifted, key_tiles, preferred_element_type=jnp.float32)
        * score_scale
    ).astype(jnp.bfloat16)
    pieces = jnp.einsum(
        "nqk,nqd->nkd", weights, upstream_tiles, preferred_element_type=jnp.float32
    ).reshape(block_total, slot_count, length, head_width)
    chooser = (
        (blocks[:, :, None] == jnp.arange(block_total)[None, None, :]) & listed[:, :, None]
    ).astype(jnp.float32)
    grad_value = jnp.einsum(
        "nsj,nsbd->jbd", chooser, pieces, precision=lax.Precision.HIGHEST
    ).astype(jnp.bfloat16)
    return (
        attended.reshape(-1, head_width),
        grad_query.reshape(-1, head_width),
        grad_value.reshape(-1, head_width),
    )


def all_heads(queries, key_rows, values, upstream, key_blocks, block_counts):
    local_heads = queries.shape[1]
    empty = jnp.zeros_like(queries)

    def one_head(head_index, buffers):

        def take_head(array):
            return lax.dynamic_index_in_dim(array, head_index, 1, keepdims=False)

        results = head_pass(
            take_head(queries),
            take_head(key_rows),
            take_head(values),
            take_head(upstream),
            lax.dynamic_index_in_dim(key_blocks, head_index, 0, keepdims=False),
            lax.dynamic_index_in_dim(block_counts, head_index, 0, keepdims=False),
        )
        return tuple(
            (
                lax.dynamic_update_index_in_dim(buffer, result, head_index, 1)
                for buffer, result in zip(buffers, results)
            )
        )

    return lax.fori_loop(0, local_heads, one_head, (empty, empty, empty))


def per_device(
    hidden,
    query_base,
    key_base,
    value_base,
    cotangent,
    down_query,
    down_value,
    up_query,
    up_value,
    key_blocks,
    block_counts,
):
    tok_rows = hidden.shape[0]
    low_query = jnp.dot(hidden, down_query, preferred_element_type=jnp.float32).astype(jnp.bfloat16)
    low_value = jnp.dot(hidden, down_value, preferred_element_type=jnp.float32).astype(jnp.bfloat16)

    def as_heads(array):
        return array.reshape(tok_rows, HEADS, HD)

    queries = (
        query_base.astype(jnp.float32)
        + jnp.dot(low_query, up_query, preferred_element_type=jnp.float32)
    ).astype(jnp.bfloat16)
    values = (
        value_base.astype(jnp.float32)
        + jnp.dot(low_value, up_value, preferred_element_type=jnp.float32)
    ).astype(jnp.bfloat16)
    head_queries, head_keys, head_values, head_upstream = (
        lax.all_to_all(as_heads(queries), "seq", split_axis=1, concat_axis=0, tiled=True),
        lax.all_to_all(as_heads(key_base), "seq", split_axis=1, concat_axis=0, tiled=True),
        lax.all_to_all(as_heads(values), "seq", split_axis=1, concat_axis=0, tiled=True),
        lax.all_to_all(as_heads(cotangent), "seq", split_axis=1, concat_axis=0, tiled=True),
    )
    attended_heads, query_grads, value_grads = all_heads(
        head_queries, head_keys, head_values, head_upstream, key_blocks, block_counts
    )
    attended = lax.all_to_all(
        attended_heads, "seq", split_axis=0, concat_axis=1, tiled=True
    ).reshape(tok_rows, HEADS * HD)
    token_query, token_value = (
        lax.all_to_all(query_grads, "seq", split_axis=0, concat_axis=1, tiled=True),
        lax.all_to_all(value_grads, "seq", split_axis=0, concat_axis=1, tiled=True),
    )
    token_query = token_query.reshape(tok_rows, HEADS * HD)
    token_value = token_value.reshape(tok_rows, HEADS * HD)
    up_terms = jnp.stack(
        [
            jnp.einsum("tr,tc->rc", low_query, token_query, preferred_element_type=jnp.float32),
            jnp.einsum("tr,tc->rc", low_value, token_value, preferred_element_type=jnp.float32),
        ],
        axis=1,
    )
    up_local = lax.psum_scatter(
        up_terms.astype(jnp.bfloat16), "seq", scatter_dimension=2, tiled=True
    )
    low_grads = jnp.stack(
        [
            jnp.einsum("tc,rc->tr", token_query, up_query, preferred_element_type=jnp.float32),
            jnp.einsum("tc,rc->tr", token_value, up_value, preferred_element_type=jnp.float32),
        ],
        axis=1,
    ).astype(jnp.bfloat16)
    grad_up = lax.psum_scatter(up_local, "dp", scatter_dimension=0, tiled=True).astype(jnp.float32)
    grad_down = lax.psum_scatter(
        jnp.einsum("td,tkr->dkr", hidden, low_grads, preferred_element_type=jnp.float32),
        ("dp", "seq"),
        scatter_dimension=0,
        tiled=True,
    )
    return (attended, grad_down, grad_up)


def solution(mesh):
    placed = (
        P(("dp", "seq"), None),
        P(("dp", "seq"), None),
        P(("dp", "seq"), None),
        P(("dp", "seq"), None),
        P(("dp", "seq"), None),
        P(),
        P(),
        P(),
        P(),
        P("seq", None, None),
        P("seq", None),
    )
    return jax.shard_map(
        per_device,
        mesh=mesh,
        in_specs=placed,
        out_specs=(P(("dp", "seq"), None), P(("dp", "seq"), None, None), P("dp", None, "seq")),
        check_vma=False,
    )
```

profile of v0, /device:TPU:0, one launch (start us, length us, event | category | flops | bytes accessed | tf_op | source)
XLA Modules:
  0.0 826.5 jit_solution(10097324528635032722)
XLA Ops:
  15.9 4.3 all-to-all-start.2
  26.5 11.0 %all-to-all-done.2 = bf16[256,20,128]{0,2,1:T(8,128)(2,1)} async-done(((bf16[256,20,128]{0,2,1:T(8,128)(2,1)}), bf16[256,20,128]{0,2,1:T(8,128)(2,1)}, u32[]{:S(2)}, u32[]{:S(2)}) %all-to-all-start.2) | async-done | bytes 1310752 | tf_op jit(solution)/shard_map/all_to_all | solution.py:122
  37.5 4.3 all-to-all-start
  44.3 14.9 %all-to-all-done = bf16[256,20,128]{0,2,1:T(8,128)(2,1)} async-done(((bf16[256,20,128]{0,2,1:T(8,128)(2,1)}), bf16[256,20,128]{0,2,1:T(8,128)(2,1)}, u32[]{:S(2)}, u32[]{:S(2)}) %all-to-all-start) | async-done | bytes 1310752 | tf_op jit(solution)/shard_map/all_to_all | solution.py:120
  59.2 4.3 all-to-all-start.1
  65.9 14.9 %all-to-all-done.1 = bf16[256,20,128]{0,2,1:T(8,128)(2,1)} async-done(((bf16[256,20,128]{0,2,1:T(8,128)(2,1)}), bf16[256,20,128]{0,2,1:T(8,128)(2,1)}, u32[]{:S(2)}, u32[]{:S(2)}) %all-to-all-start.1) | async-done | bytes 1310752 | tf_op jit(solution)/shard_map/all_to_all | solution.py:121
  80.8 4.5 all-to-all-start.3
  92.6 9.8 %all-to-all-done.3 = bf16[256,20,128]{0,2,1:T(8,128)(2,1)} async-done(((bf16[256,20,128]{0,2,1:T(8,128)(2,1)}), bf16[256,20,128]{0,2,1:T(8,128)(2,1)}, u32[]{:S(2)}, u32[]{:S(2)}) %all-to-all-start.3) | async-done | bytes 1310752 | tf_op jit(solution)/shard_map/all_to_all | solution.py:123
  104.9 127.3 %while.17 = (s32[]{:T(128)}, bf16[1024,5,128]{2,0,1:T(8,128)(2,1)}, bf16[1024,5,128]{2,0,1:T(8,128)(2,1)}, bf16[1024,5,128]{2,0,1:T(8,128)(2,1)}, s32[5,8]{1,0:T...) while((s32[]{:T(128)}, bf16[1024,5,128]{2,0,1:T(8,128)(2,1)}, ...), condition=%wide.region_4.5_spmd, body=%wide.region_0.4_spmd.sunk | while | flops 912131456 | bytes 61912728 | solution.py:88
  115.8 3.9 fusion.95
  126.2 3.3 fusion.98
  141.3 3.9 fusion.95
  151.6 3.3 fusion.98
  166.8 3.9 fusion.95
  192.2 3.9 fusion.95
  217.7 3.9 fusion.95
  232.2 3.6 copy.93
  235.8 4.5 all-to-all-start.6
  240.3 3.6 copy.90
  243.8 22.2 %all-to-all-done.6 = bf16[1024,5,128]{2,1,0:T(8,128)(2,1)} async-done(((bf16[1024,5,128]{2,1,0:T(8,128)(2,1)}), bf16[1024,5,128]{2,1,0:T(8,128)(2,1)}, u32[]{:S(2)}, u32[]{:S(2)}) %all-to-all-start.6) | async-done | bytes 1310752 | tf_op jit(solution)/shard_map/all_to_all | solution.py:133
  266.0 4.5 all-to-all-start.5
  270.8 4.0 copy.95
  276.7 19.6 %all-to-all-done.5 = bf16[1024,5,128]{2,1,0:T(8,128)(2,1)} async-done(((bf16[1024,5,128]{2,1,0:T(8,128)(2,1)}), bf16[1024,5,128]{2,1,0:T(8,128)(2,1)}, u32[]{:S(2)}, u32[]{:S(2)}) %all-to-all-start.5) | async-done | bytes 1310752 | tf_op jit(solution)/shard_map/all_to_all | solution.py:132
  296.3 4.1 copy.92
  303.4 4.3 copy.110
  317.1 8.7 %copy.97 = f32[5120,2,128]{2,1,0:T(2,128)} copy(f32[5120,2,128]{0,2,1:T(8,128)} %convolution_bitcast_fusion) | data formatting | bytes 10485760 | tf_op jit(solution)/shard_map/td,tkr->dkr/dot_general | solution.py:156
  325.9 3.6 copy.87
  329.5 4.5 all-to-all-start.4
  338.4 29.6 %all-to-all-done.4 = bf16[1024,5,128]{2,1,0:T(8,128)(2,1)} async-done(((bf16[1024,5,128]{2,1,0:T(8,128)(2,1)}), bf16[1024,5,128]{2,1,0:T(8,128)(2,1)}, u32[]{:S(2)}, u32[]{:S(2)}) %all-to-all-start.4) | async-done | bytes 1310752 | tf_op jit(solution)/shard_map/all_to_all | solution.py:128
  368.0 4.1 copy.89
  374.5 112.7 %all-reduce.5.cloned.1.call-done = f32[5120,2,128]{2,1,0:T(2,128)} async-done(((f32[5120,2,128]{2,1,0:T(2,128)}), f32[5120,2,128]{2,1,0:T(2,128)}) %all-reduce.5.cloned.1.call-update) | async-done | bytes 5242896
  488.6 329.1 %all-reduce.7.cloned.1.call-done = bf16[128,2,640]{2,0,1:T(8,128)(2,1)} async-done(((bf16[128,2,640]{2,0,1:T(8,128)(2,1)}), bf16[128,2,640]{2,0,1:T(8,128)(2,1)}) %all-reduce.7.cloned.1.call-update) | async-done | bytes 327696
  (237 shorter events, 153.4 us)
Async XLA Ops:
  8.0 3.9 copy-start.5
  8.0 3.9 copy-start.9
  15.9 21.6 %all-to-all-start.2 = ((bf16[256,20,128]{0,2,1:T(8,128)(2,1)}), bf16[256,20,128]{0,2,1:T(8,128)(2,1)}, u32[]{:S(2)}, u32[]{:S(2)}) async-start(bf16[256,20,128]{0,2,1:T(8,128)(2,1)} %bitcast.175), calls=%async_computation.2 | async-start | bytes 2621440 | tf_op jit(solution)/shard_map/all_to_all | solution.py:122
  20.2 2.3 copy-start.7
  20.2 2.3 copy-start.10
  37.5 21.7 %all-to-all-start = ((bf16[256,20,128]{0,2,1:T(8,128)(2,1)}), bf16[256,20,128]{0,2,1:T(8,128)(2,1)}, u32[]{:S(2)}, u32[]{:S(2)}) async-start(bf16[256,20,128]{0,2,1:T(8,128)(2,1)} %bitcast.173), calls=%async_computation | async-start | bytes 2621440 | tf_op jit(solution)/shard_map/all_to_all | solution.py:120
  59.2 21.6 %all-to-all-start.1 = ((bf16[256,20,128]{0,2,1:T(8,128)(2,1)}), bf16[256,20,128]{0,2,1:T(8,128)(2,1)}, u32[]{:S(2)}, u32[]{:S(2)}) async-start(bf16[256,20,128]{0,2,1:T(8,128)(2,1)} %bitcast.174), calls=%async_computation.1 | async-start | bytes 2621440 | tf_op jit(solution)/shard_map/all_to_all | solution.py:121
  80.8 21.6 %all-to-all-start.3 = ((bf16[256,20,128]{0,2,1:T(8,128)(2,1)}), bf16[256,20,128]{0,2,1:T(8,128)(2,1)}, u32[]{:S(2)}, u32[]{:S(2)}) async-start(bf16[256,20,128]{0,2,1:T(8,128)(2,1)} %bitcast.172), calls=%async_computation.3 | async-start | bytes 2621440 | tf_op jit(solution)/shard_map/all_to_all | solution.py:123
  105.6 2.8 copy-start.11
  119.7 3.6 copy-start.2
  119.7 3.6 copy-start.14
  131.1 2.8 copy-start.11
  145.2 3.6 copy-start.2
  145.2 3.6 copy-start.14
  156.6 2.8 copy-start.11
  170.6 3.6 copy-start.2
  170.6 3.6 copy-start.14
  182.0 2.8 copy-start.11
  196.1 3.6 copy-start.2
  196.1 3.6 copy-start.14
  207.5 2.8 copy-start.11
  221.6 3.6 copy-start.2
  221.6 3.6 copy-start.14
  235.8 30.2 %all-to-all-start.6 = ((bf16[1024,5,128]{2,1,0:T(8,128)(2,1)}), bf16[1024,5,128]{2,1,0:T(8,128)(2,1)}, u32[]{:S(2)}, u32[]{:S(2)}) async-start(bf16[1024,5,128]{2,1,0:T(8,128)(2,1)} %copy.93), calls=%async_computation.6 | async-start | bytes 4194304 | tf_op jit(solution)/shard_map/all_to_all | solution.py:133
  266.0 30.2 %all-to-all-start.5 = ((bf16[1024,5,128]{2,1,0:T(8,128)(2,1)}), bf16[1024,5,128]{2,1,0:T(8,128)(2,1)}, u32[]{:S(2)}, u32[]{:S(2)}) async-start(bf16[1024,5,128]{2,1,0:T(8,128)(2,1)} %copy.90), calls=%async_computation.5 | async-start | bytes 4194304 | tf_op jit(solution)/shard_map/all_to_all | solution.py:132
  270.5 64.1 %reduce-scatter.5.cloned.1.call-start = ((), (), s32[]{:S(2)}) async-start(), calls=%async_computation.8 | async-start | bytes 1638400
  310.3 177.0 %all-reduce.5.cloned.1.call-start = ((), (), s32[]{:S(2)}) async-start(), calls=%async_computation.9 | async-start | bytes 10485760
  311.3 2.0 copy-start.3
  311.3 2.0 copy-start.8
  329.5 38.5 %all-to-all-start.4 = ((bf16[1024,5,128]{2,1,0:T(8,128)(2,1)}), bf16[1024,5,128]{2,1,0:T(8,128)(2,1)}, u32[]{:S(2)}, u32[]{:S(2)}) async-start(bf16[1024,5,128]{2,1,0:T(8,128)(2,1)} %copy.87), calls=%async_computation.4 | async-start | bytes 4194304 | tf_op jit(solution)/shard_map/all_to_all | solution.py:128
  334.0 3.2 copy-start.13
  334.0 483.7 %all-reduce.7.cloned.1.call-start = ((), (), s32[]{:S(2)}) async-start(), calls=%async_computation.10 | async-start | bytes 655360
  (17 other events, 23.3 us)
Sparse Core Ops, SparseCore 0:
  310.4 24.1 reduce-scatter.4
Sparse Core Ops, SparseCore 1:
  326.0 161.2 all-reduce.4
  489.6 328.1 all-reduce.6
where the time goes:
time: 830 us; the launch traced here: 827 us
  waiting for transfers between devices  564 us (68%)
  local copies, waits for them, and re-layouts  134 us (16%)
  matrix products  78.3 us (9%)
  starting transfers between devices  31.1 us (4%)
  between operations  16.4 us (2%)
    unnamed x6, waiting for transfers between devices  442 us
    all_to_all x1, waiting for transfers between devices, per_device(): lax.all_to_all(attended_heads, 'seq', split_axis=0, concat_axis=1, tiled=...  29.6 us
    dynamic_slice x20, local copies, waits for them, and re-layouts, take_head(): return lax.dynamic_index_in_dim(array, head_index, 1, keepdims=False)  23 us
    all_to_all x1, waiting for transfers between devices, per_device(): lax.all_to_all(value_grads, 'seq', split_axis=0, concat_axis=1, tiled=True)  22.2 us
    unnamed x28, local copies, waits for them, and re-layouts  22 us
    all_to_all x1, waiting for transfers between devices, per_device(): lax.all_to_all(query_grads, 'seq', split_axis=0, concat_axis=1, tiled=True)  19.6 us
    sub x5, matrix products, head_pass(): powers = jnp.exp(scores - row_max)  19.3 us
  transfers between devices with their start and end apart: 10, of which 10 were waited for; matrix products, arithmetic and copies ran while one was open for 7% of the time, Pallas kernels for 0%

commit v1 on v0

v1 whole, which is shorter than its diff:
```python
import functools
import math

import jax
import jax.numpy as jnp
from jax import lax
from jax.experimental import pallas as pl
from jax.experimental.pallas import tpu as pltpu
from jax.sharding import Mesh
from jax.sharding import PartitionSpec as P

HEADS = 20
HD = 128
R = 128
NB = 8
ROWS = 256
K_CHUNKS = ((0, 10), (10, 10))
V_CHUNKS = ((0, 5), (5, 5), (10, 5), (15, 5))
SCALE = 1.0 / math.sqrt(HD)
SCALE2 = SCALE * math.log2(math.e)
F32 = jnp.float32
BF16 = jnp.bfloat16


def nn(a, b):
    return lax.dot_general(a, b, (((1,), (0,)), ((), ())), preferred_element_type=F32)


def nt(a, b):
    return lax.dot_general(a, b, (((1,), (1,)), ((), ())), preferred_element_type=F32)


def tn(a, b):
    return lax.dot_general(a, b, (((0,), (0,)), ((), ())), preferred_element_type=F32)


def weight_kernel(
    h0, bias_ref, qb_ref, lowq_ref, upq_ref, cot_ref, upv_ref, k0, k1, k2, k3, wt_ref, g_ref, lgv_ref
):
    step = pl.program_id(0)
    query = (qb_ref[...].astype(F32) + nn(lowq_ref[...], upq_ref[...])).astype(BF16)
    g = nt(cot_ref[...], upv_ref[...]).astype(BF16)
    g_ref[...] = g
    first_half = lax.broadcasted_iota(jnp.int32, (1, ROWS), 1) < ROWS // 2
    parts = []
    for r, key_ref in enumerate((k0, k1, k2, k3)):
        s = nt(key_ref[...], query) * SCALE2
        for b in range(2):
            j = 2 * r + b
            bias = jnp.where(first_half, bias_ref[h0 + step, j], bias_ref[h0 + step, NB + j])
            parts.append(s[b * 128 : (b + 1) * 128] + bias)
    top = functools.reduce(jnp.maximum, [jnp.max(z, axis=0, keepdims=True) for z in parts])
    parts = [jnp.exp2(z - top) for z in parts]
    total = functools.reduce(jnp.add, [jnp.sum(z, axis=0, keepdims=True) for z in parts])
    inverse = 1.0 / total
    for j, z in enumerate(parts):
        wt_ref[0, j * 128 : (j + 1) * 128, :] = (z * inverse).astype(BF16)

    @pl.when(step == 0)
    def _():
        lgv_ref[...] = jnp.zeros_like(lgv_ref)

    for r in range(4):
        lgv_ref[r] += nn(wt_ref[0, r * ROWS : (r + 1) * ROWS, :], g)


def grad_kernel(
    aliased,
    wt_ref, k0, k1, k2, k3, v0, v1, v2, v3, l0, l1, l2, l3, cot_ref, g_ref, upq_ref, upv_ref, lowqt_ref, *rest
):
    att_ref, gu_ref, lgq_ref = rest[1:] if aliased else rest
    step = pl.program_id(0)
    cot = cot_ref[...]
    cot_g = jnp.concatenate([cot, g_ref[...]], axis=1)
    out_t = jnp.zeros((HD + R, ROWS), F32)
    dot_sum = jnp.zeros((1, ROWS), F32)
    backs = []
    for r, (v_ref, l_ref) in enumerate(((v0, l0), (v1, l1), (v2, l2), (v3, l3))):
        vl = jnp.concatenate([v_ref[...], l_ref[...]], axis=1)
        w = wt_ref[0, r * ROWS : (r + 1) * ROWS, :]
        back = nt(vl, cot_g)
        dot_sum += jnp.sum(w.astype(F32) * back, axis=0, keepdims=True)
        out_t += tn(vl, w)
        backs.append(back)
    dq_t = jnp.zeros((HD, ROWS), F32)
    for r, key_ref in enumerate((k0, k1, k2, k3)):
        w = wt_ref[0, r * ROWS : (r + 1) * ROWS, :].astype(F32)
        shifted = (w * (backs[r] - dot_sum)).astype(BF16)
        dq_t += tn(key_ref[...], shifted)
    dq_t = (dq_t * SCALE).astype(BF16)
    t1_t = out_t[HD:].astype(BF16)
    att_t = out_t[:HD] + tn(upv_ref[...], t1_t)
    att_ref[...] = att_t.T.astype(BF16)
    gu_ref[0, 0] = nt(lowqt_ref[...], dq_t).astype(BF16)
    gu_ref[0, 1] = nn(t1_t, cot).astype(BF16)

    @pl.when(step == 0)
    def _():
        lgq_ref[...] = jnp.zeros_like(lgq_ref)

    lgq_ref[...] += nn(upq_ref[...], dq_t)


def col(off):
    return pl.BlockSpec((ROWS, HD), lambda h: (0, h + off))


def colup(off):
    return pl.BlockSpec((R, HD), lambda h: (0, h + off))


def const(shape):
    return pl.BlockSpec(shape, lambda h: (0,) * len(shape))


def params():
    return pltpu.CompilerParams(dimension_semantics=("arbitrary",), vmem_limit_bytes=48 * 2**20)


def weight_call(h0, nh, bias, query_base, lowq, upq, cot, upv, own, sib, zs, zd):
    return pl.pallas_call(
        functools.partial(weight_kernel, h0),
        grid=(nh,),
        in_specs=[
            pl.BlockSpec(memory_space=pltpu.SMEM),
            col(h0), const((ROWS, R)), colup(h0), col(h0), colup(h0),
            col(h0), col(h0), col(0), col(0),
        ],
        out_specs=[
            pl.BlockSpec((1, 4 * ROWS, ROWS), lambda h: (h, 0, 0)),
            col(0),
            const((4, ROWS, R)),
        ],
        out_shape=[
            jax.ShapeDtypeStruct((nh, 4 * ROWS, ROWS), BF16),
            jax.ShapeDtypeStruct((ROWS, nh * HD), BF16),
            jax.ShapeDtypeStruct((4, ROWS, R), F32),
        ],
        compiler_params=params(),
        cost_estimate=pl.CostEstimate(
            flops=nh * 6 * 1024 * 256 * 128, bytes_accessed=nh * 1200000, transcendentals=nh * 1024 * 256
        ),
        name="attention_weights",
    )(bias, query_base, lowq, upq, cot, upv, own, sib, zs, zd)


def grad_call(h0, nh, kh0, kz, att, wt, k_own, k_sib, v_own, v_sib, vz, lows, cot, g, upq, upv, lowqt):
    aliased = att is not None
    args = [wt, k_own, k_sib, *kz, v_own, v_sib, *vz, *lows, cot, g, upq, upv, lowqt]
    off = h0 - kh0
    specs = [
        pl.BlockSpec((1, 4 * ROWS, ROWS), lambda h: (h + off, 0, 0)),
        col(h0), col(h0), col(off), col(off),
        col(h0), col(h0), col(0), col(0),
        *([const((ROWS, R))] * 4),
        col(h0), col(off), colup(h0), colup(h0), const((R, ROWS)),
    ]
    if aliased:
        args.append(att)
        specs.append(pl.BlockSpec(memory_space=pl.ANY))
    return pl.pallas_call(
        functools.partial(grad_kernel, aliased),
        grid=(nh,),
        in_specs=specs,
        out_specs=[
            col(h0),
            pl.BlockSpec((1, 2, R, HD), lambda h: (h, 0, 0, 0)),
            const((R, ROWS)),
        ],
        out_shape=[
            jax.ShapeDtypeStruct((ROWS, HEADS * HD), BF16),
            jax.ShapeDtypeStruct((nh, 2, R, HD), BF16),
            jax.ShapeDtypeStruct((R, ROWS), F32),
        ],
        input_output_aliases={len(args) - 1: 0} if aliased else {},
        compiler_params=params(),
        cost_estimate=pl.CostEstimate(
            flops=nh * 10 * 1024 * 256 * 128, bytes_accessed=nh * 1200000, transcendentals=0
        ),
        name="attention_grads",
    )(*args)


CORE_SWAP = [(0, 1), (1, 0)]


def over_core(a):
    return lax.ppermute(a, "core", CORE_SWAP)


def over_z(a):
    return lax.ppermute(a, "zl", CORE_SWAP)


def per_device(
    hidden, query_base, key_base, value_base, cotangent,
    down_query, down_value, up_query, up_value, key_blocks, block_counts,
):
    dp = lax.axis_size("dp")
    core = lax.axis_index("core")
    me = lax.axis_index("zl") * 2 + core

    def columns(a, h0, nh):
        return a[:, h0 * HD : (h0 + nh) * HD]

    k_zs = [over_z(columns(key_base, *c)) for c in K_CHUNKS]
    v_zs = [over_z(columns(value_base, *c)) for c in V_CHUNKS]
    k_sib = over_core(key_base)
    v_sib = over_core(value_base)
    k_zd = [over_core(a) for a in k_zs]
    v_zd = [over_core(a) for a in v_zs]

    listed = jnp.arange(key_blocks.shape[2])[None, None, :] < block_counts[:, :, None]
    allowed = jnp.any(
        (key_blocks[..., None] == jnp.arange(NB)) & listed[..., None], axis=2
    )
    bias = jnp.where(allowed, 0.0, -1e30).astype(F32)
    bias = lax.all_gather(bias, ("zl", "core"), axis=0, tiled=True)
    bias = lax.dynamic_slice_in_dim(bias, me * 2, 2, axis=1)
    source = (me ^ (jnp.arange(NB) // 2)) * 2 + jnp.arange(NB) % 2
    bias = jnp.sum(
        jnp.where(source[:, None] == jnp.arange(NB), bias[:, :, None, :], 0.0), axis=3
    ).reshape(HEADS, 2 * NB)

    low_query = nn(hidden, down_query).astype(BF16)
    low_value = nn(hidden, down_value).astype(BF16)
    lv_zs = over_z(low_value)
    lows = [low_value, over_core(low_value), lv_zs, over_core(lv_zs)]

    weights, gs, lgv = [], [], 0.0
    for (h0, nh), zs, zd in zip(K_CHUNKS, k_zs, k_zd):
        wt, g, part = weight_call(
            h0, nh, bias, query_base, low_query, up_query, cotangent, up_value, key_base, k_sib, zs, zd
        )
        weights.append(wt)
        gs.append(g)
        lgv = lgv + part

    near = lgv[0::2]
    chip = near + over_core(lgv[1::2].astype(BF16)).astype(F32)
    low_grad_value = chip[0] + over_z(chip[1].astype(BF16)).astype(F32)

    low_query_t = low_query.T
    att, gus, lgq = None, [], 0.0
    for (h0, nh), zs, zd in zip(V_CHUNKS, v_zs, v_zd):
        which = [i for i, (a, n) in enumerate(K_CHUNKS) if a <= h0 < a + n][0]
        att, gu, part = grad_call(
            h0, nh, K_CHUNKS[which][0], (k_zs[which], k_zd[which]), att, weights[which],
            key_base, k_sib, value_base, v_sib, (zs, zd), lows,
            cotangent, gs[which], up_query, up_value, low_query_t,
        )
        gus.append(gu)
        lgq = lgq + part

    low_grads = jnp.concatenate([lgq.T.astype(BF16), low_grad_value.astype(BF16)], axis=1)
    down = lax.dot_general(
        hidden, low_grads, (((0,), (0,)), ((), ())), preferred_element_type=F32
    ).astype(BF16)
    rows = hidden.shape[1] // (4 * dp)
    down = down.reshape(2 * dp, 2, rows, 2 * R)
    ups = [
        g.reshape(5, 2, dp, R // dp, HD).transpose(2, 0, 1, 3, 4).reshape(dp, -1, HD) for g in gus
    ]
    ups = jnp.stack(
        [jnp.stack([ups[0], ups[2]], axis=1), jnp.stack([ups[1], ups[3]], axis=1)], axis=0
    ).reshape(2, 2 * dp, -1, HD)
    down_mine = lax.dynamic_index_in_dim(down, core, 1, keepdims=False)
    down_other = lax.dynamic_index_in_dim(down, 1 - core, 1, keepdims=False)
    up_mine = lax.dynamic_index_in_dim(ups, core, 0, keepdims=False)
    up_other = lax.dynamic_index_in_dim(ups, 1 - core, 0, keepdims=False)
    down_sum = (down_mine.astype(F32) + over_core(down_other).astype(F32)).astype(BF16)
    up_sum = (up_mine.astype(F32) + over_core(up_other).astype(F32)).astype(BF16)
    n_up = up_sum.shape[1]
    payload = jnp.concatenate([down_sum.reshape(2 * dp, 2 * rows, R), up_sum], axis=1)
    landed = lax.all_to_all(payload, ("dp", "zl"), 0, 0, tiled=True)
    total = jnp.sum(landed.astype(F32), axis=0)
    grad_down = total[: 2 * rows].reshape(rows, 2, R)
    grad_up = (
        total[2 * rows :].reshape(5, 2, R // dp, HD).transpose(2, 1, 0, 3).reshape(R // dp, 2, 5 * HD)
    )
    return att, grad_down, grad_up


def solution(mesh):
    fine = Mesh(mesh.devices.reshape(-1, 2, 2), ("dp", "zl", "core"))
    everyone = ("dp", "zl", "core")
    tokens = P(everyone, None)
    return jax.shard_map(
        per_device,
        mesh=fine,
        in_specs=(
            tokens, tokens, tokens, tokens, tokens, P(), P(), P(), P(),
            P(("zl", "core"), None, None), P(("zl", "core"), None),
        ),
        out_specs=(tokens, P(everyone, None, None), P("dp", None, ("zl", "core"))),
        check_vma=False,
    )
```

time: 830 us -> 197 us (0.24)
  waiting for transfers between devices: 564 us -> 27 us
  local copies, waits for them, and re-layouts: 134 us -> 35.7 us
  matrix products: 78.3 us -> 5.62 us
  Pallas kernels: 0 us -> 57.1 us
  blocking collectives: 0 us -> 45.4 us
  starting transfers between devices: 31.1 us -> 13 us
  between operations: 16.4 us -> 0.93 us
  other arithmetic: 2.04 us -> 11.1 us
    unnamed x6 -> x0, waiting for transfers between devices: 442 us -> none
    all_to_all x7 -> x0, waiting for transfers between devices: 122 us -> none  [the longest x1 29.6 us: per_device(): lax.all_to_all(attended_heads, 'seq', split_axis=0, concat_axis=1, tiled=...]
    pallas_call x0 -> x6, Pallas kernels: none -> 57.1 us  [the longest x4 32.2 us: grad_call(): pl.pallas_call(functools.partial(grad_kernel, aliased), grid=(nh,), in_sp...]
    dot_general x34 -> x3, matrix products: 59 us -> 5.62 us  [the longest x2 3.24 us: nn(): lax.dot_general(a, b, (((1,), (0,)), ((), ())), preferred_element_type=F32)]
    all_to_all x0 -> x1, blocking collectives: none -> 39.9 us  [per_device(): landed = lax.all_to_all(payload, ('dp', 'zl'), 0, 0, tiled=True)]
    all_to_all x7 -> x0, starting transfers between devices: 30.8 us -> none  [the longest x1 4.48 us: per_device(): lax.all_to_all(as_heads(cotangent), 'seq', split_axis=1, concat_axis=0, t...]
    ppermute x0 -> x21, waiting for transfers between devices: none -> 27 us  [the longest x8 24.9 us: over_z(): return lax.ppermute(a, 'zl', CORE_SWAP)]
    dynamic_slice x30 -> x2, local copies, waits for them, and re-layouts: 26.9 us -> 1.42 us  [per_device(): bias = lax.dynamic_slice_in_dim(bias, me * 2, 2, axis=1)]
  transfers between devices with their start and end apart: 10 -> 21, of which waited for: 10 -> 5; matrix products, arithmetic and copies ran while one was open for 7% -> 12% of each run, Pallas kernels for 0% -> 29%
where the time goes in v1:
time: 197 us; the launch traced here: 196 us
  Pallas kernels  57.1 us (29%)
  blocking collectives  45.4 us (23%)
  local copies, waits for them, and re-layouts  35.7 us (18%)
  waiting for transfers between devices  27 us (14%)
  starting transfers between devices  13 us (7%)
  other arithmetic  11.1 us (6%)
  matrix products  5.62 us (3%)
    all_to_all x1, blocking collectives, per_device(): landed = lax.all_to_all(payload, ('dp', 'zl'), 0, 0, tiled=True)  39.9 us
    pallas_call x4, Pallas kernels, grad_call(): pl.pallas_call(functools.partial(grad_kernel, aliased), grid=(nh,), in_sp...  32.2 us
    pallas_call x2, Pallas kernels, weight_call(): pl.pallas_call(functools.partial(weight_kernel, h0), grid=(nh,), in_specs...  24.9 us
    ppermute x8, waiting for transfers between devices, over_z(): return lax.ppermute(a, 'zl', CORE_SWAP)  24.9 us
    unnamed x55, local copies, waits for them, and re-layouts  11.5 us
    ppermute x8, starting transfers between devices, over_z(): return lax.ppermute(a, 'zl', CORE_SWAP)  9.66 us
    all_gather x1, blocking collectives, per_device(): bias = lax.all_gather(bias, ('zl', 'core'), axis=0, tiled=True)  5.49 us
    slice x2, local copies, waits for them, and re-layouts, columns(): return a[:, h0 * HD:(h0 + nh) * HD]  4.97 us
  transfers between devices with their start and end apart: 21, of which 5 were waited for; matrix products, arithmetic and copies ran while one was open for 12% of the time, Pallas kernels for 29%

profile of v1, /device:TPU:0, one launch (start us, length us, event | category | flops | bytes accessed | tf_op | source)
XLA Modules:
  0.0 195.8 jit_solution(10139646205744143970)
XLA Ops:
  0.8 2.6 %fusion.22 = (bf16[256,1280]{1,0:T(8,128)(2,1)}, bf16[256,1280]{1,0:T(8,128)(2,1)}) fusion(bf16[256,2560]{1,0:T(8,128)(2,1)} %k0.11), kind=kLoop, calls=%fused_computation.51 | loop fusion | bytes 2621440 | tf_op jit(solution)/shard_map/slice | solution.py:204
  3.4 2.0 %collective-permute-start.11 = (bf16[256,1280]{1,0:T(8,128)(2,1)}, bf16[256,1280]{1,0:T(8,128)(2,1)}, u32[]{:S(2)}, u32[]{:S(2)}) collective-permute-start(bf16[256,1280]{1,0:T(8,128)(2,1)} %get-tuple-element.45), channel_id=1, source_target_pairs={{0,2},{2,0},{1,3},{3,1},{4,6},{6,4},{5,7},{7,5},{8,10},{10,8},{9,1... | collective-permute-start | bytes 1966088 | tf_op jit(solution)/shard_map/ppermute | solution.py:192
  6.8 1.7 collective-permute-start.1
  8.5 2.4 %fusion.21 = (bf16[256,640]{1,0:T(8,128)(2,1)}, bf16[256,640]{1,0:T(8,128)(2,1)}, bf16[256,640]{1,0:T(8,128)(2,1)}, bf16[256,640]{1,0:T(8,128)(2,1)}) fusion(bf16[256,2560]{1,0:T(8,128)(2,1)} %v0.7), kind=kLoop, calls=%fused_computation.50 | loop fusion | bytes 2621440 | tf_op jit(solution)/shard_map/slice | solution.py:204
  11.1 2.4 %convolution_convert_fusion.2 = bf16[256,128]{0,1:T(8,128)(2,1)S(1)} fusion(bf16[256,5120]{1,0:T(8,128)(2,1)S(1)} %copy-done, bf16[5120,128]{1,0:T(8,128)(2,1)} %param.16), kind=kOutput, calls=%fused_computation.14 | convolution fusion | flops 335577088 | bytes 3997696 | tf_op jit(solution)/shard_map/dot_general | solution.py:26
  13.5 7.8 %collective-permute-done.11.k2 = bf16[256,1280]{1,0:T(8,128)(2,1)} collective-permute-done((bf16[256,1280]{1,0:T(8,128)(2,1)}, bf16[256,1280]{1,0:T(8,128)(2,1)}, u32[]{:S(2)}, u32[]{:S(2)}) %collective-permute-start.11) | collective-permute-done | bytes 655392 | tf_op jit(solution)/shard_map/ppermute | solution.py:192
  22.7 14.0 %collective-permute-done.1.k2 = bf16[256,1280]{1,0:T(8,128)(2,1)} collective-permute-done((bf16[256,1280]{1,0:T(8,128)(2,1)}, bf16[256,1280]{1,0:T(8,128)(2,1)}, u32[]{:S(2)}, u32[]{:S(2)}) %collective-permute-start.1) | collective-permute-done | bytes 655392 | tf_op jit(solution)/shard_map/ppermute | solution.py:192
  37.4 5.5 %all_gather.3 = f32[20,8,8]{2,1,0:T(8,128)S(1)} all-gather(f32[5,8,8]{2,1,0:T(8,128)} %broadcast_select_fusion), channel_id=1, replica_groups=mesh['dp'=32,'zl'=2,'core'=2] {'zl','core'}, dimensions={0}, use_global_device_ids=true | all-gather | bytes 6400 | tf_op jit(solution)/shard_map/all_gather | solution.py:218
  42.9 1.8 collective-permute-start.15
  48.6 1.8 collective-permute-start.9
  51.4 1.3 copy-done.5
  53.6 12.3 %attention_weights.3 = (bf16[10,1024,256]{2,1,0:T(8,128)(2,1)}, bf16[256,1280]{1,0:T(8,128)(2,1)S(1)}, f32[4,256,128]{2,1,0:T(8,128)S(1)}) custom-call(f32[20,16]{1,0:T(8,128)S(1)} %copy.55.bias_ref, bf16[256,2560]{1,0:T(8,128)(2,1)S(1)} %copy-done.5, bf16[256,128]{1,0:T(8,128)(2,1)S(1)} %copy-done.10, bf16[128,2560]{1,0:T(8,128)(2,1)S(1)} %copy-done.2, ...), custom_call_target="tpu_custom_call" | custom-call | flops 2013265920 | bytes 12000000 | tf_op jit(solution)/shard_map/attention_weights/pallas_call | solution.py:121
  67.8 12.5 %attention_weights.2 = (bf16[10,1024,256]{2,1,0:T(8,128)(2,1)}, bf16[256,1280]{1,0:T(8,128)(2,1)S(1)}, f32[4,256,128]{2,1,0:T(8,128)S(1)}) custom-call(f32[20,16]{1,0:T(8,128)S(1)} %copy.55.bias_ref, bf16[256,2560]{1,0:T(8,128)(2,1)S(1)} %copy-done.5, bf16[256,128]{1,0:T(8,128)(2,1)S(1)} %copy-done.10, bf16[128,2560]{1,0:T(8,128)(2,1)S(1)} %copy-done.2, ...), custom_call_target="tpu_custom_call" | custom-call | flops 2013265920 | bytes 12000000 | tf_op jit(solution)/shard_map/attention_weights/pallas_call | solution.py:121
  82.0 2.0 %copy.59 = f32[4,256,128]{1,2,0:T(8,128)} copy(f32[4,256,128]{2,1,0:T(8,128)} %copy-done.11) | data formatting | bytes 1048576 | tf_op jit(solution)/shard_map/attention_weights/pallas_call | solution.py:121
  84.1 2.1 %copy.60 = f32[4,256,128]{1,2,0:T(8,128)} copy(f32[4,256,128]{2,1,0:T(8,128)} %copy-done.12) | data formatting | bytes 1048576 | tf_op jit(solution)/shard_map/attention_weights/pallas_call | solution.py:121
  86.8 1.3 fusion.20
  90.0 7.9 %attention_grads.4 = (bf16[256,2560]{1,0:T(8,128)(2,1)}, bf16[5,2,128,128]{3,2,1,0:T(8,128)(2,1)S(1)}, f32[128,256]{1,0:T(8,128)S(1)}) custom-call(bf16[10,1024,256]{2,1,0:T(8,128)(2,1)} %get-tuple-element.23.wt_ref, bf16[256,2560]{1,0:T(8,128)(2,1)S(1)} %copy-done.1, bf16[256,2560]{1,0:T(8,128)(2,1)} %collective-permute-done.k1, ...), custom_call_target="tpu_custom_call" | custom-call | flops 1677721600 | bytes 6000000 | tf_op jit(solution)/shard_map/attention_grads/pallas_call | solution.py:161
  98.7 8.1 %attention_grads.5 = (bf16[256,2560]{1,0:T(8,128)(2,1)}, bf16[5,2,128,128]{3,2,1,0:T(8,128)(2,1)S(1)}, f32[128,256]{1,0:T(8,128)S(1)}) custom-call(bf16[10,1024,256]{2,1,0:T(8,128)(2,1)} %get-tuple-element.23.wt_ref, bf16[256,2560]{1,0:T(8,128)(2,1)S(1)} %copy-done.1, bf16[256,2560]{1,0:T(8,128)(2,1)} %collective-permute-done.k1, ...), custom_call_target="tpu_custom_call", output_to_operand_aliasing={{0}: (18, {})} | custom-call | flops 1677721600 | bytes 6000000 | tf_op jit(solution)/shard_map/attention_grads/pallas_call | solution.py:161
  106.8 8.1 %attention_grads.6 = (bf16[256,2560]{1,0:T(8,128)(2,1)}, bf16[5,2,128,128]{3,2,1,0:T(8,128)(2,1)S(1)}, f32[128,256]{1,0:T(8,128)S(1)}) custom-call(bf16[10,1024,256]{2,1,0:T(8,128)(2,1)} %get-tuple-element.21.wt_ref, bf16[256,2560]{1,0:T(8,128)(2,1)S(1)} %copy-done.1, bf16[256,2560]{1,0:T(8,128)(2,1)} %collective-permute-done.k1, ...), custom_call_target="tpu_custom_call", output_to_operand_aliasing={{0}: (18, {})} | custom-call | flops 1677721600 | bytes 6000000 | tf_op jit(solution)/shard_map/attention_grads/pallas_call | solution.py:161
  115.7 8.1 %attention_grads.7 = (bf16[256,2560]{1,0:T(8,128)(2,1)}, bf16[5,2,128,128]{3,2,1,0:T(8,128)(2,1)S(1)}, f32[128,256]{1,0:T(8,128)S(1)}) custom-call(bf16[10,1024,256]{2,1,0:T(8,128)(2,1)} %get-tuple-element.21.wt_ref, bf16[256,2560]{1,0:T(8,128)(2,1)S(1)} %copy-done.1, bf16[256,2560]{1,0:T(8,128)(2,1)} %collective-permute-done.k1, ...), custom_call_target="tpu_custom_call", output_to_operand_aliasing={{0}: (18, {})} | custom-call | flops 1677721600 | bytes 6000000 | tf_op jit(solution)/shard_map/attention_grads/pallas_call | solution.py:161
  124.5 1.8 collective-permute-start.18
  126.4 2.5 %collective-permute-done.18 = bf16[256,128]{0,1:T(8,128)(2,1)S(1)} collective-permute-done((bf16[256,128]{0,1:T(8,128)(2,1)S(1)}, bf16[256,128]{0,1:T(8,128)(2,1)S(1)}, u32[]{:S(2)}, u32[]{:S(2)}) %collective-permute-start.18) | collective-permute-done | bytes 65568 | tf_op jit(solution)/shard_map/ppermute | solution.py:192
  128.9 2.4 %fusion = bf16[5120,256]{0,1:T(8,128)(2,1)} fusion(bf16[256,5120]{1,0:T(8,128)(2,1)S(1)} %copy-done, bf16[256,128]{0,1:T(8,128)(2,1)S(1)} %fusion.8, bf16[256,128]{0,1:T(8,128)(2,1)S(1)} %fusion.14), kind=kOutput, calls=%fused_computation.1 | convolution fusion | flops 672661504 | bytes 5373952 | tf_op jit(solution)/shard_map/dot_general | solution.py:256
  131.3 4.4 %copy.61 = bf16[5120,256]{1,0:T(8,128)(2,1)} copy(bf16[5120,256]{0,1:T(8,128)(2,1)} %fusion) | data formatting | bytes 5242880 | tf_op jit(solution)/shard_map/convert_element_type | solution.py:258
  135.7 2.6 %dynamic-slice_bitcast_fusion = bf16[64,40,256]{2,1,0:T(8,128)(2,1)} fusion(bf16[64,2,40,256]{3,2,1,0:T(8,128)(2,1)} %bitcast.62, s32[]{:T(128)S(6)} %select_n.47), kind=kLoop, calls=%fused_computation.12 | loop fusion | bytes 2621444 | tf_op jit(solution)/shard_map/jit(dynamic_index_in_dim)/squeeze | solution.py:268
  140.7 1.1 fusion.4
  142.3 2.1 %collective-permute-done.20 = bf16[64,40,128]{2,1,0:T(8,128)(2,1)} collective-permute-done((bf16[64,40,128]{2,1,0:T(8,128)(2,1)}, bf16[64,40,128]{2,1,0:T(8,128)(2,1)}, u32[]{:S(2)}, u32[]{:S(2)}) %collective-permute-start.20) | collective-permute-done | bytes 655392 | tf_op jit(solution)/shard_map/ppermute | solution.py:188
  144.4 2.5 %fusion.2 = bf16[64,40,128]{2,1,0:T(8,128)(2,1)} fusion(bf16[64,40,128]{2,1,0:T(8,128)(2,1)} %collective-permute-done.20, s32[]{:T(128)S(6)} %select_n.46, bf16[1,64,40,128]{3,2,1,0:T(8,128)(2,1)} %bitcast.67, bf16[1,64,40,128]{3,2,1,0:T(8,128)(2,1)S(1)} %bitcast.65), kind=kLoop, calls=%fused_computation.11 | loop fusion | flops 1638400 | bytes 2621444 | tf_op jit(solution)/shard_map/convert_element_type | solution.py:272
  146.9 2.8 %fusion.1 = bf16[64,40,256]{2,1,0:T(8,128)(2,1)} fusion(bf16[64,40,256]{2,1,0:T(8,128)(2,1)} %collective-permute-done.19, bf16[64,2,40,256]{3,2,1,0:T(8,128)(2,1)S(1)} %bitcast.63, s32[]{:T(128)S(6)} %select_n.46), kind=kLoop, calls=%fused_computation.4 | loop fusion | flops 2621440 | bytes 3932164 | tf_op jit(solution)/shard_map/convert_element_type | solution.py:271
  149.7 3.2 %reshape.79 = bf16[64,80,128]{2,1,0:T(8,128)(2,1)} reshape(bf16[64,40,256]{2,1,0:T(8,128)(2,1)} %fusion.1) | data formatting | bytes 2621440 | tf_op jit(solution)/shard_map/reshape | solution.py:274
  152.9 1.5 pad_maximum_fusion
  154.4 39.9 %all_to_all.5 = bf16[64,120,128]{2,1,0:T(8,128)(2,1)S(1)} all-to-all(bf16[64,120,128]{2,1,0:T(8,128)(2,1)S(1)} %pad_maximum_fusion), channel_id=1, replica_groups=mesh['dp'=32,'zl'=2,'core'=2] {'dp','zl'}, dimensions={0} | all-to-all | bytes 3932160 | tf_op jit(solution)/shard_map/all_to_all | solution.py:275
  (116 shorter events, 22.6 us)
Async XLA Ops:
  0.6 4.7 %copy-start = (bf16[256,5120]{1,0:T(8,128)(2,1)S(1)}, bf16[256,5120]{1,0:T(8,128)(2,1)}, u32[]{:S(2)}) copy-start(bf16[256,5120]{1,0:T(8,128)(2,1)} %param.11) | copy-start | bytes 7864324
  0.6 4.7 %copy-start.24 = (bf16[5120,128]{1,0:T(8,128)(2,1)S(1)}, bf16[5120,128]{1,0:T(8,128)(2,1)}, u32[]{:S(2)}) copy-start(bf16[5120,128]{1,0:T(8,128)(2,1)} %param.17) | copy-start | bytes 3932164
  0.7 47.9 %collective-permute-start = (bf16[256,2560]{1,0:T(8,128)(2,1)}, bf16[256,2560]{1,0:T(8,128)(2,1)}, u32[]{:S(2)}, u32[]{:S(2)}) collective-permute-start(bf16[256,2560]{1,0:T(8,128)(2,1)} %k0.11), channel_id=1, source_target_pairs={{0,1},{1,0},{2,3},{3,2},{4,5},{5,4},{6,7},{7,6},{8,9},{9,8},{10,11... | collective-permute-start | bytes 3932168 | tf_op jit(solution)/shard_map/ppermute | solution.py:188
  3.4 17.9 %collective-permute-start.11 = (bf16[256,1280]{1,0:T(8,128)(2,1)}, bf16[256,1280]{1,0:T(8,128)(2,1)}, u32[]{:S(2)}, u32[]{:S(2)}) collective-permute-start(bf16[256,1280]{1,0:T(8,128)(2,1)} %get-tuple-element.45), channel_id=1, source_target_pairs={{0,2},{2,0},{1,3},{3,1},{4,6},{6,4},{5,7},{7,5},{8,10},{10,8},{9,1... | collective-permute-start | bytes 1966088 | tf_op jit(solution)/shard_map/ppermute | solution.py:192
  6.2 16.3 %collective-permute-start.7 = (bf16[256,128]{1,0:T(8,128)(2,1)S(1)}, bf16[256,128]{1,0:T(8,128)(2,1)S(1)}, u32[]{:S(2)}, u32[]{:S(2)}) collective-permute-start(bf16[256,128]{1,0:T(8,128)(2,1)S(1)} %convolution_convert_fusion.1.l0), channel_id=1, source_target_pairs={{0,2},{2,0},{1,3},{3,1},{4,6},{6,4},{5,7},{7,5},{8,10},{10,8},{9,1... | collective-permute-start | bytes 196616 | tf_op jit(solution)/shard_map/ppermute | solution.py:192
  6.3 82.6 %collective-permute-start.3 = (bf16[256,2560]{1,0:T(8,128)(2,1)}, bf16[256,2560]{1,0:T(8,128)(2,1)}, u32[]{:S(2)}, u32[]{:S(2)}) collective-permute-start(bf16[256,2560]{1,0:T(8,128)(2,1)} %v0.7), channel_id=1, source_target_pairs={{0,1},{1,0},{2,3},{3,2},{4,5},{5,4},{6,7},{7,6},{8,9},{9,8},{10,11... | collective-permute-start | bytes 3932168 | tf_op jit(solution)/shard_map/ppermute | solution.py:188
  6.8 4.0 %copy-start.26 = (s32[5,8]{1,0:T(8,128)S(1)}, s32[5,8]{1,0:T(8,128)}, u32[]{:S(2)}) copy-start(s32[5,8]{1,0:T(8,128)} %param.21) | copy-start | bytes 484
  6.8 4.0 %copy-start.25 = (s32[5,8,5]{2,1,0:T(8,128)S(1)}, s32[5,8,5]{2,1,0:T(8,128)}, u32[]{:S(2)}) copy-start(s32[5,8,5]{2,1,0:T(8,128)} %param.20) | copy-start | bytes 2404
  6.8 29.9 %collective-permute-start.1 = (bf16[256,1280]{1,0:T(8,128)(2,1)}, bf16[256,1280]{1,0:T(8,128)(2,1)}, u32[]{:S(2)}, u32[]{:S(2)}) collective-permute-start(bf16[256,1280]{1,0:T(8,128)(2,1)} %get-tuple-element.46), channel_id=1, source_target_pairs={{0,2},{2,0},{1,3},{3,1},{4,6},{6,4},{5,7},{7,5},{8,10},{10,8},{9,1... | collective-permute-start | bytes 1966088 | tf_op jit(solution)/shard_map/ppermute | solution.py:192
  11.1 39.2 %copy-start.2 = (bf16[128,2560]{1,0:T(8,128)(2,1)S(1)}, bf16[128,2560]{1,0:T(8,128)(2,1)}, u32[]{:S(2)}) copy-start(bf16[128,2560]{1,0:T(8,128)(2,1)} %upq_ref.11) | copy-start | bytes 1966084
  21.3 27.0 %collective-permute-start.12 = (bf16[256,1280]{1,0:T(8,128)(2,1)}, bf16[256,1280]{1,0:T(8,128)(2,1)}, u32[]{:S(2)}, u32[]{:S(2)}) collective-permute-start(bf16[256,1280]{1,0:T(8,128)(2,1)} %collective-permute-done.11.k2), channel_id=1, source_target_pairs={{0,1},{1,0},{2,3},{3,2},{4,5},{5,4},{6,7},{7,6},{8,9},{9,8},{10,11... | collective-permute-start | bytes 1966088 | tf_op jit(solution)/shard_map/ppermute | solution.py:188
  22.6 14.3 %collective-permute-start.6 = (bf16[256,128]{1,0:T(8,128)(2,1)S(1)}, bf16[256,128]{1,0:T(8,128)(2,1)S(1)}, u32[]{:S(2)}, u32[]{:S(2)}) collective-permute-start(bf16[256,128]{1,0:T(8,128)(2,1)S(1)} %convolution_convert_fusion.1.l0), channel_id=1, source_target_pairs={{0,1},{1,0},{2,3},{3,2},{4,5},{5,4},{6,7},{7,6},{8,9},{9,8},{10,11... | collective-permute-start | bytes 196616 | tf_op jit(solution)/shard_map/ppermute | solution.py:188
  36.7 31.1 %collective-permute-start.2 = (bf16[256,1280]{1,0:T(8,128)(2,1)}, bf16[256,1280]{1,0:T(8,128)(2,1)}, u32[]{:S(2)}, u32[]{:S(2)}) collective-permute-start(bf16[256,1280]{1,0:T(8,128)(2,1)} %collective-permute-done.1.k2), channel_id=1, source_target_pairs={{0,1},{1,0},{2,3},{3,2},{4,5},{5,4},{6,7},{7,6},{8,9},{9,8},{10,11... | collective-permute-start | bytes 1966088 | tf_op jit(solution)/shard_map/ppermute | solution.py:188
  36.9 6.0 %collective-permute-start.8 = (bf16[256,128]{1,0:T(8,128)(2,1)S(1)}, bf16[256,128]{1,0:T(8,128)(2,1)}, u32[]{:S(2)}, u32[]{:S(2)}) collective-permute-start(bf16[256,128]{1,0:T(8,128)(2,1)S(1)} %collective-permute-done.7.l2), channel_id=1, source_target_pairs={{0,1},{1,0},{2,3},{3,2},{4,5},{5,4},{6,7},{7,6},{8,9},{9,8},{10,11... | collective-permute-start | bytes 196616 | tf_op jit(solution)/shard_map/ppermute | solution.py:188
  42.9 24.7 %collective-permute-start.15 = (bf16[256,640]{1,0:T(8,128)(2,1)}, bf16[256,640]{1,0:T(8,128)(2,1)}, u32[]{:S(2)}, u32[]{:S(2)}) collective-permute-start(bf16[256,640]{1,0:T(8,128)(2,1)} %get-tuple-element.41), channel_id=1, source_target_pairs={{0,2},{2,0},{1,3},{3,1},{4,6},{6,4},{5,7},{7,5},{8,10},{10,8},{9,1... | collective-permute-start | bytes 983048 | tf_op jit(solution)/shard_map/ppermute | solution.py:192
  48.3 37.9 %collective-permute-start.13 = (bf16[256,640]{1,0:T(8,128)(2,1)}, bf16[256,640]{1,0:T(8,128)(2,1)}, u32[]{:S(2)}, u32[]{:S(2)}) collective-permute-start(bf16[256,640]{1,0:T(8,128)(2,1)} %get-tuple-element.42), channel_id=1, source_target_pairs={{0,2},{2,0},{1,3},{3,1},{4,6},{6,4},{5,7},{7,5},{8,10},{10,8},{9,1... | collective-permute-start | bytes 983048 | tf_op jit(solution)/shard_map/ppermute | solution.py:192
  48.6 38.1 %collective-permute-start.9 = (bf16[256,640]{1,0:T(8,128)(2,1)}, bf16[256,640]{1,0:T(8,128)(2,1)}, u32[]{:S(2)}, u32[]{:S(2)}) collective-permute-start(bf16[256,640]{1,0:T(8,128)(2,1)} %get-tuple-element.43), channel_id=1, source_target_pairs={{0,2},{2,0},{1,3},{3,1},{4,6},{6,4},{5,7},{7,5},{8,10},{10,8},{9,1... | collective-permute-start | bytes 983048 | tf_op jit(solution)/shard_map/ppermute | solution.py:192
  67.6 20.6 %collective-permute-start.4 = (bf16[256,640]{1,0:T(8,128)(2,1)}, bf16[256,640]{1,0:T(8,128)(2,1)}, u32[]{:S(2)}, u32[]{:S(2)}) collective-permute-start(bf16[256,640]{1,0:T(8,128)(2,1)} %get-tuple-element.44), channel_id=1, source_target_pairs={{0,2},{2,0},{1,3},{3,1},{4,6},{6,4},{5,7},{7,5},{8,10},{10,8},{9,1... | collective-permute-start | bytes 983048 | tf_op jit(solution)/shard_map/ppermute | solution.py:192
  67.8 20.8 %collective-permute-start.16 = (bf16[256,640]{1,0:T(8,128)(2,1)}, bf16[256,640]{1,0:T(8,128)(2,1)}, u32[]{:S(2)}, u32[]{:S(2)}) collective-permute-start(bf16[256,640]{1,0:T(8,128)(2,1)} %collective-permute-done.15.v2), channel_id=1, source_target_pairs={{0,1},{1,0},{2,3},{3,2},{4,5},{5,4},{6,7},{7,6},{8,9},{9,8},{10,11... | collective-permute-start | bytes 983048 | tf_op jit(solution)/shard_map/ppermute | solution.py:188
  86.1 2.8 %copy-start.1 = (bf16[256,2560]{1,0:T(8,128)(2,1)S(1)}, bf16[256,2560]{1,0:T(8,128)(2,1)}, u32[]{:S(2)}) copy-start(bf16[256,2560]{1,0:T(8,128)(2,1)} %k0.11) | copy-start | bytes 3932164
  86.1 2.8 %copy-start.4 = (bf16[128,2560]{1,0:T(8,128)(2,1)S(1)}, bf16[128,2560]{1,0:T(8,128)(2,1)}, u32[]{:S(2)}) copy-start(bf16[128,2560]{1,0:T(8,128)(2,1)} %upv_ref.11) | copy-start | bytes 1966084
  86.2 12.5 %collective-permute-start.14 = (bf16[256,640]{1,0:T(8,128)(2,1)}, bf16[256,640]{1,0:T(8,128)(2,1)S(1)}, u32[]{:S(2)}, u32[]{:S(2)}) collective-permute-start(bf16[256,640]{1,0:T(8,128)(2,1)} %collective-permute-done.13.v2), channel_id=1, source_target_pairs={{0,1},{1,0},{2,3},{3,2},{4,5},{5,4},{6,7},{7,6},{8,9},{9,8},{10,11... | collective-permute-start | bytes 983048 | tf_op jit(solution)/shard_map/ppermute | solution.py:188
  86.7 20.1 %collective-permute-start.10 = (bf16[256,640]{1,0:T(8,128)(2,1)}, bf16[256,640]{1,0:T(8,128)(2,1)S(1)}, u32[]{:S(2)}, u32[]{:S(2)}) collective-permute-start(bf16[256,640]{1,0:T(8,128)(2,1)} %collective-permute-done.9.v2), channel_id=1, source_target_pairs={{0,1},{1,0},{2,3},{3,2},{4,5},{5,4},{6,7},{7,6},{8,9},{9,8},{10,11... | collective-permute-start | bytes 983048 | tf_op jit(solution)/shard_map/ppermute | solution.py:188
  88.1 27.5 %collective-permute-start.5 = (bf16[256,640]{1,0:T(8,128)(2,1)}, bf16[256,640]{1,0:T(8,128)(2,1)S(1)}, u32[]{:S(2)}, u32[]{:S(2)}) collective-permute-start(bf16[256,640]{1,0:T(8,128)(2,1)} %collective-permute-done.4.v2), channel_id=1, source_target_pairs={{0,1},{1,0},{2,3},{3,2},{4,5},{5,4},{6,7},{7,6},{8,9},{9,8},{10,11... | collective-permute-start | bytes 983048 | tf_op jit(solution)/shard_map/ppermute | solution.py:188
  88.6 35.9 %collective-permute-start.17 = (bf16[2,256,128]{1,2,0:T(8,128)(2,1)S(1)}, bf16[2,256,128]{1,2,0:T(8,128)(2,1)S(1)}, u32[]{:S(2)}, u32[]{:S(2)}) collective-permute-start(bf16[2,256,128]{1,2,0:T(8,128)(2,1)S(1)} %slice.45), channel_id=1, source_target_pairs={{0,1},{1,0},{2,3},{3,2},{4,5},{5,4},{6,7},{7,6},{8,9},{9,8},{10,11... | collective-permute-start | bytes 393224 | tf_op jit(solution)/shard_map/ppermute | solution.py:188
  98.7 8.1 %copy-start.7 = (bf16[256,1280]{1,0:T(8,128)(2,1)S(1)}, bf16[256,1280]{1,0:T(8,128)(2,1)}, u32[]{:S(2)}) copy-start(bf16[256,1280]{1,0:T(8,128)(2,1)} %copy-done.6) | copy-start | bytes 1966084
  106.8 8.1 %copy-start.15 = (bf16[5,2,128,128]{3,2,1,0:T(8,128)(2,1)}, bf16[5,2,128,128]{3,2,1,0:T(8,128)(2,1)S(1)}, u32[]{:S(2)}) copy-start(bf16[5,2,128,128]{3,2,1,0:T(8,128)(2,1)S(1)} %get-tuple-element.37) | copy-start | bytes 983044
  124.5 4.3 %collective-permute-start.18 = (bf16[256,128]{0,1:T(8,128)(2,1)S(1)}, bf16[256,128]{0,1:T(8,128)(2,1)S(1)}, u32[]{:S(2)}, u32[]{:S(2)}) collective-permute-start(bf16[256,128]{0,1:T(8,128)(2,1)S(1)} %fusion.15), channel_id=1, source_target_pairs={{0,2},{2,0},{1,3},{3,1},{4,6},{6,4},{5,7},{7,5},{8,10},{10,8},{9,1... | collective-permute-start | bytes 196616 | tf_op jit(solution)/shard_map/ppermute | solution.py:192
  138.3 8.6 %collective-permute-start.19 = (bf16[64,40,256]{2,1,0:T(8,128)(2,1)}, bf16[64,40,256]{2,1,0:T(8,128)(2,1)}, u32[]{:S(2)}, u32[]{:S(2)}) collective-permute-start(bf16[64,40,256]{2,1,0:T(8,128)(2,1)} %dynamic-slice_bitcast_fusion), channel_id=1, source_target_pairs={{0,1},{1,0},{2,3},{3,2},{4,5},{5,4},{6,7},{7,6},{8,9},{9,8},{10,11... | collective-permute-start | bytes 3932168 | tf_op jit(solution)/shard_map/ppermute | solution.py:188
  141.8 2.6 %collective-permute-start.20 = (bf16[64,40,128]{2,1,0:T(8,128)(2,1)}, bf16[64,40,128]{2,1,0:T(8,128)(2,1)}, u32[]{:S(2)}, u32[]{:S(2)}) collective-permute-start(bf16[64,40,128]{2,1,0:T(8,128)(2,1)} %fusion.4), channel_id=1, source_target_pairs={{0,1},{1,0},{2,3},{3,2},{4,5},{5,4},{6,7},{7,6},{8,9},{9,8},{10,11... | collective-permute-start | bytes 1966088 | tf_op jit(solution)/shard_map/ppermute | solution.py:188
  142.3 4.6 %copy-start.21 = (bf16[5120,256]{1,0:T(8,128)(2,1)S(1)}, bf16[5120,256]{1,0:T(8,128)(2,1)}, u32[]{:S(2)}) copy-start(bf16[5120,256]{1,0:T(8,128)(2,1)} %copy.61) | copy-start | bytes 7864324
  149.6 3.3 %copy-start.23 = (bf16[64,40,128]{2,1,0:T(8,128)(2,1)S(1)}, bf16[64,40,128]{2,1,0:T(8,128)(2,1)}, u32[]{:S(2)}) copy-start(bf16[64,40,128]{2,1,0:T(8,128)(2,1)} %fusion.2) | copy-start | bytes 1966084
  (16 other events, 17.9 us)

commit v2 on v1

v2 whole, which is shorter than its diff:
```python
import functools
import math

import jax
import jax.numpy as jnp
from jax import lax
from jax.experimental import pallas as pl
from jax.experimental.pallas import tpu as pltpu
from jax.sharding import Mesh
from jax.sharding import PartitionSpec as P

HEADS = 20
HD = 128
R = 128
NB = 8
ROWS = 256
GH = 5
K_CHUNKS = ((0, 2), (2, 2))
V_CHUNKS = ((0, 2), (2, 2))
SCALE = 1.0 / math.sqrt(HD)
SCALE2 = SCALE * math.log2(math.e)
F32 = jnp.float32
BF16 = jnp.bfloat16


def nn(a, b):
    return lax.dot_general(a, b, (((1,), (0,)), ((), ())), preferred_element_type=F32)


def nt(a, b):
    return lax.dot_general(a, b, (((1,), (1,)), ((), ())), preferred_element_type=F32)


def tn(a, b):
    return lax.dot_general(a, b, (((0,), (0,)), ((), ())), preferred_element_type=F32)


def heads_of(h):
    return slice(h * HD, (h + 1) * HD)


def weight_kernel(
    chunk0, me_ref, bias_ref, qb_ref, lowq_ref, upq_ref, cot_ref, upv_ref, k0, k1, k2, k3, *rest
):
    step = pl.program_id(0)
    keys = (k0, k1, k2, k3)
    last_call = chunk0 > 0
    if last_call:
        before_ref, *rest = rest
    wt_ref, inv_ref, g_ref, *rest = rest
    if last_call:
        here_ref, sib_ref, zs_ref, zd_ref, *rest = rest
    lgv_ref, z_ref, q_ref = rest
    first_half = lax.broadcasted_iota(jnp.int32, (1, ROWS), 1) < ROWS // 2
    me = me_ref[0, 0]
    head0 = ((chunk0 + step) ^ me) * GH

    @pl.when(step == 0)
    def _():
        lgv_ref[...] = before_ref[...] if last_call else jnp.zeros_like(lgv_ref)

    tops, sums, scaled = [None] * GH, [None] * GH, [None] * GH

    def prepare(h):
        c = heads_of(h)
        q_ref[h % 2] = (qb_ref[:, c].astype(F32) + nn(lowq_ref[...], upq_ref[:, c])).astype(BF16)
        g_ref[:, c] = nt(cot_ref[:, c], upv_ref[:, c]).astype(BF16)

    def score(h, r):
        s = nt(keys[r][:, heads_of(h)], q_ref[h % 2]) * SCALE2
        for b in range(2):
            j = 2 * r + b
            block = (me ^ r) * 2 + b
            low, high = (bias_ref[head0 + h, (me * 2 + i) * NB + block] for i in range(2))
            z = s[b * 128 : (b + 1) * 128] + jnp.where(first_half, low, high)
            top = jnp.max(z.reshape(16, 8, ROWS), axis=0)
            tops[h] = top if tops[h] is None else jnp.maximum(tops[h], top)
            z_ref[h % 2, j * 128 : (j + 1) * 128] = z

    def power(h, r):
        if r == 0:
            tops[h] = jnp.max(tops[h], axis=0, keepdims=True)
        rows = slice(r * ROWS, (r + 1) * ROWS)
        p = jnp.exp2(z_ref[h % 2, rows] - tops[h])
        wt_ref[h, rows] = p.astype(BF16)
        part = jnp.sum(p.reshape(32, 8, ROWS), axis=0)
        sums[h] = part if sums[h] is None else sums[h] + part

    def finish(h):
        inv = 1.0 / jnp.sum(sums[h], axis=0, keepdims=True)
        inv_ref[h] = jnp.broadcast_to(inv, (8, ROWS))
        inv_rows = jnp.transpose(jnp.broadcast_to(inv, (R, ROWS)))
        scaled[h] = (g_ref[:, heads_of(h)].astype(F32) * inv_rows).astype(BF16)

    def low_grad(h, r):
        lgv_ref[r] += nn(wt_ref[h, r * ROWS : (r + 1) * ROWS], scaled[h])

    for i in range(GH + 2):
        if i < GH:
            prepare(i)
        for r in range(4):
            if i < GH:
                score(i, r)
            if 1 <= i <= GH:
                power(i - 1, r)
            if i >= 2:
                low_grad(i - 2, r)
        if 1 <= i <= GH:
            finish(i - 1)

    if last_call:

        @pl.when(step == pl.num_programs(0) - 1)
        def _():
            here_ref[...] = lgv_ref[0]
            for r, ref in enumerate((sib_ref, zs_ref, zd_ref)):
                ref[...] = lgv_ref[r + 1].astype(BF16)


def grad_kernel(
    aliased, downs,
    wt_ref, inv_ref, k0, k1, k2, k3, v0, v1, v2, v3, l0, l1, l2, l3,
    cot_ref, g_ref, upq_ref, upv_ref, lowqp_ref, perm_ref, *rest,
):
    rest = list(rest[1:] if aliased else rest)
    core_ref, *rest = rest
    if downs:
        hidden_ref, here_ref, *low_refs = rest[:6]
        rest = rest[6:]
    att_ref, lgq_ref, up_mine, up_other, *rest = rest
    if downs:
        down_mine, down_other, *rest = rest
    vl_ref, back_ref, sh_ref, gu_ref, up_ref, *rest = rest
    step = pl.program_id(0)
    first_step, last_step = step == 0, step == pl.num_programs(0) - 1
    if downs:
        held_ref, sem = rest
        fetch = pltpu.make_async_copy(hidden_ref, held_ref, sem)
        pl.when(first_step)(fetch.start)
    keys, vals, lows = (k0, k1, k2, k3), (v0, v1, v2, v3), (l0, l1, l2, l3)

    @pl.when(first_step)
    def _():
        lgq_ref[...] = jnp.zeros_like(lgq_ref)
        for p in range(2):
            for r in range(4):
                vl_ref[p, r * ROWS : (r + 1) * ROWS, HD:] = lows[r][...]

    cot_g, dots, outs, dqs = [None] * GH, [None] * GH, [None] * GH, [None] * GH

    def prepare(h):
        c = heads_of(h)
        cot_g[h] = jnp.concatenate([cot_ref[:, c], g_ref[:, c]], axis=1)
        for r in range(4):
            vl_ref[h % 2, r * ROWS : (r + 1) * ROWS, :HD] = vals[r][:, c]

    def back(h, r):
        rows = slice(r * ROWS, (r + 1) * ROWS)
        b = nt(vl_ref[h % 2, rows], cot_g[h])
        back_ref[h % 2, rows] = b
        part = jnp.sum((b * wt_ref[h, rows].astype(F32)).reshape(32, 8, ROWS), axis=0)
        dots[h] = part if dots[h] is None else dots[h] + part

    def shift(h, r):
        rows = slice(r * ROWS, (r + 1) * ROWS)
        if r == 0:
            dots[h] = jnp.sum(dots[h], axis=0, keepdims=True) * inv_ref[h, 0:1]
        sh_ref[h % 2, rows] = (
            wt_ref[h, rows].astype(F32) * (back_ref[h % 2, rows] - dots[h])
        ).astype(BF16)
        if r == 3:
            key = jnp.concatenate([k[:, heads_of(h)] for k in keys], axis=0)
            dqs[h] = tn(key, sh_ref[h % 2])

    def attend(h):
        outs[h] = tn(vl_ref[h % 2], wt_ref[h])

    def finish_out(h):
        c = heads_of(h)
        out = outs[h] * inv_ref[h, 0:1]
        t1 = out[HD:].astype(BF16)
        att_ref[:, c] = (out[:HD] + tn(upv_ref[:, c], t1)).T.astype(BF16)
        t1_rows = nn(perm_ref[...], t1).astype(BF16)
        gu_ref[1, :, c] = nn(t1_rows, cot_ref[:, c])

    def finish_query(h):
        dq = (dqs[h] * (inv_ref[h, 0:1] * SCALE)).astype(BF16)
        gu_ref[0, :, heads_of(h)] = nt(lowqp_ref[...], dq)
        lgq_ref[...] += nn(upq_ref[:, heads_of(h)], dq)

    for i in range(GH + 2):
        if i < GH:
            prepare(i)
        for r in range(4):
            if i < GH:
                back(i, r)
            if 1 <= i <= GH:
                shift(i - 1, r)
        if i < GH:
            attend(i)
        if 1 <= i <= GH:
            finish_out(i - 1)
        if i >= 2:
            finish_query(i - 2)

    dp, count, _ = up_mine.shape
    for i in range(count):
        which, row, h = i // (count // 2), i // GH % (R // dp), i % GH
        up_ref[step, :, i, :] = gu_ref[which, row * dp : (row + 1) * dp, heads_of(h)]

    @pl.when(last_step)
    def _():
        first = core_ref[0, 0] == 0
        up_mine[...] = jnp.where(first, up_ref[0], up_ref[1]).astype(BF16)
        up_other[...] = jnp.where(first, up_ref[1], up_ref[0]).astype(BF16)
        if downs:
            query = functools.reduce(jnp.add, [ref[...] for ref in low_refs[3:]], lgq_ref[...])
            value = functools.reduce(jnp.add, [ref[...].astype(F32) for ref in low_refs[:3]], here_ref[...])
            low = jnp.concatenate([query.T, value], axis=1).astype(BF16)
            fetch.wait()
            down(core_ref, held_ref, low, down_mine, down_other)


def down(core_ref, hidden_ref, low, mine_ref, other_ref):
    first = core_ref[0, 0] == 0
    dests, rows, _ = mine_ref.shape
    rows //= 2
    group = min(8, dests)
    for g in range(dests // group):
        res = tn(hidden_ref[:, 2 * rows * group * g : 2 * rows * group * (g + 1)], low)
        for d in range(group):
            a0 = res[2 * d * rows : (2 * d + 1) * rows]
            a1 = res[(2 * d + 1) * rows : (2 * d + 2) * rows]
            for ref, a in ((mine_ref, jnp.where(first, a0, a1)), (other_ref, jnp.where(first, a1, a0))):
                ref[g * group + d] = jnp.concatenate([a[:, :R], a[:, R:]], axis=0).astype(BF16)


def col(off):
    return pl.BlockSpec((ROWS, GH * HD), lambda i: (0, i + off))


def colup(off):
    return pl.BlockSpec((R, GH * HD), lambda i: (0, i + off))


def const(shape):
    return pl.BlockSpec(shape, lambda i: (0,) * len(shape))


def per_head(shape, off):
    return pl.BlockSpec((GH,) + shape, lambda i: (i + off,) + (0,) * len(shape))


def params():
    return pltpu.CompilerParams(dimension_semantics=("arbitrary",), vmem_limit_bytes=60 * 2**20)


def weight_call(c0, n, me, before, bias, query_base, lowq, upq, cot, upv, own, sib, zs, zd):
    keys = 4 * ROWS
    sums = jax.ShapeDtypeStruct((4, ROWS, R), F32)
    part = jax.ShapeDtypeStruct((ROWS, R), BF16)
    scratch = [pltpu.VMEM((2, keys, ROWS), F32), pltpu.VMEM((2, ROWS, HD), BF16)]
    if c0:
        extra, taken = [jax.ShapeDtypeStruct((ROWS, R), F32), part, part, part], [before]
        scratch = [pltpu.VMEM(sums.shape, F32), *scratch]
    else:
        extra, taken = [sums], []
    return pl.pallas_call(
        functools.partial(weight_kernel, c0),
        grid=(n,),
        in_specs=[
            pl.BlockSpec(memory_space=pltpu.SMEM),
            pl.BlockSpec(memory_space=pltpu.SMEM),
            col(c0), const((ROWS, R)), colup(c0), col(c0), colup(c0),
            col(c0), col(c0), col(0), col(0),
            *[const(sums.shape) for _ in taken],
        ],
        out_specs=[
            per_head((keys, ROWS), 0), per_head((8, ROWS), 0), col(0), *[const(out.shape) for out in extra],
        ],
        out_shape=[
            jax.ShapeDtypeStruct((n * GH, keys, ROWS), BF16),
            jax.ShapeDtypeStruct((n * GH, 8, ROWS), F32),
            jax.ShapeDtypeStruct((ROWS, n * GH * HD), BF16),
            *extra,
        ],
        scratch_shapes=scratch,
        compiler_params=params(),
        cost_estimate=pl.CostEstimate(
            flops=1_000_000, bytes_accessed=1_000, transcendentals=0
        ),
        name="attention_weights",
    )(me.reshape(1, 1), bias, query_base, lowq, upq, cot, upv, own, sib, zs, zd, *taken)


def grad_call(c0, n, kc0, core, att, wt, inv, keys, vals, lows, cot, g, upq, upv, lowqp, perm, dp, downs=None):
    off = c0 - kc0
    args = [wt, inv, *keys, *vals, *[low for low, _ in lows], cot, g, upq, upv, lowqp, perm]
    specs = [
        per_head((4 * ROWS, ROWS), off), per_head((8, ROWS), off),
        col(c0), col(c0), col(off), col(off),
        col(c0), col(c0), col(0), col(0),
        *[pl.BlockSpec((ROWS, R), functools.partial(lambda at, i: (0, at), at)) for _, at in lows],
        col(c0), col(off), colup(c0), colup(c0), const((R, ROWS)), const((R, R)),
    ]
    alias = {}
    if att is not None:
        alias = {len(args): 0}
        args.append(att)
        specs.append(pl.BlockSpec(memory_space=pl.ANY))
    args.append(core.reshape(1, 1))
    specs.append(pl.BlockSpec(memory_space=pltpu.SMEM))
    packed = (dp, 2 * (R // dp) * GH, HD)
    outs = [
        jax.ShapeDtypeStruct((ROWS, HEADS * HD), BF16),
        jax.ShapeDtypeStruct((R, ROWS), F32),
        jax.ShapeDtypeStruct(packed, BF16),
        jax.ShapeDtypeStruct(packed, BF16),
    ]
    out_specs = [col(c0), *[const(out.shape) for out in outs[1:]]]
    scratch = [
        pltpu.VMEM((2, 4 * ROWS, HD + R), BF16),
        pltpu.VMEM((2, 4 * ROWS, ROWS), F32),
        pltpu.VMEM((2, 4 * ROWS, ROWS), BF16),
        pltpu.VMEM((2, R, GH * HD), F32),
        pltpu.VMEM((n,) + packed, F32),
    ]
    if downs:
        hidden, *lows = downs
        args += [hidden, *lows]
        specs += [pl.BlockSpec(memory_space=pl.ANY), *[const(low.shape) for low in lows]]
        halves = (2 * dp, hidden.shape[1] // (2 * dp), R)
        outs += [jax.ShapeDtypeStruct(halves, BF16)] * 2
        out_specs += [const(halves)] * 2
        scratch += [pltpu.VMEM(hidden.shape, BF16), pltpu.SemaphoreType.DMA]
    return pl.pallas_call(
        functools.partial(grad_kernel, att is not None, bool(downs)),
        grid=(n,),
        in_specs=specs,
        out_specs=out_specs,
        out_shape=outs,
        scratch_shapes=scratch,
        input_output_aliases=alias,
        compiler_params=params(),
        cost_estimate=pl.CostEstimate(flops=1_000_000, bytes_accessed=1_000, transcendentals=0),
        name="attention_grads",
    )(*args)


DP = ("x", "zh", "y")
CORE_SWAP = [(0, 1), (1, 0)]


def over_core(a):
    return lax.ppermute(a, "core", CORE_SWAP)


def over_z(a):
    return lax.ppermute(a, "zl", CORE_SWAP)


def over_z_and_core(a):
    return lax.ppermute(a, ("zl", "core"), [(0, 3), (1, 2), (2, 1), (3, 0)])


def over_far_z(a):
    return lax.ppermute(a, ("zh", "zl"), [(0, 3), (1, 2), (2, 1), (3, 0)])


def per_device(
    hidden, query_base, key_base, value_base, cotangent,
    down_query, down_value, up_query, up_value, key_blocks, block_counts,
):
    dp = lax.axis_size(DP)
    core = lax.axis_index("core")
    me = lax.axis_index("zl") * 2 + core
    after = lax.optimization_barrier

    def columns(a, c0, n):
        return a[:, c0 * GH * HD : (c0 + n) * GH * HD]

    k_first = columns(key_base, *K_CHUNKS[0])
    key_rest, value_rest, key_blocks, block_counts, k_first = after(
        (key_base, value_base, key_blocks, block_counts, k_first)
    )
    k_zs = [over_z(k_first)]
    k_sib = over_core(key_rest)

    listed = jnp.arange(key_blocks.shape[2])[None, None, :] < block_counts[:, :, None]
    allowed = jnp.any((key_blocks[..., None] == jnp.arange(NB)) & listed[..., None], axis=2)
    bias = jnp.where(allowed, 0.0, -1e30).astype(F32).reshape(GH, NB * NB)
    bias = jnp.stack([bias, over_far_z(bias)])
    bias = jnp.stack([bias, over_core(bias)], axis=1).reshape(HEADS, NB * NB)

    low_value = nn(hidden, down_value).astype(BF16)
    low_query = nn(hidden, down_query).astype(BF16)
    key_rest, low_query = after((key_rest, low_query))
    k_second = columns(key_rest, *K_CHUNKS[1])
    v_first = jnp.concatenate([columns(value_rest, *V_CHUNKS[0]), low_value], axis=1)
    k_zs.append(over_z(k_second))
    k_zs[0], low_query, bias = after((k_zs[0], low_query, bias))
    k_zd = [over_core(k_zs[0])]
    v_zs = [over_z(v_first)]
    v_sib = over_core(value_base)
    low_sib = over_core(low_value)

    weights, lgv = [], [None]
    for i, (c0, n) in enumerate(K_CHUNKS):
        if i:
            value_rest, arrived, weights[-1] = after((value_rest, k_zs[i], weights[-1]))
            k_zd.append(over_core(arrived))
            v_zs.append(over_z(columns(value_rest, *V_CHUNKS[1])))
        wt, inv, g, *lgv = weight_call(
            c0, n, me, lgv[0], bias, query_base, low_query, up_query, cotangent, up_value,
            key_base, k_sib, k_zs[i], k_zd[i],
        )
        weights.append([wt, inv, g])
    lgv = [lgv[0], over_core(lgv[1]), over_z(lgv[2]), over_z_and_core(lgv[3])]

    att, lgqs, ups, v_zd = None, [], [], []
    for i, (c0, n) in enumerate(V_CHUNKS):
        which = [w for w, (a, m) in enumerate(K_CHUNKS) if a <= c0 < a + m][0]
        if i:
            arrived, att = after((v_zs[i], att))
        else:
            arrived, weights[-1], low_query, turn = after((v_zs[i], weights[-1], low_query, me * 0 + jnp.arange(R)))
            low_query_p = low_query.T.reshape(dp, R // dp, ROWS).transpose(1, 0, 2).reshape(R, ROWS)
            turn = turn % dp * (R // dp) + turn // dp
            perm = (turn[:, None] == jnp.arange(R)[None, :]).astype(BF16)
        v_zd.append(over_core(arrived))
        if not i:
            lows = [(low_value, 0), (low_sib, 0), (v_zs[0], 2 * GH), (v_zd[0], 2 * GH)]
        wt, inv, g = weights[which]
        att, lgq, *pair = grad_call(
            c0, n, K_CHUNKS[which][0], core, att, wt, inv,
            (key_base, k_sib, k_zs[which], k_zd[which]), (value_base, v_sib, v_zs[i], v_zd[i]),
            lows, cotangent, g, up_query, up_value, low_query_p, perm, dp,
            downs=(hidden, *lgv, *lgqs) if i else None,
        )
        lgqs.append(lgq)
        ups.append(pair)

    def both(mine, other):
        return (mine.astype(F32) + over_core(other).astype(F32)).astype(BF16)

    up = jnp.stack([both(*ups[0]), both(*ups[1][:2])], axis=1)
    down_sum = both(*ups[1][2:])
    payload = jnp.concatenate([down_sum, up.reshape(2 * dp, -1, HD)], axis=1)
    landed = lax.all_to_all(payload, DP + ("zl",), 0, 0, tiled=True)
    total = jnp.sum(landed.astype(F32), axis=0)
    rows = hidden.shape[1] // (4 * dp)
    grad_down = total[: 2 * rows].reshape(2, rows, R).transpose(1, 0, 2)
    grad_up = total[2 * rows :].reshape(2, R // dp, GH * HD).transpose(1, 0, 2)
    return att, grad_down, grad_up


def solution(mesh):
    dp = mesh.devices.shape[0]
    side = math.isqrt(dp // 2)
    fine = Mesh(mesh.devices.reshape(side, 2, side, 2, 2), DP + ("zl", "core"))
    everyone = DP + ("zl", "core")
    tokens = P(everyone, None)
    return jax.shard_map(
        per_device,
        mesh=fine,
        in_specs=(
            tokens, tokens, tokens, tokens, tokens, P(), P(), P(), P(),
            P(("zl", "core"), None, None), P(("zl", "core"), None),
        ),
        out_specs=(tokens, P(everyone, None, None), P(DP, None, ("zl", "core"))),
        check_vma=False,
    )
```

time: 197 us -> 140 us (0.71)
  local copies, waits for them, and re-layouts: 35.7 us -> 10.9 us
  Pallas kernels: 57.1 us -> 44.6 us
  other arithmetic: 11.1 us -> 4.46 us
  blocking collectives: 45.4 us -> 39.5 us
  waiting for transfers between devices: 27 us -> 21.5 us
    ppermute x8 -> x5, waiting for transfers between devices: 24.9 us -> 11.1 us  [over_z(): return lax.ppermute(a, 'zl', CORE_SWAP)]
    pallas_call x6 -> x4, Pallas kernels: 57.1 us -> 44.6 us  [the longest x2 24.2 us: grad_call(): pl.pallas_call(functools.partial(grad_kernel, att is not None, bool(downs...]
    unnamed x55 -> x38, local copies, waits for them, and re-layouts: 11.5 us -> 3.97 us
    all_gather x1 -> x0, blocking collectives: 5.49 us -> none  [per_device(): bias = lax.all_gather(bias, ('zl', 'core'), axis=0, tiled=True)]
    convert_element_type x3 -> x0, local copies, waits for them, and re-layouts: 5.14 us -> none  [the longest x1 4.39 us: per_device(): down = lax.dot_general(hidden, low_grads, (((0,), (0,)), ((), ())), prefe...]
    convert_element_type x4 -> x2, other arithmetic: 5.29 us -> 1.04 us  [the longest x1 0.7 us: per_device(): perm = (turn[:, None] == jnp.arange(R)[None, :]).astype(BF16)]
    ppermute x13 -> x12, waiting for transfers between devices: 2.1 us -> 6.29 us  [over_core(): return lax.ppermute(a, 'core', CORE_SWAP)]
    pallas_call x2 -> x0, local copies, waits for them, and re-layouts: 4.11 us -> none  [weight_call(): pl.pallas_call(functools.partial(weight_kernel, h0), grid=(nh,), in_specs...]
  transfers between devices with their start and end apart: 21 -> 19, of which waited for: 5 -> 10; matrix products, arithmetic and copies ran while one was open for 12% -> 11% of each run, Pallas kernels for 29% -> 22%
where the time goes in v2:
time: 140 us
  Pallas kernels  44.6 us (32%)
  blocking collectives  39.5 us (28%)
  waiting for transfers between devices  21.5 us (15%)
  starting transfers between devices  12.1 us (9%)
  local copies, waits for them, and re-layouts  10.9 us (8%)
  matrix products  5.91 us (4%)
  other arithmetic  4.46 us (3%)
    all_to_all x1, blocking collectives, per_device(): landed = lax.all_to_all(payload, DP + ('zl',), 0, 0, tiled=True)  39.5 us
    pallas_call x2, Pallas kernels, grad_call(): pl.pallas_call(functools.partial(grad_kernel, att is not None, bool(downs...  24.2 us
    pallas_call x2, Pallas kernels, weight_call(): pl.pallas_call(functools.partial(weight_kernel, c0), grid=(n,), in_specs=...  20.4 us
    ppermute x5, waiting for transfers between devices, over_z(): return lax.ppermute(a, 'zl', CORE_SWAP)  11.1 us
    ppermute x5, starting transfers between devices, over_z(): return lax.ppermute(a, 'zl', CORE_SWAP)  7.58 us
    ppermute x12, waiting for transfers between devices, over_core(): return lax.ppermute(a, 'core', CORE_SWAP)  6.29 us
    dot_general x2, matrix products, nn(): lax.dot_general(a, b, (((1,), (0,)), ((), ())), preferred_element_type=F32)  5.91 us
    unnamed x38, local copies, waits for them, and re-layouts  3.97 us
  transfers between devices with their start and end apart: 19, of which 10 were waited for; matrix products, arithmetic and copies ran while one was open for 11% of the time, Pallas kernels for 22%

profile of v2, /device:TPU:0, one launch (start us, length us, event | category | flops | bytes accessed | tf_op | source)
XLA Modules:
  0.0 139.9 jit_solution(11474908739219384010)
XLA Ops:
  0.6 1.2 slice.18
  1.9 2.1 %collective-permute-start.1 = (bf16[256,1280]{1,0:T(8,128)(2,1)S(1)}, bf16[256,1280]{1,0:T(8,128)(2,1)}, u32[]{:S(2)}, u32[]{:S(2)}) collective-permute-start(bf16[256,1280]{1,0:T(8,128)(2,1)S(1)} %slice.18), channel_id=1, source_target_pairs={{0,2},{2,0},{1,3},{3,1},{4,6},{6,4},{5,7},{7,5},{8,10},{10,8},{9,1... | collective-permute-start | bytes 1966088 | tf_op jit(solution)/shard_map/ppermute | solution.py:359
  4.0 0.8 copy.27
  4.8 0.7 iota_compare_fusion.2
  5.7 2.5 %collective-permute-start.2 = (f32[5,64]{1,0:T(8,128)S(1)}, f32[5,64]{1,0:T(8,128)S(1)}, u32[]{:S(2)}, u32[]{:S(2)}) collective-permute-start(f32[5,64]{1,0:T(8,128)S(1)} %select_n.32), channel_id=1, source_target_pairs={{0,18},{2,16},{16,2},{18,0},{1,19},{3,17},{17,3},{19,1},{4,22},{6,... | collective-permute-start | bytes 3848 | tf_op jit(solution)/shard_map/ppermute | solution.py:367
  8.3 2.2 %collective-permute-done.2 = f32[5,64]{1,0:T(8,128)S(1)} collective-permute-done((f32[5,64]{1,0:T(8,128)S(1)}, f32[5,64]{1,0:T(8,128)S(1)}, u32[]{:S(2)}, u32[]{:S(2)}) %collective-permute-start.2) | collective-permute-done | bytes 1312 | tf_op jit(solution)/shard_map/ppermute | solution.py:367
  10.7 3.3 %convolution_convert_fusion.lowq_ref = bf16[256,128]{1,0:T(8,128)(2,1)} fusion(bf16[256,5120]{1,0:T(8,128)(2,1)} %rest_2_.1, bf16[5120,128]{1,0:T(8,128)(2,1)S(1)} %copy-done), kind=kOutput, calls=%fused_computation.3 | convolution fusion | flops 335577088 | bytes 3997696 | tf_op jit(solution)/shard_map/dot_general | solution.py:27
  14.6 4.2 %collective-permute-done.1.k2 = bf16[256,1280]{1,0:T(8,128)(2,1)} collective-permute-done((bf16[256,1280]{1,0:T(8,128)(2,1)S(1)}, bf16[256,1280]{1,0:T(8,128)(2,1)}, u32[]{:S(2)}, u32[]{:S(2)}) %collective-permute-start.1) | collective-permute-done | bytes 655392 | tf_op jit(solution)/shard_map/ppermute | solution.py:359
  18.8 0.9 slice.20
  19.7 1.7 %collective-permute-start.5 = (bf16[256,1280]{1,0:T(8,128)(2,1)}, bf16[256,1280]{1,0:T(8,128)(2,1)}, u32[]{:S(2)}, u32[]{:S(2)}) collective-permute-start(bf16[256,1280]{1,0:T(8,128)(2,1)} %slice.20), channel_id=1, source_target_pairs={{0,2},{2,0},{1,3},{3,1},{4,6},{6,4},{5,7},{7,5},{8,10},{10,8},{9,1... | collective-permute-start | bytes 1966088 | tf_op jit(solution)/shard_map/ppermute | solution.py:359
  21.5 2.6 %convolution_convert_fusion.1.l0 = bf16[256,128]{1,0:T(8,128)(2,1)S(1)} fusion(bf16[256,5120]{1,0:T(8,128)(2,1)} %rest_2_.1, bf16[5120,128]{1,0:T(8,128)(2,1)S(1)} %copy-done.4), kind=kOutput, calls=%fused_computation.4 | convolution fusion | flops 335577088 | bytes 3997696 | tf_op jit(solution)/shard_map/dot_general | solution.py:27
  24.1 0.9 pad_maximum_fusion.1
  25.3 9.8 %attention_weights.2 = (bf16[10,1024,256]{2,1,0:T(8,128)(2,1)}, f32[10,8,256]{2,1,0:T(8,128)}, bf16[256,1280]{1,0:T(8,128)(2,1)}, f32[4,256,128]{2,1,0:T(8,128)}) custom-call(s32[1,1]{1,0:T(1,128)} %bitcast.me_ref, f32[20,64]{1,0:T(8,128)} %reshape.57.bias_ref, bf16[256,2560]{1,0:T(8,128)(2,1)} %qb_ref.3, bf16[256,128]{1,0:T(8,128)(2,1)} %convolution_convert_fusion.lowq_ref, ...), custom_call_target="tpu_custom_call" | custom-call | flops 1000000 | bytes 1000 | tf_op jit(solution)/shard_map/attention_weights/pallas_call | solution.py:268
  35.1 2.5 %collective-permute-done.5.k2 = bf16[256,1280]{1,0:T(8,128)(2,1)} collective-permute-done((bf16[256,1280]{1,0:T(8,128)(2,1)}, bf16[256,1280]{1,0:T(8,128)(2,1)}, u32[]{:S(2)}, u32[]{:S(2)}) %collective-permute-start.5) | collective-permute-done | bytes 655392 | tf_op jit(solution)/shard_map/ppermute | solution.py:359
  38.1 2.8 %collective-permute-done.7.k3 = bf16[256,1280]{1,0:T(8,128)(2,1)} collective-permute-done((bf16[256,1280]{1,0:T(8,128)(2,1)}, bf16[256,1280]{1,0:T(8,128)(2,1)}, u32[]{:S(2)}, u32[]{:S(2)}) %collective-permute-start.7) | collective-permute-done | bytes 655392 | tf_op jit(solution)/shard_map/ppermute | solution.py:355
  40.9 10.6 %attention_weights.3 = (bf16[10,1024,256]{2,1,0:T(8,128)(2,1)}, f32[10,8,256]{2,1,0:T(8,128)}, bf16[256,1280]{1,0:T(8,128)(2,1)}, f32[256,128]{1,0:T(8,128)}, bf...) custom-call(s32[1,1]{1,0:T(1,128)} %bitcast.me_ref, f32[20,64]{1,0:T(8,128)} %reshape.57.bias_ref, ...), custom_call_target="tpu_custom_call" | custom-call | flops 1000000 | bytes 1000 | tf_op jit(solution)/shard_map/attention_weights/pallas_call | solution.py:268
  51.5 1.0 collective-permute-done.v2.l2
  52.5 0.9 slice.21
  53.5 1.7 %collective-permute-start.9 = (bf16[256,1280]{1,0:T(8,128)(2,1)}, bf16[256,1280]{1,0:T(8,128)(2,1)}, u32[]{:S(2)}, u32[]{:S(2)}) collective-permute-start(bf16[256,1280]{1,0:T(8,128)(2,1)} %slice.21), channel_id=1, source_target_pairs={{0,2},{2,0},{1,3},{3,1},{4,6},{6,4},{5,7},{7,5},{8,10},{10,8},{9,1... | collective-permute-start | bytes 1966088 | tf_op jit(solution)/shard_map/ppermute | solution.py:359
  55.4 0.7 fusion.4.perm_ref
  56.1 0.7 copy.29
  56.8 0.9 reshape.58
  59.0 11.0 %attention_grads.2 = (bf16[256,2560]{1,0:T(8,128)(2,1)}, f32[128,256]{1,0:T(8,128)}, bf16[32,40,128]{2,1,0:T(8,128)(2,1)}, bf16[32,40,128]{2,1,0:T(8,128)(2,1)}) custom-call(bf16[10,1024,256]{2,1,0:T(8,128)(2,1)} %get-tuple-element.67.wt_ref, f32[10,8,256]{2,1,0:T(8,128)} %get-tuple-element.68.inv_ref, bf16[256,2560]{1,0:T(8,128)(2,1)} %k0.7, ...), custom_call_target="tpu_custom_call" | custom-call | flops 1000000 | bytes 1000 | tf_op jit(solution)/shard_map/attention_grads/pallas_call | solution.py:336
  69.9 0.9 collective-permute-done.9.v2
  71.4 1.7 %collective-permute-start.14 = (bf16[256,128]{1,0:T(8,128)(2,1)S(1)}, bf16[256,128]{1,0:T(8,128)(2,1)S(1)}, u32[]{:S(2)}, u32[]{:S(2)}) collective-permute-start(bf16[256,128]{1,0:T(8,128)(2,1)S(1)} %copy-done.16), channel_id=1, source_target_pairs={{0,2},{2,0},{1,3},{3,1},{4,6},{6,4},{5,7},{7,5},{8,10},{10,8},{9,1... | collective-permute-start | bytes 196616 | tf_op jit(solution)/shard_map/ppermute | solution.py:359
  73.2 2.5 %collective-permute-done.14.rest_5_ = bf16[256,128]{1,0:T(8,128)(2,1)S(1)} collective-permute-done((bf16[256,128]{1,0:T(8,128)(2,1)S(1)}, bf16[256,128]{1,0:T(8,128)(2,1)S(1)}, u32[]{:S(2)}, u32[]{:S(2)}) %collective-permute-start.14) | collective-permute-done | bytes 65568 | tf_op jit(solution)/shard_map/ppermute | solution.py:359
  75.7 1.9 %collective-permute-done.15.rest_6_ = bf16[256,128]{1,0:T(8,128)(2,1)S(1)} collective-permute-done((bf16[256,128]{1,0:T(8,128)(2,1)S(1)}, bf16[256,128]{1,0:T(8,128)(2,1)S(1)}, u32[]{:S(2)}, u32[]{:S(2)}) %collective-permute-start.15) | collective-permute-done | bytes 65568 | tf_op jit(solution)/shard_map/ppermute | solution.py:363
  78.4 13.2 %attention_grads.3 = (bf16[256,2560]{1,0:T(8,128)(2,1)}, f32[128,256]{1,0:T(8,128)}, bf16[32,40,128]{2,1,0:T(8,128)(2,1)}, bf16[32,40,128]{2,1,0:T(8,128)(2,1)},...) custom-call(bf16[10,1024,256]{2,1,0:T(8,128)(2,1)} %get-tuple-element.64.wt_ref, ...), custom_call_target="tpu_custom_call", output_to_operand_aliasing={{0}: (20, {})} | custom-call | flops 1000000 | bytes 1000 | tf_op jit(solution)/shard_map/attention_grads/pallas_call | solution.py:336
  92.3 3.1 %collective-permute-done.17 = bf16[32,40,128]{2,1,0:T(8,128)(2,1)S(1)} collective-permute-done((bf16[32,40,128]{2,1,0:T(8,128)(2,1)S(1)}, bf16[32,40,128]{2,1,0:T(8,128)(2,1)S(1)}, u32[]{:S(2)}, u32[]{:S(2)}) %collective-permute-start.17) | collective-permute-done | bytes 327712 | tf_op jit(solution)/shard_map/ppermute | solution.py:355
  95.9 1.1 fusion.1
  97.1 1.2 copy-done.5
  98.8 39.5 %all_to_all.5 = bf16[64,120,128]{2,1,0:T(8,128)(2,1)S(1)} all-to-all(bf16[64,120,128]{2,1,0:T(8,128)(2,1)S(1)} %pad_maximum_fusion), channel_id=1, replica_groups=mesh['x'=4,'zh'=2,'y'=4,'zl'=2,'core'=2] {'x','zh','y','zl'}, dimensions={0} | all-to-all | bytes 3932160 | tf_op jit(solution)/shard_map/all_to_all | solution.py:449
  (83 shorter events, 8.1 us)
Async XLA Ops:
  0.6 10.0 %copy-start = (bf16[5120,128]{1,0:T(8,128)(2,1)S(1)}, bf16[5120,128]{1,0:T(8,128)(2,1)}, u32[]{:S(2)}) copy-start(bf16[5120,128]{1,0:T(8,128)(2,1)} %param.16) | copy-start | bytes 3932164
  1.9 16.9 %collective-permute-start.1 = (bf16[256,1280]{1,0:T(8,128)(2,1)S(1)}, bf16[256,1280]{1,0:T(8,128)(2,1)}, u32[]{:S(2)}, u32[]{:S(2)}) collective-permute-start(bf16[256,1280]{1,0:T(8,128)(2,1)S(1)} %slice.18), channel_id=1, source_target_pairs={{0,2},{2,0},{1,3},{3,1},{4,6},{6,4},{5,7},{7,5},{8,10},{10,8},{9,1... | collective-permute-start | bytes 1966088 | tf_op jit(solution)/shard_map/ppermute | solution.py:359
  4.0 21.4 %collective-permute-start.4 = (bf16[256,2560]{1,0:T(8,128)(2,1)}, bf16[256,2560]{1,0:T(8,128)(2,1)}, u32[]{:S(2)}, u32[]{:S(2)}) collective-permute-start(bf16[256,2560]{1,0:T(8,128)(2,1)} %k0.7), channel_id=1, source_target_pairs={{0,1},{1,0},{2,3},{3,2},{4,5},{5,4},{6,7},{7,6},{8,9},{9,8},{10,11... | collective-permute-start | bytes 3932168 | tf_op jit(solution)/shard_map/ppermute | solution.py:355
  5.7 4.8 %collective-permute-start.2 = (f32[5,64]{1,0:T(8,128)S(1)}, f32[5,64]{1,0:T(8,128)S(1)}, u32[]{:S(2)}, u32[]{:S(2)}) collective-permute-start(f32[5,64]{1,0:T(8,128)S(1)} %select_n.32), channel_id=1, source_target_pairs={{0,18},{2,16},{16,2},{18,0},{1,19},{3,17},{17,3},{19,1},{4,22},{6,... | collective-permute-start | bytes 3848 | tf_op jit(solution)/shard_map/ppermute | solution.py:367
  10.6 8.2 %copy-start.1 = (bf16[256,2560]{1,0:T(8,128)(2,1)S(1)}, bf16[256,2560]{1,0:T(8,128)(2,1)}, u32[]{:S(2)}) copy-start(bf16[256,2560]{1,0:T(8,128)(2,1)} %k0.7) | copy-start | bytes 3932164
  10.6 3.4 %collective-permute-start.3 = (f32[2,5,64]{2,1,0:T(8,128)S(1)}, f32[2,5,64]{2,1,0:T(8,128)S(1)}, u32[]{:S(2)}, u32[]{:S(2)}) collective-permute-start(f32[2,5,64]{2,1,0:T(8,128)S(1)} %get-tuple-element.96), channel_id=1, source_target_pairs={{0,1},{1,0},{2,3},{3,2},{4,5},{5,4},{6,7},{7,6},{8,9},{9,8},{10,11... | collective-permute-start | bytes 7688 | tf_op jit(solution)/shard_map/ppermute | solution.py:355
  14.6 6.9 %copy-start.4 = (bf16[5120,128]{1,0:T(8,128)(2,1)S(1)}, bf16[5120,128]{1,0:T(8,128)(2,1)}, u32[]{:S(2)}) copy-start(bf16[5120,128]{1,0:T(8,128)(2,1)} %param.17) | copy-start | bytes 3932164
  18.8 6.5 %collective-permute-start.6 = (bf16[256,1280]{1,0:T(8,128)(2,1)}, bf16[256,1280]{1,0:T(8,128)(2,1)}, u32[]{:S(2)}, u32[]{:S(2)}) collective-permute-start(bf16[256,1280]{1,0:T(8,128)(2,1)} %collective-permute-done.1.k2), channel_id=1, source_target_pairs={{0,1},{1,0},{2,3},{3,2},{4,5},{5,4},{6,7},{7,6},{8,9},{9,8},{10,11... | collective-permute-start | bytes 1966088 | tf_op jit(solution)/shard_map/ppermute | solution.py:355
  19.7 17.8 %collective-permute-start.5 = (bf16[256,1280]{1,0:T(8,128)(2,1)}, bf16[256,1280]{1,0:T(8,128)(2,1)}, u32[]{:S(2)}, u32[]{:S(2)}) collective-permute-start(bf16[256,1280]{1,0:T(8,128)(2,1)} %slice.20), channel_id=1, source_target_pairs={{0,2},{2,0},{1,3},{3,1},{4,6},{6,4},{5,7},{7,5},{8,10},{10,8},{9,1... | collective-permute-start | bytes 1966088 | tf_op jit(solution)/shard_map/ppermute | solution.py:359
  24.1 31.1 %copy-start.6 = (bf16[256,128]{1,0:T(8,128)(2,1)}, bf16[256,128]{1,0:T(8,128)(2,1)S(1)}, u32[]{:S(2)}) copy-start(bf16[256,128]{1,0:T(8,128)(2,1)S(1)} %convolution_convert_fusion.1.l0) | copy-start | bytes 196612
  25.0 27.5 %collective-permute-start = (bf16[256,1408]{1,0:T(8,128)(2,1)}, bf16[256,1408]{1,0:T(8,128)(2,1)S(1)}, u32[]{:S(2)}, u32[]{:S(2)}) collective-permute-start(bf16[256,1408]{1,0:T(8,128)(2,1)} %pad_maximum_fusion.1), channel_id=1, source_target_pairs={{0,2},{2,0},{1,3},{3,1},{4,6},{6,4},{5,7},{7,5},{8,10},{10,8},{9,1... | collective-permute-start | bytes 2162696 | tf_op jit(solution)/shard_map/ppermute | solution.py:359
  25.3 12.2 %copy-start.2 = (bf16[256,2560]{1,0:T(8,128)(2,1)S(1)}, bf16[256,2560]{1,0:T(8,128)(2,1)}, u32[]{:S(2)}) copy-start(bf16[256,2560]{1,0:T(8,128)(2,1)} %v0.3) | copy-start | bytes 3932164
  37.6 3.3 %collective-permute-start.7 = (bf16[256,1280]{1,0:T(8,128)(2,1)}, bf16[256,1280]{1,0:T(8,128)(2,1)}, u32[]{:S(2)}, u32[]{:S(2)}) collective-permute-start(bf16[256,1280]{1,0:T(8,128)(2,1)} %collective-permute-done.5.k2), channel_id=1, source_target_pairs={{0,1},{1,0},{2,3},{3,2},{4,5},{5,4},{6,7},{7,6},{8,9},{9,8},{10,11... | collective-permute-start | bytes 1966088 | tf_op jit(solution)/shard_map/ppermute | solution.py:355
  37.6 20.8 %collective-permute-start.8 = (bf16[256,2560]{1,0:T(8,128)(2,1)S(1)}, bf16[256,2560]{1,0:T(8,128)(2,1)}, u32[]{:S(2)}, u32[]{:S(2)}) collective-permute-start(bf16[256,2560]{1,0:T(8,128)(2,1)S(1)} %copy-done.2), channel_id=1, source_target_pairs={{0,1},{1,0},{2,3},{3,2},{4,5},{5,4},{6,7},{7,6},{8,9},{9,8},{10,11... | collective-permute-start | bytes 3932168 | tf_op jit(solution)/shard_map/ppermute | solution.py:355
  40.9 15.2 %copy-start.7 = (bf16[256,128]{1,0:T(8,128)(2,1)S(1)}, bf16[256,128]{1,0:T(8,128)(2,1)}, u32[]{:S(2)}) copy-start(bf16[256,128]{1,0:T(8,128)(2,1)} %convolution_convert_fusion.lowq_ref) | copy-start | bytes 196612
  52.5 5.8 %copy-start.3 = (bf16[256,1408]{1,0:T(8,128)(2,1)}, bf16[256,1408]{1,0:T(8,128)(2,1)S(1)}, u32[]{:S(2)}) copy-start(bf16[256,1408]{1,0:T(8,128)(2,1)S(1)} %collective-permute-done.v2.l2) | copy-start | bytes 2162692
  52.5 5.8 %collective-permute-start.10 = (bf16[256,1408]{1,0:T(8,128)(2,1)S(1)}, bf16[256,1408]{1,0:T(8,128)(2,1)}, u32[]{:S(2)}, u32[]{:S(2)}) collective-permute-start(bf16[256,1408]{1,0:T(8,128)(2,1)S(1)} %collective-permute-done.v2.l2), channel_id=1, source_target_pairs={{0,1},{1,0},{2,3},{3,2},{4,5},{5,4},{6,7},{7,6},{8,9},{9,8},{10,11... | collective-permute-start | bytes 2162696 | tf_op jit(solution)/shard_map/ppermute | solution.py:355
  53.5 17.4 %collective-permute-start.9 = (bf16[256,1280]{1,0:T(8,128)(2,1)}, bf16[256,1280]{1,0:T(8,128)(2,1)}, u32[]{:S(2)}, u32[]{:S(2)}) collective-permute-start(bf16[256,1280]{1,0:T(8,128)(2,1)} %slice.21), channel_id=1, source_target_pairs={{0,2},{2,0},{1,3},{3,1},{4,6},{6,4},{5,7},{7,5},{8,10},{10,8},{9,1... | collective-permute-start | bytes 1966088 | tf_op jit(solution)/shard_map/ppermute | solution.py:359
  55.2 3.1 %collective-permute-start.11 = (bf16[256,128]{1,0:T(8,128)(2,1)S(1)}, bf16[256,128]{1,0:T(8,128)(2,1)S(1)}, u32[]{:S(2)}, u32[]{:S(2)}) collective-permute-start(bf16[256,128]{1,0:T(8,128)(2,1)S(1)} %convolution_convert_fusion.1.l0), channel_id=1, source_target_pairs={{0,1},{1,0},{2,3},{3,2},{4,5},{5,4},{6,7},{7,6},{8,9},{9,8},{10,11... | collective-permute-start | bytes 196616 | tf_op jit(solution)/shard_map/ppermute | solution.py:355
  59.0 11.9 %copy-start.17 = (bf16[256,128]{1,0:T(8,128)(2,1)S(1)}, bf16[256,128]{1,0:T(8,128)(2,1)}, u32[]{:S(2)}) copy-start(bf16[256,128]{1,0:T(8,128)(2,1)} %get-tuple-element.78) | copy-start | bytes 196612
  59.0 12.4 %copy-start.16 = (bf16[256,128]{1,0:T(8,128)(2,1)S(1)}, bf16[256,128]{1,0:T(8,128)(2,1)}, u32[]{:S(2)}) copy-start(bf16[256,128]{1,0:T(8,128)(2,1)} %get-tuple-element.79) | copy-start | bytes 196612
  59.0 14.1 %copy-start.15 = (bf16[256,128]{1,0:T(8,128)(2,1)S(1)}, bf16[256,128]{1,0:T(8,128)(2,1)}, u32[]{:S(2)}) copy-start(bf16[256,128]{1,0:T(8,128)(2,1)} %get-tuple-element.80) | copy-start | bytes 196612
  70.9 6.6 %collective-permute-start.12 = (bf16[256,1280]{1,0:T(8,128)(2,1)}, bf16[256,1280]{1,0:T(8,128)(2,1)S(1)}, u32[]{:S(2)}, u32[]{:S(2)}) collective-permute-start(bf16[256,1280]{1,0:T(8,128)(2,1)} %collective-permute-done.9.v2), channel_id=1, source_target_pairs={{0,1},{1,0},{2,3},{3,2},{4,5},{5,4},{6,7},{7,6},{8,9},{9,8},{10,11... | collective-permute-start | bytes 1966088 | tf_op jit(solution)/shard_map/ppermute | solution.py:355
  70.9 2.3 %collective-permute-start.13 = (bf16[256,128]{1,0:T(8,128)(2,1)S(1)}, bf16[256,128]{1,0:T(8,128)(2,1)S(1)}, u32[]{:S(2)}, u32[]{:S(2)}) collective-permute-start(bf16[256,128]{1,0:T(8,128)(2,1)S(1)} %copy-done.17), channel_id=1, source_target_pairs={{0,1},{1,0},{2,3},{3,2},{4,5},{5,4},{6,7},{7,6},{8,9},{9,8},{10,11... | collective-permute-start | bytes 196616 | tf_op jit(solution)/shard_map/ppermute | solution.py:355
  71.4 4.3 %collective-permute-start.14 = (bf16[256,128]{1,0:T(8,128)(2,1)S(1)}, bf16[256,128]{1,0:T(8,128)(2,1)S(1)}, u32[]{:S(2)}, u32[]{:S(2)}) collective-permute-start(bf16[256,128]{1,0:T(8,128)(2,1)S(1)} %copy-done.16), channel_id=1, source_target_pairs={{0,2},{2,0},{1,3},{3,1},{4,6},{6,4},{5,7},{7,5},{8,10},{10,8},{9,1... | collective-permute-start | bytes 196616 | tf_op jit(solution)/shard_map/ppermute | solution.py:359
  73.1 4.4 %collective-permute-start.15 = (bf16[256,128]{1,0:T(8,128)(2,1)S(1)}, bf16[256,128]{1,0:T(8,128)(2,1)S(1)}, u32[]{:S(2)}, u32[]{:S(2)}) collective-permute-start(bf16[256,128]{1,0:T(8,128)(2,1)S(1)} %copy-done.15), channel_id=1, source_target_pairs={{0,3},{1,2},{2,1},{3,0},{4,7},{5,6},{6,5},{7,4},{8,11},{9,10},{10,... | collective-permute-start | bytes 196616 | tf_op jit(solution)/shard_map/ppermute | solution.py:363
  73.1 4.4 %copy-start.11 = (bf16[256,128]{1,0:T(8,128)(2,1)}, bf16[256,128]{1,0:T(8,128)(2,1)S(1)}, u32[]{:S(2)}) copy-start(bf16[256,128]{1,0:T(8,128)(2,1)S(1)} %collective-permute-done.13.rest_4_) | copy-start | bytes 196612
  78.4 13.4 %copy-start.14 = (bf16[32,40,128]{2,1,0:T(8,128)(2,1)S(1)}, bf16[32,40,128]{2,1,0:T(8,128)(2,1)}, u32[]{:S(2)}) copy-start(bf16[32,40,128]{2,1,0:T(8,128)(2,1)} %get-tuple-element.86) | copy-start | bytes 983044
  78.4 17.0 %copy-start.9 = (bf16[32,40,128]{2,1,0:T(8,128)(2,1)S(1)}, bf16[32,40,128]{2,1,0:T(8,128)(2,1)}, u32[]{:S(2)}) copy-start(bf16[32,40,128]{2,1,0:T(8,128)(2,1)} %get-tuple-element.85) | copy-start | bytes 983044
  91.6 5.5 %collective-permute-start.16 = (bf16[64,80,128]{2,1,0:T(8,128)(2,1)}, bf16[64,80,128]{2,1,0:T(8,128)(2,1)S(1)}, u32[]{:S(2)}, u32[]{:S(2)}) collective-permute-start(bf16[64,80,128]{2,1,0:T(8,128)(2,1)} %get-tuple-element.84), channel_id=1, source_target_pairs={{0,1},{1,0},{2,3},{3,2},{4,5},{5,4},{6,7},{7,6},{8,9},{9,8},{10,11... | collective-permute-start | bytes 3932168 | tf_op jit(solution)/shard_map/ppermute | solution.py:355
  91.8 3.6 %collective-permute-start.17 = (bf16[32,40,128]{2,1,0:T(8,128)(2,1)S(1)}, bf16[32,40,128]{2,1,0:T(8,128)(2,1)S(1)}, u32[]{:S(2)}, u32[]{:S(2)}) collective-permute-start(bf16[32,40,128]{2,1,0:T(8,128)(2,1)S(1)} %copy-done.14), channel_id=1, source_target_pairs={{0,1},{1,0},{2,3},{3,2},{4,5},{5,4},{6,7},{7,6},{8,9},{9,8},{10,11... | collective-permute-start | bytes 983048 | tf_op jit(solution)/shard_map/ppermute | solution.py:355
  92.2 3.7 %collective-permute-start.18 = (bf16[32,40,128]{2,1,0:T(8,128)(2,1)}, bf16[32,40,128]{2,1,0:T(8,128)(2,1)S(1)}, u32[]{:S(2)}, u32[]{:S(2)}) collective-permute-start(bf16[32,40,128]{2,1,0:T(8,128)(2,1)} %get-tuple-element.88), channel_id=1, source_target_pairs={{0,1},{1,0},{2,3},{3,2},{4,5},{5,4},{6,7},{7,6},{8,9},{9,8},{10,11... | collective-permute-start | bytes 983048 | tf_op jit(solution)/shard_map/ppermute | solution.py:355
  (6 other events, 8.0 us)

commit v3 on v2

--- a/solution.py
+++ b/solution.py
@@ -49,7 +49,7 @@
         before_ref, *rest = rest
     wt_ref, inv_ref, g_ref, *rest = rest
     if last_call:
-        here_ref, sib_ref, zs_ref, zd_ref, *rest = rest
+        here_ref, sib_ref, *rest = rest
     lgv_ref, z_ref, q_ref = rest
     first_half = lax.broadcasted_iota(jnp.int32, (1, ROWS), 1) < ROWS // 2
     me = me_ref[0, 0]
@@ -112,22 +112,24 @@
 
         @pl.when(step == pl.num_programs(0) - 1)
         def _():
-            here_ref[...] = lgv_ref[0]
-            for r, ref in enumerate((sib_ref, zs_ref, zd_ref)):
-                ref[...] = lgv_ref[r + 1].astype(BF16)
+            for i in range(2):
+                here_ref[i] = lgv_ref[2 * i]
+                sib_ref[i] = lgv_ref[2 * i + 1].astype(BF16)
 
 
 def grad_kernel(
-    aliased, downs,
+    first_call, downs,
     wt_ref, inv_ref, k0, k1, k2, k3, v0, v1, v2, v3, l0, l1, l2, l3,
     cot_ref, g_ref, upq_ref, upv_ref, lowqp_ref, perm_ref, *rest,
 ):
-    rest = list(rest[1:] if aliased else rest)
-    core_ref, *rest = rest
+    core_ref, *rest = rest[0 if first_call else 1 :]
+    if first_call:
+        near_ref, far_ref, *rest = rest
     if downs:
-        hidden_ref, here_ref, *low_refs = rest[:6]
-        rest = rest[6:]
+        hidden_ref, here_ref, there_ref, low_query_ref, *rest = rest
     att_ref, lgq_ref, up_mine, up_other, *rest = rest
+    if first_call:
+        here_ref, there_ref, *rest = rest
     if downs:
         down_mine, down_other, *rest = rest
     vl_ref, back_ref, sh_ref, gu_ref, up_ref, *rest = rest
@@ -142,6 +144,9 @@
     @pl.when(first_step)
     def _():
         lgq_ref[...] = jnp.zeros_like(lgq_ref)
+        if first_call:
+            here_ref[...] = near_ref[0] + far_ref[0].astype(F32)
+            there_ref[...] = (near_ref[1] + far_ref[1].astype(F32)).astype(BF16)
         for p in range(2):
             for r in range(4):
                 vl_ref[p, r * ROWS : (r + 1) * ROWS, HD:] = lows[r][...]
@@ -214,8 +219,8 @@
         up_mine[...] = jnp.where(first, up_ref[0], up_ref[1]).astype(BF16)
         up_other[...] = jnp.where(first, up_ref[1], up_ref[0]).astype(BF16)
         if downs:
-            query = functools.reduce(jnp.add, [ref[...] for ref in low_refs[3:]], lgq_ref[...])
-            value = functools.reduce(jnp.add, [ref[...].astype(F32) for ref in low_refs[:3]], here_ref[...])
+            query = low_query_ref[...] + lgq_ref[...]
+            value = here_ref[...] + there_ref[...].astype(F32)
             low = jnp.concatenate([query.T, value], axis=1).astype(BF16)
             fetch.wait()
             down(core_ref, held_ref, low, down_mine, down_other)
@@ -252,16 +257,15 @@
 
 
 def params():
-    return pltpu.CompilerParams(dimension_semantics=("arbitrary",), vmem_limit_bytes=60 * 2**20)
+    return pltpu.CompilerParams(dimension_semantics=("arbitrary",), vmem_limit_bytes=46 * 2**20)
 
 
 def weight_call(c0, n, me, before, bias, query_base, lowq, upq, cot, upv, own, sib, zs, zd):
     keys = 4 * ROWS
     sums = jax.ShapeDtypeStruct((4, ROWS, R), F32)
-    part = jax.ShapeDtypeStruct((ROWS, R), BF16)
     scratch = [pltpu.VMEM((2, keys, ROWS), F32), pltpu.VMEM((2, ROWS, HD), BF16)]
     if c0:
-        extra, taken = [jax.ShapeDtypeStruct((ROWS, R), F32), part, part, part], [before]
+        extra, taken = [jax.ShapeDtypeStruct((2, ROWS, R), dtype) for dtype in (F32, BF16)], [before]
         scratch = [pltpu.VMEM(sums.shape, F32), *scratch]
     else:
         extra, taken = [sums], []
@@ -293,7 +297,7 @@
     )(me.reshape(1, 1), bias, query_base, lowq, upq, cot, upv, own, sib, zs, zd, *taken)
 
 
-def grad_call(c0, n, kc0, core, att, wt, inv, keys, vals, lows, cot, g, upq, upv, lowqp, perm, dp, downs=None):
+def grad_call(c0, n, kc0, core, att, wt, inv, keys, vals, lows, cot, g, upq, upv, lowqp, perm, dp, low_sums, downs=None):
     off = c0 - kc0
     args = [wt, inv, *keys, *vals, *[low for low, _ in lows], cot, g, upq, upv, lowqp, perm]
     specs = [
@@ -310,6 +314,9 @@
         specs.append(pl.BlockSpec(memory_space=pl.ANY))
     args.append(core.reshape(1, 1))
     specs.append(pl.BlockSpec(memory_space=pltpu.SMEM))
+    if not downs:
+        args += low_sums
+        specs += [const(low.shape) for low in low_sums]
     packed = (dp, 2 * (R // dp) * GH, HD)
     outs = [
         jax.ShapeDtypeStruct((ROWS, HEADS * HD), BF16),
@@ -317,6 +324,8 @@
         jax.ShapeDtypeStruct(packed, BF16),
         jax.ShapeDtypeStruct(packed, BF16),
     ]
+    if not downs:
+        outs += [jax.ShapeDtypeStruct((ROWS, R), dtype) for dtype in (F32, BF16)]
     out_specs = [col(c0), *[const(out.shape) for out in outs[1:]]]
     scratch = [
         pltpu.VMEM((2, 4 * ROWS, HD + R), BF16),
@@ -334,7 +343,7 @@
         out_specs += [const(halves)] * 2
         scratch += [pltpu.VMEM(hidden.shape, BF16), pltpu.SemaphoreType.DMA]
     return pl.pallas_call(
-        functools.partial(grad_kernel, att is not None, bool(downs)),
+        functools.partial(grad_kernel, att is None, bool(downs)),
         grid=(n,),
         in_specs=specs,
         out_specs=out_specs,
@@ -359,10 +368,6 @@
     return lax.ppermute(a, "zl", CORE_SWAP)
 
 
-def over_z_and_core(a):
-    return lax.ppermute(a, ("zl", "core"), [(0, 3), (1, 2), (2, 1), (3, 0)])
-
-
 def over_far_z(a):
     return lax.ppermute(a, ("zh", "zl"), [(0, 3), (1, 2), (2, 1), (3, 0)])
 
@@ -397,8 +402,15 @@
     key_rest, low_query = after((key_rest, low_query))
     k_second = columns(key_rest, *K_CHUNKS[1])
     v_first = jnp.concatenate([columns(value_rest, *V_CHUNKS[0]), low_value], axis=1)
+    v_second = columns(value_rest, *V_CHUNKS[1])
+    low_query_p = low_query.T.reshape(dp, R // dp, ROWS).transpose(1, 0, 2).reshape(R, ROWS)
+    turn = jnp.arange(R)
+    turn = turn % dp * (R // dp) + turn // dp
+    perm = (turn[:, None] == jnp.arange(R)[None, :]).astype(BF16)
+    k_zs[0], low_query, low_query_p, perm, bias, k_second, v_second = after(
+        (k_zs[0], low_query, low_query_p, perm, bias, k_second, v_second)
+    )
     k_zs.append(over_z(k_second))
-    k_zs[0], low_query, bias = after((k_zs[0], low_query, bias))
     k_zd = [over_core(k_zs[0])]
     v_zs = [over_z(v_first)]
     v_sib = over_core(value_base)
@@ -407,44 +419,45 @@
     weights, lgv = [], [None]
     for i, (c0, n) in enumerate(K_CHUNKS):
         if i:
-            value_rest, arrived, weights[-1] = after((value_rest, k_zs[i], weights[-1]))
+            v_second, arrived, weights[-1] = after((v_second, k_zs[i], weights[-1]))
             k_zd.append(over_core(arrived))
-            v_zs.append(over_z(columns(value_rest, *V_CHUNKS[1])))
+            v_zs.append(over_z(v_second))
         wt, inv, g, *lgv = weight_call(
             c0, n, me, lgv[0], bias, query_base, low_query, up_query, cotangent, up_value,
             key_base, k_sib, k_zs[i], k_zd[i],
         )
         weights.append([wt, inv, g])
-    lgv = [lgv[0], over_core(lgv[1]), over_z(lgv[2]), over_z_and_core(lgv[3])]
-
-    att, lgqs, ups, v_zd = None, [], [], []
+    near, far = lgv[0], over_core(lgv[1])
+
+    def both(mine, other):
+        return (mine.astype(F32) + over_core(other).astype(F32)).astype(BF16)
+
+    att, v_zd = None, []
     for i, (c0, n) in enumerate(V_CHUNKS):
         which = [w for w, (a, m) in enumerate(K_CHUNKS) if a <= c0 < a + m][0]
         if i:
             arrived, att = after((v_zs[i], att))
         else:
-            arrived, weights[-1], low_query, turn = after((v_zs[i], weights[-1], low_query, me * 0 + jnp.arange(R)))
-            low_query_p = low_query.T.reshape(dp, R // dp, ROWS).transpose(1, 0, 2).reshape(R, ROWS)
-            turn = turn % dp * (R // dp) + turn // dp
-            perm = (turn[:, None] == jnp.arange(R)[None, :]).astype(BF16)
+            arrived, weights[-1] = after((v_zs[i], weights[-1]))
         v_zd.append(over_core(arrived))
         if not i:
             lows = [(low_value, 0), (low_sib, 0), (v_zs[0], 2 * GH), (v_zd[0], 2 * GH)]
+        else:
+            v_zd[i], up_first = after((v_zd[i], up_first))
         wt, inv, g = weights[which]
-        att, lgq, *pair = grad_call(
+        att, *made = grad_call(
             c0, n, K_CHUNKS[which][0], core, att, wt, inv,
             (key_base, k_sib, k_zs[which], k_zd[which]), (value_base, v_sib, v_zs[i], v_zd[i]),
             lows, cotangent, g, up_query, up_value, low_query_p, perm, dp,
-            downs=(hidden, *lgv, *lgqs) if i else None,
+            (near, far), downs=(hidden, lgv_here, over_z(lgv_there), lgq) if i else None,
         )
-        lgqs.append(lgq)
-        ups.append(pair)
-
-    def both(mine, other):
-        return (mine.astype(F32) + over_core(other).astype(F32)).astype(BF16)
-
-    up = jnp.stack([both(*ups[0]), both(*ups[1][:2])], axis=1)
-    down_sum = both(*ups[1][2:])
+        if not i:
+            lgq, up_mine, up_other, lgv_here, lgv_there = made
+            up_first = both(up_mine, up_other)
+    up_mine, up_other, down_mine, down_other = made[1:]
+
+    up = jnp.stack([up_first, both(up_mine, up_other)], axis=1)
+    down_sum = both(down_mine, down_other)
     payload = jnp.concatenate([down_sum, up.reshape(2 * dp, -1, HD)], axis=1)
     landed = lax.all_to_all(payload, DP + ("zl",), 0, 0, tiled=True)
     total = jnp.sum(landed.astype(F32), axis=0)

time: 140 us -> 135 us (0.964)
  waiting for transfers between devices: 21.5 us -> 27.3 us
  Pallas kernels: 44.6 us -> 40.7 us
  blocking collectives: 39.5 us -> 36.8 us
  starting transfers between devices: 12.1 us -> 9.45 us
  matrix products: 5.91 us -> 3.79 us
  local copies, waits for them, and re-layouts: 10.9 us -> 12.8 us
  other arithmetic: 4.46 us -> 2.86 us
    ppermute x5, waiting for transfers between devices: 11.1 us -> 19.1 us  [over_z(): return lax.ppermute(a, 'zl', CORE_SWAP)]
    ppermute x5, starting transfers between devices: 7.58 us -> 2.6 us  [over_z(): return lax.ppermute(a, 'zl', CORE_SWAP)]
    unnamed x38 -> x28, local copies, waits for them, and re-layouts: 3.97 us -> 6.96 us
    all_to_all x1, blocking collectives: 39.5 us -> 36.8 us  [per_device(): landed = lax.all_to_all(payload, DP + ('zl',), 0, 0, tiled=True)]
    ppermute x1, waiting for transfers between devices: 2.22 us -> 0.01 us  [over_far_z(): return lax.ppermute(a, ('zh', 'zl'), [(0, 3), (1, 2), (2, 1), (3, 0)])]
    dot_general x2, matrix products: 5.91 us -> 3.79 us  [nn(): lax.dot_general(a, b, (((1,), (0,)), ((), ())), preferred_element_type=F32)]
    pallas_call x2, Pallas kernels: 24.2 us -> 22.2 us  [grad_call(): pl.pallas_call(functools.partial(grad_kernel, att is None, bool(downs)),...]
    pallas_call x2, Pallas kernels: 20.4 us -> 18.5 us  [weight_call(): pl.pallas_call(functools.partial(weight_kernel, c0), grid=(n,), in_specs=...]
  transfers between devices with their start and end apart: 19 -> 18, of which waited for: 10 -> 9; matrix products, arithmetic and copies ran while one was open for 11% -> 6% of each run, Pallas kernels for 22% -> 21%
where the time goes in v3:
time: 135 us
  Pallas kernels  40.7 us (30%)
  blocking collectives  36.8 us (27%)
  waiting for transfers between devices  27.3 us (20%)
  local copies, waits for them, and re-layouts  12.8 us (9%)
  starting transfers between devices  9.45 us (7%)
  matrix products  3.79 us (3%)
  other arithmetic  2.86 us (2%)
    all_to_all x1, blocking collectives, per_device(): landed = lax.all_to_all(payload, DP + ('zl',), 0, 0, tiled=True)  36.8 us
    pallas_call x2, Pallas kernels, grad_call(): pl.pallas_call(functools.partial(grad_kernel, att is None, bool(downs)),...  22.2 us
    ppermute x5, waiting for transfers between devices, over_z(): return lax.ppermute(a, 'zl', CORE_SWAP)  19.1 us
    pallas_call x2, Pallas kernels, weight_call(): pl.pallas_call(functools.partial(weight_kernel, c0), grid=(n,), in_specs=...  18.5 us
    ppermute x12, waiting for transfers between devices, over_core(): return lax.ppermute(a, 'core', CORE_SWAP)  8.22 us
    unnamed x28, local copies, waits for them, and re-layouts  6.96 us
    slice x3, local copies, waits for them, and re-layouts, columns(): return a[:, c0 * GH * HD:(c0 + n) * GH * HD]  4.65 us
    ppermute x1, starting transfers between devices, over_far_z(): return lax.ppermute(a, ('zh', 'zl'), [(0, 3), (1, 2), (2, 1), (3, 0)])  4.16 us
  transfers between devices with their start and end apart: 18, of which 9 were waited for; matrix products, arithmetic and copies ran while one was open for 6% of the time, Pallas kernels for 21%

profile of v3, /device:TPU:0, one launch (start us, length us, event | category | flops | bytes accessed | tf_op | source)
XLA Modules:
  0.0 134.5 jit_solution(10431267874569232761)
XLA Ops:
  0.7 1.3 slice.18
  1.9 0.7 iota_compare_fusion.2
  2.6 0.8 copy.29
  3.7 4.2 %collective-permute-start.2 = (f32[5,64]{1,0:T(8,128)S(1)}, f32[5,64]{1,0:T(8,128)S(1)}, u32[]{:S(2)}, u32[]{:S(2)}) collective-permute-start(f32[5,64]{1,0:T(8,128)S(1)} %select_n.42), channel_id=1, source_target_pairs={{0,18},{2,16},{16,2},{18,0},{1,19},{3,17},{17,3},{19,1},{4,22},{6,... | collective-permute-start | bytes 3848 | tf_op jit(solution)/shard_map/ppermute | solution.py:372
  7.9 2.4 %fusion.7 = (bf16[256,1280]{1,0:T(8,128)(2,1)}, bf16[256,1280]{1,0:T(8,128)(2,1)}) fusion(bf16[256,2560]{1,0:T(8,128)(2,1)} %v0.3), kind=kLoop, calls=%fused_computation.27 | loop fusion | bytes 2621440 | tf_op jit(solution)/shard_map/slice | solution.py:385
  10.3 0.9 convolution_convert_fusion.lowq_ref
  11.3 0.6 collective-permute-start.3
  12.1 0.9 slice.20
  13.1 11.1 %collective-permute-done.1.k2 = bf16[256,1280]{1,0:T(8,128)(2,1)} collective-permute-done((bf16[256,1280]{1,0:T(8,128)(2,1)S(1)}, bf16[256,1280]{1,0:T(8,128)(2,1)}, u32[]{:S(2)}, u32[]{:S(2)}) %collective-permute-start.1) | collective-permute-done | bytes 655392 | tf_op jit(solution)/shard_map/ppermute | solution.py:368
  24.4 2.9 %convolution_convert_fusion.1.l0 = bf16[256,128]{1,0:T(8,128)(2,1)S(1)} fusion(bf16[256,5120]{1,0:T(8,128)(2,1)} %rest_2_.1, bf16[5120,128]{1,0:T(8,128)(2,1)} %param.17), kind=kOutput, calls=%fused_computation.4 | convolution fusion | flops 335577088 | bytes 3997696 | tf_op jit(solution)/shard_map/dot_general | solution.py:27
  27.4 0.9 pad_maximum_fusion.1
  28.3 1.7 %collective-permute-start = (bf16[256,1408]{1,0:T(8,128)(2,1)}, bf16[256,1408]{1,0:T(8,128)(2,1)}, u32[]{:S(2)}, u32[]{:S(2)}) collective-permute-start(bf16[256,1408]{1,0:T(8,128)(2,1)} %pad_maximum_fusion.1), channel_id=1, source_target_pairs={{0,2},{2,0},{1,3},{3,1},{4,6},{6,4},{5,7},{7,5},{8,10},{10,8},{9,1... | collective-permute-start | bytes 2162696 | tf_op jit(solution)/shard_map/ppermute | solution.py:368
  30.1 1.3 copy-done.2
  31.4 1.1 copy-done.4
  32.5 1.3 copy-done.6
  33.8 9.2 %attention_weights.2 = (bf16[10,1024,256]{2,1,0:T(8,128)(2,1)}, f32[10,8,256]{2,1,0:T(8,128)S(1)}, bf16[256,1280]{1,0:T(8,128)(2,1)S(1)}, f32[4,256,128]{2,1,0:T(8,128)S(1)}) custom-call(s32[1,1]{1,0:T(1,128)} %bitcast.me_ref, f32[20,64]{1,0:T(8,128)S(1)} %reshape.80.bias_ref, bf16[256,2560]{1,0:T(8,128)(2,1)S(1)} %copy-done.6, ...), custom_call_target="tpu_custom_call" | custom-call | flops 1000000 | bytes 1000 | tf_op jit(solution)/shard_map/attention_weights/pallas_call | solution.py:272
  43.5 1.8 %collective-permute-done.7.k3 = bf16[256,1280]{1,0:T(8,128)(2,1)S(1)} collective-permute-done((bf16[256,1280]{1,0:T(8,128)(2,1)}, bf16[256,1280]{1,0:T(8,128)(2,1)S(1)}, u32[]{:S(2)}, u32[]{:S(2)}) %collective-permute-start.7) | collective-permute-done | bytes 655392 | tf_op jit(solution)/shard_map/ppermute | solution.py:364
  45.3 9.2 %attention_weights.3 = (bf16[10,1024,256]{2,1,0:T(8,128)(2,1)}, f32[10,8,256]{2,1,0:T(8,128)S(1)}, bf16[256,1280]{1,0:T(8,128)(2,1)S(1)}, f32[2,256,128]{2,1,0:T(8,128)S(1)}, bf16[2,256,128]{2,1,0:T(8,128)(2,1)S(1)}) custom-call(s32[1,1]{1,0:T(1,128)} %bitcast.me_ref, f32[20,64]{1,0:T(8,128)S(1)} %reshape.80.bias_ref, bf16[256,2560]{1,0:T(8,128)(2,1)S(1)} %copy-done.6, ...), custom_call_target="tpu_custom_call" | custom-call | flops 1000000 | bytes 1000 | tf_op jit(solution)/shard_map/attention_weights/pallas_call | solution.py:272
  54.6 2.5 %collective-permute-done.v2.l2 = bf16[256,1408]{1,0:T(8,128)(2,1)} collective-permute-done((bf16[256,1408]{1,0:T(8,128)(2,1)}, bf16[256,1408]{1,0:T(8,128)(2,1)}, u32[]{:S(2)}, u32[]{:S(2)}) %collective-permute-start) | collective-permute-done | bytes 720928 | tf_op jit(solution)/shard_map/ppermute | solution.py:368
  57.9 1.7 %collective-permute-done.11.l1 = bf16[256,128]{1,0:T(8,128)(2,1)S(1)} collective-permute-done((bf16[256,128]{1,0:T(8,128)(2,1)S(1)}, bf16[256,128]{1,0:T(8,128)(2,1)S(1)}, u32[]{:S(2)}, u32[]{:S(2)}) %collective-permute-start.11) | collective-permute-done | bytes 65568 | tf_op jit(solution)/shard_map/ppermute | solution.py:364
  59.6 1.1 copy-done.9
  60.7 10.1 %attention_grads.2 = (bf16[256,2560]{1,0:T(8,128)(2,1)}, f32[128,256]{1,0:T(8,128)S(1)}, bf16[32,40,128]{2,1,0:T(8,128)(2,1)S(1)}, bf16[32,40,128]{2,1,0:T(8,128...) custom-call(bf16[10,1024,256]{2,1,0:T(8,128)(2,1)} %get-tuple-element.73.wt_ref, ...), custom_call_target="tpu_custom_call" | custom-call | flops 1000000 | bytes 1000 | tf_op jit(solution)/shard_map/attention_grads/pallas_call | solution.py:345
  70.8 3.4 %collective-permute-done.9.v2 = bf16[256,1280]{1,0:T(8,128)(2,1)S(1)} collective-permute-done((bf16[256,1280]{1,0:T(8,128)(2,1)S(1)}, bf16[256,1280]{1,0:T(8,128)(2,1)S(1)}, u32[]{:S(2)}, u32[]{:S(2)}) %collective-permute-start.9) | collective-permute-done | bytes 655392 | tf_op jit(solution)/shard_map/ppermute | solution.py:368
  74.2 0.5 collective-permute-start.14
  75.0 1.8 %collective-permute-done.14 = bf16[32,40,128]{2,1,0:T(8,128)(2,1)S(1)} collective-permute-done((bf16[32,40,128]{2,1,0:T(8,128)(2,1)S(1)}, bf16[32,40,128]{2,1,0:T(8,128)(2,1)S(1)}, u32[]{:S(2)}, u32[]{:S(2)}) %collective-permute-start.14) | collective-permute-done | bytes 327712 | tf_op jit(solution)/shard_map/ppermute | solution.py:364
  76.9 2.1 %collective-permute-done.15.rest_4_ = bf16[256,128]{1,0:T(8,128)(2,1)S(1)} collective-permute-done((bf16[256,128]{1,0:T(8,128)(2,1)S(1)}, bf16[256,128]{1,0:T(8,128)(2,1)S(1)}, u32[]{:S(2)}, u32[]{:S(2)}) %collective-permute-start.15) | collective-permute-done | bytes 65568 | tf_op jit(solution)/shard_map/ppermute | solution.py:368
  79.0 12.1 %attention_grads.3 = (bf16[256,2560]{1,0:T(8,128)(2,1)}, f32[128,256]{1,0:T(8,128)}, bf16[32,40,128]{2,1,0:T(8,128)(2,1)S(1)}, bf16[32,40,128]{2,1,0:T(8,128)(2,...) custom-call(bf16[10,1024,256]{2,1,0:T(8,128)(2,1)} %get-tuple-element.70.wt_r, ...), custom_call_target="tpu_custom_call", output_to_operand_aliasing={{0}: (20, {})} | custom-call | flops 1000000 | bytes 1000 | tf_op jit(solution)/shard_map/attention_grads/pallas_call | solution.py:345
  91.7 2.6 %collective-permute-done.17 = bf16[32,40,128]{2,1,0:T(8,128)(2,1)S(1)} collective-permute-done((bf16[32,40,128]{2,1,0:T(8,128)(2,1)S(1)}, bf16[32,40,128]{2,1,0:T(8,128)(2,1)S(1)}, u32[]{:S(2)}, u32[]{:S(2)}) %collective-permute-start.17) | collective-permute-done | bytes 327712 | tf_op jit(solution)/shard_map/ppermute | solution.py:364
  94.9 0.8 copy-done.11
  96.2 36.8 %all_to_all.5 = bf16[64,120,128]{2,1,0:T(8,128)(2,1)S(1)} all-to-all(bf16[64,120,128]{2,1,0:T(8,128)(2,1)S(1)} %pad_maximum_fusion), channel_id=1, replica_groups=mesh['x'=4,'zh'=2,'y'=4,'zl'=2,'core'=2] {'x','zh','y','zl'}, dimensions={0} | all-to-all | bytes 3932160 | tf_op jit(solution)/shard_map/all_to_all | solution.py:462
  133.3 0.6 copy.32
  133.9 0.6 copy.33
  (68 shorter events, 4.5 us)
Async XLA Ops:
  0.6 9.7 %copy-start = (bf16[5120,128]{1,0:T(8,128)(2,1)S(1)}, bf16[5120,128]{1,0:T(8,128)(2,1)}, u32[]{:S(2)}) copy-start(bf16[5120,128]{1,0:T(8,128)(2,1)} %param.16) | copy-start | bytes 3932164
  0.6 7.2 %copy-start.1 = (bf16[256,2560]{1,0:T(8,128)(2,1)S(1)}, bf16[256,2560]{1,0:T(8,128)(2,1)}, u32[]{:S(2)}) copy-start(bf16[256,2560]{1,0:T(8,128)(2,1)} %k0.7) | copy-start | bytes 3932164
  3.7 6.6 %copy-start.7 = (bf16[256,5120]{1,0:T(8,128)(2,1)S(1)}, bf16[256,5120]{1,0:T(8,128)(2,1)}, u32[]{:S(2)}) copy-start(bf16[256,5120]{1,0:T(8,128)(2,1)} %rest_2_.1) | copy-start | bytes 7864324
  3.7 7.6 %collective-permute-start.2 = (f32[5,64]{1,0:T(8,128)S(1)}, f32[5,64]{1,0:T(8,128)S(1)}, u32[]{:S(2)}, u32[]{:S(2)}) collective-permute-start(f32[5,64]{1,0:T(8,128)S(1)} %select_n.42), channel_id=1, source_target_pairs={{0,18},{2,16},{16,2},{18,0},{1,19},{3,17},{17,3},{19,1},{4,22},{6,... | collective-permute-start | bytes 3848 | tf_op jit(solution)/shard_map/ppermute | solution.py:372
  7.9 16.3 %collective-permute-start.1 = (bf16[256,1280]{1,0:T(8,128)(2,1)S(1)}, bf16[256,1280]{1,0:T(8,128)(2,1)}, u32[]{:S(2)}, u32[]{:S(2)}) collective-permute-start(bf16[256,1280]{1,0:T(8,128)(2,1)S(1)} %slice.18), channel_id=1, source_target_pairs={{0,2},{2,0},{1,3},{3,1},{4,6},{6,4},{5,7},{7,5},{8,10},{10,8},{9,1... | collective-permute-start | bytes 1966088 | tf_op jit(solution)/shard_map/ppermute | solution.py:368
  7.9 22.2 %collective-permute-start.4 = (bf16[256,2560]{1,0:T(8,128)(2,1)S(1)}, bf16[256,2560]{1,0:T(8,128)(2,1)}, u32[]{:S(2)}, u32[]{:S(2)}) collective-permute-start(bf16[256,2560]{1,0:T(8,128)(2,1)S(1)} %copy-done.1), channel_id=1, source_target_pairs={{0,1},{1,0},{2,3},{3,2},{4,5},{5,4},{6,7},{7,6},{8,9},{9,8},{10,11... | collective-permute-start | bytes 3932168 | tf_op jit(solution)/shard_map/ppermute | solution.py:364
  11.3 1.8 %collective-permute-start.3 = (f32[2,5,64]{2,1,0:T(8,128)S(1)}, f32[2,5,64]{2,1,0:T(8,128)S(1)}, u32[]{:S(2)}, u32[]{:S(2)}) collective-permute-start(f32[2,5,64]{2,1,0:T(8,128)S(1)} %get-tuple-element.106), channel_id=1, source_target_pairs={{0,1},{1,0},{2,3},{3,2},{4,5},{5,4},{6,7},{7,6},{8,9},{9,8},{10,11... | collective-permute-start | bytes 7688 | tf_op jit(solution)/shard_map/ppermute | solution.py:364
  24.2 3.2 %copy-start.10 = (bf16[256,1280]{1,0:T(8,128)(2,1)S(1)}, bf16[256,1280]{1,0:T(8,128)(2,1)}, u32[]{:S(2)}) copy-start(bf16[256,1280]{1,0:T(8,128)(2,1)} %get-tuple-element.104) | copy-start | bytes 1966084
  24.2 5.9 %collective-permute-start.6 = (bf16[256,1280]{1,0:T(8,128)(2,1)}, bf16[256,1280]{1,0:T(8,128)(2,1)}, u32[]{:S(2)}, u32[]{:S(2)}) collective-permute-start(bf16[256,1280]{1,0:T(8,128)(2,1)} %collective-permute-done.1.k2), channel_id=1, source_target_pairs={{0,1},{1,0},{2,3},{3,2},{4,5},{5,4},{6,7},{7,6},{8,9},{9,8},{10,11... | collective-permute-start | bytes 1966088 | tf_op jit(solution)/shard_map/ppermute | solution.py:364
  24.2 18.9 %collective-permute-start.5 = (bf16[256,1280]{1,0:T(8,128)(2,1)}, bf16[256,1280]{1,0:T(8,128)(2,1)}, u32[]{:S(2)}, u32[]{:S(2)}) collective-permute-start(bf16[256,1280]{1,0:T(8,128)(2,1)} %slice.20), channel_id=1, source_target_pairs={{0,2},{2,0},{1,3},{3,1},{4,6},{6,4},{5,7},{7,5},{8,10},{10,8},{9,1... | collective-permute-start | bytes 1966088 | tf_op jit(solution)/shard_map/ppermute | solution.py:368
  27.4 2.7 %copy-start.3 = (bf16[128,2560]{1,0:T(8,128)(2,1)S(1)}, bf16[128,2560]{1,0:T(8,128)(2,1)}, u32[]{:S(2)}) copy-start(bf16[128,2560]{1,0:T(8,128)(2,1)} %upq_ref.7) | copy-start | bytes 1966084
  28.3 28.8 %collective-permute-start = (bf16[256,1408]{1,0:T(8,128)(2,1)}, bf16[256,1408]{1,0:T(8,128)(2,1)}, u32[]{:S(2)}, u32[]{:S(2)}) collective-permute-start(bf16[256,1408]{1,0:T(8,128)(2,1)} %pad_maximum_fusion.1), channel_id=1, source_target_pairs={{0,2},{2,0},{1,3},{3,1},{4,6},{6,4},{5,7},{7,5},{8,10},{10,8},{9,1... | collective-permute-start | bytes 2162696 | tf_op jit(solution)/shard_map/ppermute | solution.py:368
  30.1 1.3 copy-start.2
  31.4 1.1 copy-start.4
  32.5 1.3 copy-start.6
  33.8 9.2 %copy-start.8 = (bf16[256,2560]{1,0:T(8,128)(2,1)S(1)}, bf16[256,2560]{1,0:T(8,128)(2,1)}, u32[]{:S(2)}) copy-start(bf16[256,2560]{1,0:T(8,128)(2,1)} %v0.3) | copy-start | bytes 3932164
  43.0 2.3 %collective-permute-start.7 = (bf16[256,1280]{1,0:T(8,128)(2,1)}, bf16[256,1280]{1,0:T(8,128)(2,1)S(1)}, u32[]{:S(2)}, u32[]{:S(2)}) collective-permute-start(bf16[256,1280]{1,0:T(8,128)(2,1)} %collective-permute-done.5.k2), channel_id=1, source_target_pairs={{0,1},{1,0},{2,3},{3,2},{4,5},{5,4},{6,7},{7,6},{8,9},{9,8},{10,11... | collective-permute-start | bytes 1966088 | tf_op jit(solution)/shard_map/ppermute | solution.py:364
  43.0 16.5 %collective-permute-start.8 = (bf16[256,2560]{1,0:T(8,128)(2,1)S(1)}, bf16[256,2560]{1,0:T(8,128)(2,1)S(1)}, u32[]{:S(2)}, u32[]{:S(2)}) collective-permute-start(bf16[256,2560]{1,0:T(8,128)(2,1)S(1)} %copy-done.8), channel_id=1, source_target_pairs={{0,1},{1,0},{2,3},{3,2},{4,5},{5,4},{6,7},{7,6},{8,9},{9,8},{10,11... | collective-permute-start | bytes 3932168 | tf_op jit(solution)/shard_map/ppermute | solution.py:364
  45.3 11.7 %copy-start.12 = (bf16[256,1280]{1,0:T(8,128)(2,1)S(1)}, bf16[256,1280]{1,0:T(8,128)(2,1)}, u32[]{:S(2)}) copy-start(bf16[256,1280]{1,0:T(8,128)(2,1)} %get-tuple-element.72) | copy-start | bytes 1966084
  57.1 2.5 %collective-permute-start.10 = (bf16[256,1408]{1,0:T(8,128)(2,1)}, bf16[256,1408]{1,0:T(8,128)(2,1)S(1)}, u32[]{:S(2)}, u32[]{:S(2)}) collective-permute-start(bf16[256,1408]{1,0:T(8,128)(2,1)} %collective-permute-done.v2.l2), channel_id=1, source_target_pairs={{0,1},{1,0},{2,3},{3,2},{4,5},{5,4},{6,7},{7,6},{8,9},{9,8},{10,11... | collective-permute-start | bytes 2162696 | tf_op jit(solution)/shard_map/ppermute | solution.py:364
  57.1 17.1 %collective-permute-start.9 = (bf16[256,1280]{1,0:T(8,128)(2,1)S(1)}, bf16[256,1280]{1,0:T(8,128)(2,1)S(1)}, u32[]{:S(2)}, u32[]{:S(2)}) collective-permute-start(bf16[256,1280]{1,0:T(8,128)(2,1)S(1)} %copy-done.12), channel_id=1, source_target_pairs={{0,2},{2,0},{1,3},{3,1},{4,6},{6,4},{5,7},{7,5},{8,10},{10,8},{9,1... | collective-permute-start | bytes 1966088 | tf_op jit(solution)/shard_map/ppermute | solution.py:368
  57.4 2.2 %collective-permute-start.12 = (bf16[2,256,128]{2,1,0:T(8,128)(2,1)S(1)}, bf16[2,256,128]{2,1,0:T(8,128)(2,1)S(1)}, u32[]{:S(2)}, u32[]{:S(2)}) collective-permute-start(bf16[2,256,128]{2,1,0:T(8,128)(2,1)S(1)} %get-tuple-element.80), channel_id=1, source_target_pairs={{0,1},{1,0},{2,3},{3,2},{4,5},{5,4},{6,7},{7,6},{8,9},{9,8},{10,11... | collective-permute-start | bytes 393224 | tf_op jit(solution)/shard_map/ppermute | solution.py:364
  57.6 2.0 %collective-permute-start.11 = (bf16[256,128]{1,0:T(8,128)(2,1)S(1)}, bf16[256,128]{1,0:T(8,128)(2,1)S(1)}, u32[]{:S(2)}, u32[]{:S(2)}) collective-permute-start(bf16[256,128]{1,0:T(8,128)(2,1)S(1)} %convolution_convert_fusion.1.l0), channel_id=1, source_target_pairs={{0,1},{1,0},{2,3},{3,2},{4,5},{5,4},{6,7},{7,6},{8,9},{9,8},{10,11... | collective-permute-start | bytes 196616 | tf_op jit(solution)/shard_map/ppermute | solution.py:364
  59.5 1.1 copy-start.9
  70.8 8.2 %copy-start.5 = (bf16[128,2560]{1,0:T(8,128)(2,1)S(1)}, bf16[128,2560]{1,0:T(8,128)(2,1)}, u32[]{:S(2)}) copy-start(bf16[128,2560]{1,0:T(8,128)(2,1)} %upv_ref.7) | copy-start | bytes 1966084
  74.2 2.7 %collective-permute-start.13 = (bf16[256,1280]{1,0:T(8,128)(2,1)S(1)}, bf16[256,1280]{1,0:T(8,128)(2,1)S(1)}, u32[]{:S(2)}, u32[]{:S(2)}) collective-permute-start(bf16[256,1280]{1,0:T(8,128)(2,1)S(1)} %collective-permute-done.9.v2), channel_id=1, source_target_pairs={{0,1},{1,0},{2,3},{3,2},{4,5},{5,4},{6,7},{7,6},{8,9},{9,8},{10,11... | collective-permute-start | bytes 1966088 | tf_op jit(solution)/shard_map/ppermute | solution.py:364
  74.2 2.6 %collective-permute-start.14 = (bf16[32,40,128]{2,1,0:T(8,128)(2,1)S(1)}, bf16[32,40,128]{2,1,0:T(8,128)(2,1)S(1)}, u32[]{:S(2)}, u32[]{:S(2)}) collective-permute-start(bf16[32,40,128]{2,1,0:T(8,128)(2,1)S(1)} %get-tuple-element.84), channel_id=1, source_target_pairs={{0,1},{1,0},{2,3},{3,2},{4,5},{5,4},{6,7},{7,6},{8,9},{9,8},{10,11... | collective-permute-start | bytes 983048 | tf_op jit(solution)/shard_map/ppermute | solution.py:364
  74.7 4.3 %collective-permute-start.15 = (bf16[256,128]{1,0:T(8,128)(2,1)S(1)}, bf16[256,128]{1,0:T(8,128)(2,1)S(1)}, u32[]{:S(2)}, u32[]{:S(2)}) collective-permute-start(bf16[256,128]{1,0:T(8,128)(2,1)S(1)} %get-tuple-element.89), channel_id=1, source_target_pairs={{0,2},{2,0},{1,3},{3,1},{4,6},{6,4},{5,7},{7,5},{8,10},{10,8},{9,1... | collective-permute-start | bytes 196616 | tf_op jit(solution)/shard_map/ppermute | solution.py:368
  91.1 3.8 %collective-permute-start.16 = (bf16[64,80,128]{2,1,0:T(8,128)(2,1)}, bf16[64,80,128]{2,1,0:T(8,128)(2,1)S(1)}, u32[]{:S(2)}, u32[]{:S(2)}) collective-permute-start(bf16[64,80,128]{2,1,0:T(8,128)(2,1)} %get-tuple-element.93), channel_id=1, source_target_pairs={{0,1},{1,0},{2,3},{3,2},{4,5},{5,4},{6,7},{7,6},{8,9},{9,8},{10,11... | collective-permute-start | bytes 3932168 | tf_op jit(solution)/shard_map/ppermute | solution.py:364
  91.2 3.1 %collective-permute-start.17 = (bf16[32,40,128]{2,1,0:T(8,128)(2,1)S(1)}, bf16[32,40,128]{2,1,0:T(8,128)(2,1)S(1)}, u32[]{:S(2)}, u32[]{:S(2)}) collective-permute-start(bf16[32,40,128]{2,1,0:T(8,128)(2,1)S(1)} %get-tuple-element.96), channel_id=1, source_target_pairs={{0,1},{1,0},{2,3},{3,2},{4,5},{5,4},{6,7},{7,6},{8,9},{9,8},{10,11... | collective-permute-start | bytes 983048 | tf_op jit(solution)/shard_map/ppermute | solution.py:364
  94.4 1.3 copy-start.11

commit v4 on v3

--- a/solution.py
+++ b/solution.py
@@ -35,15 +35,27 @@
     return lax.dot_general(a, b, (((0,), (0,)), ((), ())), preferred_element_type=F32)
 
 
+def low_kernel(hidden_ref, down_query_ref, down_value_ref, query_ref, value_ref):
+    query_ref[...] = nn(hidden_ref[...], down_query_ref[...]).astype(BF16)
+    value_ref[...] = nn(hidden_ref[...], down_value_ref[...]).astype(BF16)
+
+
 def heads_of(h):
     return slice(h * HD, (h + 1) * HD)
 
 
+def of_step(a_ref, b_ref, cols):
+    return jnp.where(pl.program_id(0) == 0, a_ref[:, cols], b_ref[:, cols])
+
+
 def weight_kernel(
-    chunk0, me_ref, bias_ref, qb_ref, lowq_ref, upq_ref, cot_ref, upv_ref, k0, k1, k2, k3, *rest
+    chunk0, me_ref, bias_ref, qb_ref, lowq_ref, upq_ref, cot_ref, upv_ref, k0, k1, k2a, k2b, k3a, k3b, *rest
 ):
     step = pl.program_id(0)
-    keys = (k0, k1, k2, k3)
+    keys = (
+        lambda c: k0[:, c], lambda c: k1[:, c],
+        functools.partial(of_step, k2a, k2b), functools.partial(of_step, k3a, k3b),
+    )
     last_call = chunk0 > 0
     if last_call:
         before_ref, *rest = rest
@@ -67,7 +79,7 @@
         g_ref[:, c] = nt(cot_ref[:, c], upv_ref[:, c]).astype(BF16)
 
     def score(h, r):
-        s = nt(keys[r][:, heads_of(h)], q_ref[h % 2]) * SCALE2
+        s = nt(keys[r](heads_of(h)), q_ref[h % 2]) * SCALE2
         for b in range(2):
             j = 2 * r + b
             block = (me ^ r) * 2 + b
@@ -119,7 +131,7 @@
 
 def grad_kernel(
     first_call, downs,
-    wt_ref, inv_ref, k0, k1, k2, k3, v0, v1, v2, v3, l0, l1, l2, l3,
+    wt_ref, inv_ref, k0, k1, k2a, k2b, k3a, k3b, v0, v1, v2a, v2b, v3a, v3b, l0, l1, l2, l3,
     cot_ref, g_ref, upq_ref, upv_ref, lowqp_ref, perm_ref, *rest,
 ):
     core_ref, *rest = rest[0 if first_call else 1 :]
@@ -139,7 +151,15 @@
         held_ref, sem = rest
         fetch = pltpu.make_async_copy(hidden_ref, held_ref, sem)
         pl.when(first_step)(fetch.start)
-    keys, vals, lows = (k0, k1, k2, k3), (v0, v1, v2, v3), (l0, l1, l2, l3)
+    keys = (
+        lambda c: k0[:, c], lambda c: k1[:, c],
+        functools.partial(of_step, k2a, k2b), functools.partial(of_step, k3a, k3b),
+    )
+    vals = (
+        lambda c: v0[:, c], lambda c: v1[:, c],
+        functools.partial(of_step, v2a, v2b), functools.partial(of_step, v3a, v3b),
+    )
+    lows = (l0, l1, l2, l3)
 
     @pl.when(first_step)
     def _():
@@ -157,7 +177,7 @@
         c = heads_of(h)
         cot_g[h] = jnp.concatenate([cot_ref[:, c], g_ref[:, c]], axis=1)
         for r in range(4):
-            vl_ref[h % 2, r * ROWS : (r + 1) * ROWS, :HD] = vals[r][:, c]
+            vl_ref[h % 2, r * ROWS : (r + 1) * ROWS, :HD] = vals[r](c)
 
     def back(h, r):
         rows = slice(r * ROWS, (r + 1) * ROWS)
@@ -174,7 +194,7 @@
             wt_ref[h, rows].astype(F32) * (back_ref[h % 2, rows] - dots[h])
         ).astype(BF16)
         if r == 3:
-            key = jnp.concatenate([k[:, heads_of(h)] for k in keys], axis=0)
+            key = jnp.concatenate([k(heads_of(h)) for k in keys], axis=0)
             dqs[h] = tn(key, sh_ref[h % 2])
 
     def attend(h):
@@ -244,6 +264,10 @@
     return pl.BlockSpec((ROWS, GH * HD), lambda i: (0, i + off))
 
 
+def group():
+    return pl.BlockSpec((ROWS, GH * HD), lambda i: (0, 0))
+
+
 def colup(off):
     return pl.BlockSpec((R, GH * HD), lambda i: (0, i + off))
 
@@ -258,6 +282,20 @@
 
 def params():
     return pltpu.CompilerParams(dimension_semantics=("arbitrary",), vmem_limit_bytes=46 * 2**20)
+
+
+def low_call(hidden, down_query, down_value):
+    out = jax.ShapeDtypeStruct((ROWS, R), BF16)
+    return pl.pallas_call(
+        low_kernel,
+        grid=(1,),
+        in_specs=[const(hidden.shape), const(down_query.shape), const(down_value.shape)],
+        out_specs=[const(out.shape)] * 2,
+        out_shape=[out, out],
+        compiler_params=params(),
+        cost_estimate=pl.CostEstimate(flops=1_000_000, bytes_accessed=1_000, transcendentals=0),
+        name="low_products",
+    )(hidden, down_query, down_value)
 
 
 def weight_call(c0, n, me, before, bias, query_base, lowq, upq, cot, upv, own, sib, zs, zd):
@@ -276,7 +314,7 @@
             pl.BlockSpec(memory_space=pltpu.SMEM),
             pl.BlockSpec(memory_space=pltpu.SMEM),
             col(c0), const((ROWS, R)), colup(c0), col(c0), colup(c0),
-            col(c0), col(c0), col(0), col(0),
+            col(c0), col(c0), group(), group(), group(), group(),
             *[const(sums.shape) for _ in taken],
         ],
         out_specs=[
@@ -294,7 +332,7 @@
             flops=1_000_000, bytes_accessed=1_000, transcendentals=0
         ),
         name="attention_weights",
-    )(me.reshape(1, 1), bias, query_base, lowq, upq, cot, upv, own, sib, zs, zd, *taken)
+    )(me.reshape(1, 1), bias, query_base, lowq, upq, cot, upv, own, sib, *zs, *zd, *taken)
 
 
 def grad_call(c0, n, kc0, core, att, wt, inv, keys, vals, lows, cot, g, upq, upv, lowqp, perm, dp, low_sums, downs=None):
@@ -302,8 +340,8 @@
     args = [wt, inv, *keys, *vals, *[low for low, _ in lows], cot, g, upq, upv, lowqp, perm]
     specs = [
         per_head((4 * ROWS, ROWS), off), per_head((8, ROWS), off),
-        col(c0), col(c0), col(off), col(off),
-        col(c0), col(c0), col(0), col(0),
+        col(c0), col(c0), group(), group(), group(), group(),
+        col(c0), col(c0), group(), group(), group(), group(),
         *[pl.BlockSpec((ROWS, R), functools.partial(lambda at, i: (0, at), at)) for _, at in lows],
         col(c0), col(off), colup(c0), colup(c0), const((R, ROWS)), const((R, R)),
     ]
@@ -384,12 +422,11 @@
     def columns(a, c0, n):
         return a[:, c0 * GH * HD : (c0 + n) * GH * HD]
 
-    k_first = columns(key_base, *K_CHUNKS[0])
-    key_rest, value_rest, key_blocks, block_counts, k_first = after(
-        (key_base, value_base, key_blocks, block_counts, k_first)
-    )
-    k_zs = [over_z(k_first)]
+    k_first = tuple(columns(key_base, g, 1) for g in (0, 1))
+    key_rest, value_rest, k_first = after((key_base, value_base, k_first))
+    k_zs = [tuple(over_z(a) for a in k_first)]
     k_sib = over_core(key_rest)
+    k_sib, hidden, key_blocks, block_counts = after((k_sib, hidden, key_blocks, block_counts))
 
     listed = jnp.arange(key_blocks.shape[2])[None, None, :] < block_counts[:, :, None]
     allowed = jnp.any((key_blocks[..., None] == jnp.arange(NB)) & listed[..., None], axis=2)
@@ -397,12 +434,11 @@
     bias = jnp.stack([bias, over_far_z(bias)])
     bias = jnp.stack([bias, over_core(bias)], axis=1).reshape(HEADS, NB * NB)
 
-    low_value = nn(hidden, down_value).astype(BF16)
-    low_query = nn(hidden, down_query).astype(BF16)
+    low_query, low_value = low_call(hidden, down_query, down_value)
     key_rest, low_query = after((key_rest, low_query))
-    k_second = columns(key_rest, *K_CHUNKS[1])
-    v_first = jnp.concatenate([columns(value_rest, *V_CHUNKS[0]), low_value], axis=1)
-    v_second = columns(value_rest, *V_CHUNKS[1])
+    k_second = tuple(columns(key_rest, g, 1) for g in (2, 3))
+    v_first = (jnp.concatenate([columns(value_rest, 0, 1), low_value], axis=1), columns(value_rest, 1, 1))
+    v_second = tuple(columns(value_rest, g, 1) for g in (2, 3))
     low_query_p = low_query.T.reshape(dp, R // dp, ROWS).transpose(1, 0, 2).reshape(R, ROWS)
     turn = jnp.arange(R)
     turn = turn % dp * (R // dp) + turn // dp
@@ -410,9 +446,9 @@
     k_zs[0], low_query, low_query_p, perm, bias, k_second, v_second = after(
         (k_zs[0], low_query, low_query_p, perm, bias, k_second, v_second)
     )
-    k_zs.append(over_z(k_second))
-    k_zd = [over_core(k_zs[0])]
-    v_zs = [over_z(v_first)]
+    k_zs.append(tuple(over_z(a) for a in k_second))
+    k_zd = [tuple(over_core(a) for a in k_zs[0])]
+    v_zs = [tuple(over_z(a) for a in v_first)]
     v_sib = over_core(value_base)
     low_sib = over_core(low_value)
 
@@ -420,8 +456,8 @@
     for i, (c0, n) in enumerate(K_CHUNKS):
         if i:
             v_second, arrived, weights[-1] = after((v_second, k_zs[i], weights[-1]))
-            k_zd.append(over_core(arrived))
-            v_zs.append(over_z(v_second))
+            k_zd.append(tuple(over_core(a) for a in arrived))
+            v_zs.append(tuple(over_z(a) for a in v_second))
         wt, inv, g, *lgv = weight_call(
             c0, n, me, lgv[0], bias, query_base, low_query, up_query, cotangent, up_value,
             key_base, k_sib, k_zs[i], k_zd[i],
@@ -439,15 +475,15 @@
             arrived, att = after((v_zs[i], att))
         else:
             arrived, weights[-1] = after((v_zs[i], weights[-1]))
-        v_zd.append(over_core(arrived))
+        v_zd.append(tuple(over_core(a) for a in arrived))
         if not i:
-            lows = [(low_value, 0), (low_sib, 0), (v_zs[0], 2 * GH), (v_zd[0], 2 * GH)]
+            lows = [(low_value, 0), (low_sib, 0), (v_zs[0][0], GH), (v_zd[0][0], GH)]
         else:
             v_zd[i], up_first = after((v_zd[i], up_first))
         wt, inv, g = weights[which]
         att, *made = grad_call(
             c0, n, K_CHUNKS[which][0], core, att, wt, inv,
-            (key_base, k_sib, k_zs[which], k_zd[which]), (value_base, v_sib, v_zs[i], v_zd[i]),
+            (key_base, k_sib, *k_zs[which], *k_zd[which]), (value_base, v_sib, *v_zs[i], *v_zd[i]),
             lows, cotangent, g, up_query, up_value, low_query_p, perm, dp,
             (near, far), downs=(hidden, lgv_here, over_z(lgv_there), lgq) if i else None,
         )

time: 135 us -> 134 us (level)
  waiting for transfers between devices: 27.3 us -> 14.5 us
  starting transfers between devices: 9.45 us -> 16.5 us
  local copies, waits for them, and re-layouts: 12.8 us -> 17 us
  matrix products: 3.79 us -> 0 us
  Pallas kernels: 40.7 us -> 42.7 us
  blocking collectives: 36.8 us -> 38.8 us
    ppermute x5 -> x9, waiting for transfers between devices: 19.1 us -> 9.34 us  [over_z(): return lax.ppermute(a, 'zl', CORE_SWAP)]
    ppermute x5 -> x9, starting transfers between devices: 2.6 us -> 8.41 us  [over_z(): return lax.ppermute(a, 'zl', CORE_SWAP)]
    dot_general x2 -> x0, matrix products: 3.79 us -> none  [nn(): lax.dot_general(a, b, (((1,), (0,)), ((), ())), preferred_element_type=F32)]
    ppermute x12 -> x16, waiting for transfers between devices: 8.22 us -> 5.17 us  [over_core(): return lax.ppermute(a, 'core', CORE_SWAP)]
    unnamed x28 -> x38, local copies, waits for them, and re-layouts: 6.96 us -> 9.62 us
    all_to_all x1, blocking collectives: 36.8 us -> 38.8 us  [per_device(): landed = lax.all_to_all(payload, DP + ('zl',), 0, 0, tiled=True)]
    pallas_call x0 -> x1, Pallas kernels: none -> 1.51 us  [low_call(): pl.pallas_call(low_kernel, grid=(1,), in_specs=[const(hidden.shape), cons...]
    ppermute x12 -> x16, starting transfers between devices: 2.69 us -> 3.96 us  [over_core(): return lax.ppermute(a, 'core', CORE_SWAP)]
  transfers between devices with their start and end apart: 18 -> 26, of which waited for: 9 -> 10; matrix products, arithmetic and copies ran while one was open for 6% -> 6% of each run, Pallas kernels for 21% -> 23%
where the time goes in v4:
time: 134 us
  Pallas kernels  42.7 us (32%)
  blocking collectives  38.8 us (29%)
  local copies, waits for them, and re-layouts  17 us (13%)
  starting transfers between devices  16.5 us (12%)
  waiting for transfers between devices  14.5 us (11%)
  other arithmetic  3 us (2%)
    all_to_all x1, blocking collectives, per_device(): landed = lax.all_to_all(payload, DP + ('zl',), 0, 0, tiled=True)  38.8 us
    pallas_call x2, Pallas kernels, grad_call(): pl.pallas_call(functools.partial(grad_kernel, att is None, bool(downs)),...  22.5 us
    pallas_call x2, Pallas kernels, weight_call(): pl.pallas_call(functools.partial(weight_kernel, c0), grid=(n,), in_specs=...  18.7 us
    unnamed x38, local copies, waits for them, and re-layouts  9.62 us
    ppermute x9, waiting for transfers between devices, over_z(): return lax.ppermute(a, 'zl', CORE_SWAP)  9.34 us
    ppermute x9, starting transfers between devices, over_z(): return lax.ppermute(a, 'zl', CORE_SWAP)  8.41 us
    slice x3, local copies, waits for them, and re-layouts, columns(): return a[:, c0 * GH * HD:(c0 + n) * GH * HD]  5.46 us
    ppermute x16, waiting for transfers between devices, over_core(): return lax.ppermute(a, 'core', CORE_SWAP)  5.17 us
  transfers between devices with their start and end apart: 26, of which 10 were waited for; matrix products, arithmetic and copies ran while one was open for 6% of the time, Pallas kernels for 23%

profile of v4, /device:TPU:0, one launch (start us, length us, event | category | flops | bytes accessed | tf_op | source)
XLA Modules:
  0.0 133.5 jit_solution(4437968150387346447)
XLA Ops:
  0.6 2.1 %fusion.9 = (bf16[256,640]{1,0:T(8,128)(2,1)}, bf16[256,640]{1,0:T(8,128)(2,1)}) fusion(bf16[256,2560]{1,0:T(8,128)(2,1)} %k0.7), kind=kLoop, calls=%fused_computation.27 | loop fusion | bytes 1310720 | tf_op jit(solution)/shard_map/slice | solution.py:423
  3.2 2.0 %collective-permute-start.3 = (bf16[256,640]{1,0:T(8,128)(2,1)}, bf16[256,640]{1,0:T(8,128)(2,1)}, u32[]{:S(2)}, u32[]{:S(2)}) collective-permute-start(bf16[256,640]{1,0:T(8,128)(2,1)} %get-tuple-element.67), channel_id=1, source_target_pairs={{0,2},{2,0},{1,3},{3,1},{4,6},{6,4},{5,7},{7,5},{8,10},{10,8},{9,1... | collective-permute-start | bytes 983048 | tf_op jit(solution)/shard_map/ppermute | solution.py:406
  5.3 2.5 %fusion.7 = (bf16[256,640]{1,0:T(8,128)(2,1)}, bf16[256,640]{1,0:T(8,128)(2,1)}, bf16[256,640]{1,0:T(8,128)(2,1)}, bf16[256,640]{1,0:T(8,128)(2,1)}) fusion(bf16[256,2560]{1,0:T(8,128)(2,1)} %v0.3), kind=kLoop, calls=%fused_computation.25 | loop fusion | bytes 2621440 | tf_op jit(solution)/shard_map/slice | solution.py:423
  7.7 1.1 copy-done.12
  9.2 4.1 %collective-permute-start.5 = (f32[5,64]{1,0:T(8,128)S(1)}, f32[5,64]{1,0:T(8,128)S(1)}, u32[]{:S(2)}, u32[]{:S(2)}) collective-permute-start(f32[5,64]{1,0:T(8,128)S(1)} %select_n.42), channel_id=1, source_target_pairs={{0,18},{2,16},{16,2},{18,0},{1,19},{3,17},{17,3},{19,1},{4,22},{6,... | collective-permute-start | bytes 3848 | tf_op jit(solution)/shard_map/ppermute | solution.py:410
  13.5 1.7 %copy-done.5 = bf16[256,5120]{1,0:T(8,128)(2,1)S(1)} copy-done((bf16[256,5120]{1,0:T(8,128)(2,1)S(1)}, bf16[256,5120]{1,0:T(8,128)(2,1)}, u32[]{:S(2)}) %copy-start.5) | copy-done | bytes 2621464
  15.3 1.3 copy-done.8
  16.6 1.5 %low_products.1 = (bf16[256,128]{1,0:T(8,128)(2,1)S(1)}, bf16[256,128]{1,0:T(8,128)(2,1)S(1)}) custom-call(bf16[256,5120]{1,0:T(8,128)(2,1)S(1)} %copy-done.5, bf16[5120,128]{1,0:T(8,128)(2,1)S(1)} %copy-done.7, bf16[5120,128]{1,0:T(8,128)(2,1)S(1)} %copy-done.8), custom_call_target="tpu_custom_call" | custom-call | flops 1000000 | bytes 1000 | tf_op jit(solution)/shard_map/low_products/pallas_call | solution.py:289
  18.3 0.9 fusion.8
  19.3 0.6 reshape.78
  19.9 0.8 copy.25
  21.5 1.2 collective-permute-start.7
  22.7 0.8 collective-permute-start.8
  23.6 1.7 %pad_maximum_fusion.2 = bf16[256,768]{1,0:T(8,128)(2,1)} fusion(bf16[256,128]{1,0:T(8,128)(2,1)S(1)} %get-tuple-element.66.l0, bf16[256,640]{1,0:T(8,128)(2,1)} %get-tuple-element.132), kind=kLoop, calls=%fused_computation.6 | loop fusion | flops 786432 | bytes 786432 | tf_op jit(solution)/shard_map/concatenate | solution.py:440
  25.3 0.7 copy-done.9
  26.1 1.2 collective-permute-start.1
  27.3 1.1 copy-done.3
  28.4 1.3 copy-done.6
  29.7 1.0 copy-done.10
  30.7 9.3 %attention_weights.2 = (bf16[10,1024,256]{2,1,0:T(8,128)(2,1)}, f32[10,8,256]{2,1,0:T(8,128)S(1)}, bf16[256,1280]{1,0:T(8,128)(2,1)S(1)}, f32[4,256,128]{2,1,0:T(8,128)S(1)}) custom-call(s32[1,1]{1,0:T(1,128)} %bitcast.me_ref, f32[20,64]{1,0:T(8,128)S(1)} %reshape.80.bias_ref, bf16[256,2560]{1,0:T(8,128)(2,1)S(1)} %copy-done.6, ...), custom_call_target="tpu_custom_call" | custom-call | flops 1000000 | bytes 1000 | tf_op jit(solution)/shard_map/attention_weights/pallas_call | solution.py:310
  40.5 0.8 collective-permute-start.2
  42.3 9.4 %attention_weights.3 = (bf16[10,1024,256]{2,1,0:T(8,128)(2,1)}, f32[10,8,256]{2,1,0:T(8,128)S(1)}, bf16[256,1280]{1,0:T(8,128)(2,1)S(1)}, f32[2,256,128]{2,1,0:T(8,128)S(1)}, bf16[2,256,128]{2,1,0:T(8,128)(2,1)S(1)}) custom-call(s32[1,1]{1,0:T(1,128)} %bitcast.me_ref, f32[20,64]{1,0:T(8,128)S(1)} %reshape.80.bias_ref, bf16[256,2560]{1,0:T(8,128)(2,1)S(1)} %copy-done.6, ...), custom_call_target="tpu_custom_call" | custom-call | flops 1000000 | bytes 1000 | tf_op jit(solution)/shard_map/attention_weights/pallas_call | solution.py:310
  51.7 2.5 %collective-permute-done.2.v2b = bf16[256,640]{1,0:T(8,128)(2,1)S(1)} collective-permute-done((bf16[256,640]{1,0:T(8,128)(2,1)S(1)}, bf16[256,640]{1,0:T(8,128)(2,1)S(1)}, u32[]{:S(2)}, u32[]{:S(2)}) %collective-permute-start.2) | collective-permute-done | bytes 327712 | tf_op jit(solution)/shard_map/ppermute | solution.py:406
  55.3 0.8 collective-permute-start.14
  56.6 0.8 collective-permute-start.15
  57.4 10.5 %attention_grads.2 = (bf16[256,2560]{1,0:T(8,128)(2,1)}, f32[128,256]{1,0:T(8,128)S(1)}, bf16[32,40,128]{2,1,0:T(8,128)(2,1)S(1)}, bf16[32,40,128]{2,1,0:T(8,128...) custom-call(bf16[10,1024,256]{2,1,0:T(8,128)(2,1)} %get-tuple-element.96.wt_ref, ...), custom_call_target="tpu_custom_call" | custom-call | flops 1000000 | bytes 1000 | tf_op jit(solution)/shard_map/attention_grads/pallas_call | solution.py:383
  67.9 4.1 %collective-permute-done.15.v2b = bf16[256,640]{1,0:T(8,128)(2,1)S(1)} collective-permute-done((bf16[256,640]{1,0:T(8,128)(2,1)S(1)}, bf16[256,640]{1,0:T(8,128)(2,1)S(1)}, u32[]{:S(2)}, u32[]{:S(2)}) %collective-permute-start.15) | collective-permute-done | bytes 327712 | tf_op jit(solution)/shard_map/ppermute | solution.py:406
  72.5 0.8 collective-permute-start.23
  74.1 2.7 %collective-permute-done.23.rest_4_ = bf16[256,128]{1,0:T(8,128)(2,1)S(1)} collective-permute-done((bf16[256,128]{1,0:T(8,128)(2,1)S(1)}, bf16[256,128]{1,0:T(8,128)(2,1)S(1)}, u32[]{:S(2)}, u32[]{:S(2)}) %collective-permute-start.23) | collective-permute-done | bytes 65568 | tf_op jit(solution)/shard_map/ppermute | solution.py:406
  76.8 12.0 %attention_grads.3 = (bf16[256,2560]{1,0:T(8,128)(2,1)}, f32[128,256]{1,0:T(8,128)}, bf16[32,40,128]{2,1,0:T(8,128)(2,1)S(1)}, bf16[32,40,128]{2,1,0:T(8,128)(2,...) custom-call(bf16[10,1024,256]{2,1,0:T(8,128)(2,1)} %get-tuple-element.92., ...), custom_call_target="tpu_custom_call", output_to_operand_aliasing={{0}: (24, {})} | custom-call | flops 1000000 | bytes 1000 | tf_op jit(solution)/shard_map/attention_grads/pallas_call | solution.py:383
  89.4 2.6 %collective-permute-done.25 = bf16[32,40,128]{2,1,0:T(8,128)(2,1)S(1)} collective-permute-done((bf16[32,40,128]{2,1,0:T(8,128)(2,1)S(1)}, bf16[32,40,128]{2,1,0:T(8,128)(2,1)S(1)}, u32[]{:S(2)}, u32[]{:S(2)}) %collective-permute-start.25) | collective-permute-done | bytes 327712 | tf_op jit(solution)/shard_map/ppermute | solution.py:402
  93.1 38.8 %all_to_all.5 = bf16[64,120,128]{2,1,0:T(8,128)(2,1)S(1)} all-to-all(bf16[64,120,128]{2,1,0:T(8,128)(2,1)S(1)} %pad_maximum_fusion), channel_id=1, replica_groups=mesh['x'=4,'zh'=2,'y'=4,'zl'=2,'core'=2] {'x','zh','y','zl'}, dimensions={0} | all-to-all | bytes 3932160 | tf_op jit(solution)/shard_map/all_to_all | solution.py:498
  (93 shorter events, 9.6 us)
Async XLA Ops:
  2.7 5.0 %collective-permute-start = (bf16[256,2560]{1,0:T(8,128)(2,1)S(1)}, bf16[256,2560]{1,0:T(8,128)(2,1)S(1)}, u32[]{:S(2)}, u32[]{:S(2)}) collective-permute-start(bf16[256,2560]{1,0:T(8,128)(2,1)S(1)} %copy-done), channel_id=1, source_target_pairs={{0,1},{1,0},{2,3},{3,2},{4,5},{5,4},{6,7},{7,6},{8,9},{9,8},{10,11... | collective-permute-start | bytes 3932168 | tf_op jit(solution)/shard_map/ppermute | solution.py:402
  2.7 52.6 %collective-permute-start.13 = (bf16[256,2560]{1,0:T(8,128)(2,1)}, bf16[256,2560]{1,0:T(8,128)(2,1)}, u32[]{:S(2)}, u32[]{:S(2)}) collective-permute-start(bf16[256,2560]{1,0:T(8,128)(2,1)} %v0.3), channel_id=1, source_target_pairs={{0,1},{1,0},{2,3},{3,2},{4,5},{5,4},{6,7},{7,6},{8,9},{9,8},{10,11... | collective-permute-start | bytes 3932168 | tf_op jit(solution)/shard_map/ppermute | solution.py:402
  3.2 17.6 %collective-permute-start.3 = (bf16[256,640]{1,0:T(8,128)(2,1)}, bf16[256,640]{1,0:T(8,128)(2,1)}, u32[]{:S(2)}, u32[]{:S(2)}) collective-permute-start(bf16[256,640]{1,0:T(8,128)(2,1)} %get-tuple-element.67), channel_id=1, source_target_pairs={{0,2},{2,0},{1,3},{3,1},{4,6},{6,4},{5,7},{7,5},{8,10},{10,8},{9,1... | collective-permute-start | bytes 983048 | tf_op jit(solution)/shard_map/ppermute | solution.py:406
  5.2 15.6 %collective-permute-start.4 = (bf16[256,640]{1,0:T(8,128)(2,1)}, bf16[256,640]{1,0:T(8,128)(2,1)}, u32[]{:S(2)}, u32[]{:S(2)}) collective-permute-start(bf16[256,640]{1,0:T(8,128)(2,1)} %get-tuple-element.68), channel_id=1, source_target_pairs={{0,2},{2,0},{1,3},{3,1},{4,6},{6,4},{5,7},{7,5},{8,10},{10,8},{9,1... | collective-permute-start | bytes 983048 | tf_op jit(solution)/shard_map/ppermute | solution.py:406
  9.2 8.9 %collective-permute-start.5 = (f32[5,64]{1,0:T(8,128)S(1)}, f32[5,64]{1,0:T(8,128)S(1)}, u32[]{:S(2)}, u32[]{:S(2)}) collective-permute-start(f32[5,64]{1,0:T(8,128)S(1)} %select_n.42), channel_id=1, source_target_pairs={{0,18},{2,16},{16,2},{18,0},{1,19},{3,17},{17,3},{19,1},{4,22},{6,... | collective-permute-start | bytes 3848 | tf_op jit(solution)/shard_map/ppermute | solution.py:410
  18.1 9.1 %copy-start.1 = (bf16[256,2560]{1,0:T(8,128)(2,1)S(1)}, bf16[256,2560]{1,0:T(8,128)(2,1)}, u32[]{:S(2)}) copy-start(bf16[256,2560]{1,0:T(8,128)(2,1)} %cot_ref.7) | copy-start | bytes 3932164
  18.2 9.1 %copy-start.2 = (bf16[128,2560]{1,0:T(8,128)(2,1)S(1)}, bf16[128,2560]{1,0:T(8,128)(2,1)}, u32[]{:S(2)}) copy-start(bf16[128,2560]{1,0:T(8,128)(2,1)} %upq_ref.7) | copy-start | bytes 1966084
  18.2 2.6 %collective-permute-start.6 = (f32[2,5,64]{2,1,0:T(8,128)S(1)}, f32[2,5,64]{2,1,0:T(8,128)S(1)}, u32[]{:S(2)}, u32[]{:S(2)}) collective-permute-start(f32[2,5,64]{2,1,0:T(8,128)S(1)} %get-tuple-element.138), channel_id=1, source_target_pairs={{0,1},{1,0},{2,3},{3,2},{4,5},{5,4},{6,7},{7,6},{8,9},{9,8},{10,11... | collective-permute-start | bytes 7688 | tf_op jit(solution)/shard_map/ppermute | solution.py:402
  20.9 4.4 %collective-permute-start.9 = (bf16[256,640]{1,0:T(8,128)(2,1)}, bf16[256,640]{1,0:T(8,128)(2,1)S(1)}, u32[]{:S(2)}, u32[]{:S(2)}) collective-permute-start(bf16[256,640]{1,0:T(8,128)(2,1)} %collective-permute-done.3.k2a), channel_id=1, source_target_pairs={{0,1},{1,0},{2,3},{3,2},{4,5},{5,4},{6,7},{7,6},{8,9},{9,8},{10,11... | collective-permute-start | bytes 983048 | tf_op jit(solution)/shard_map/ppermute | solution.py:402
  21.4 5.8 %collective-permute-start.10 = (bf16[256,640]{1,0:T(8,128)(2,1)}, bf16[256,640]{1,0:T(8,128)(2,1)}, u32[]{:S(2)}, u32[]{:S(2)}) collective-permute-start(bf16[256,640]{1,0:T(8,128)(2,1)} %collective-permute-done.4.k2b), channel_id=1, source_target_pairs={{0,1},{1,0},{2,3},{3,2},{4,5},{5,4},{6,7},{7,6},{8,9},{9,8},{10,11... | collective-permute-start | bytes 983048 | tf_op jit(solution)/shard_map/ppermute | solution.py:402
  21.5 18.4 %collective-permute-start.7 = (bf16[256,640]{1,0:T(8,128)(2,1)}, bf16[256,640]{1,0:T(8,128)(2,1)}, u32[]{:S(2)}, u32[]{:S(2)}) collective-permute-start(bf16[256,640]{1,0:T(8,128)(2,1)} %get-tuple-element.77), channel_id=1, source_target_pairs={{0,2},{2,0},{1,3},{3,1},{4,6},{6,4},{5,7},{7,5},{8,10},{10,8},{9,1... | collective-permute-start | bytes 983048 | tf_op jit(solution)/shard_map/ppermute | solution.py:406
  22.7 17.2 %collective-permute-start.8 = (bf16[256,640]{1,0:T(8,128)(2,1)}, bf16[256,640]{1,0:T(8,128)(2,1)}, u32[]{:S(2)}, u32[]{:S(2)}) collective-permute-start(bf16[256,640]{1,0:T(8,128)(2,1)} %get-tuple-element.78), channel_id=1, source_target_pairs={{0,2},{2,0},{1,3},{3,1},{4,6},{6,4},{5,7},{7,5},{8,10},{10,8},{9,1... | collective-permute-start | bytes 983048 | tf_op jit(solution)/shard_map/ppermute | solution.py:406
  26.1 28.2 %collective-permute-start.1 = (bf16[256,768]{1,0:T(8,128)(2,1)}, bf16[256,768]{1,0:T(8,128)(2,1)}, u32[]{:S(2)}, u32[]{:S(2)}) collective-permute-start(bf16[256,768]{1,0:T(8,128)(2,1)} %pad_maximum_fusion.2), channel_id=1, source_target_pairs={{0,2},{2,0},{1,3},{3,1},{4,6},{6,4},{5,7},{7,5},{8,10},{10,8},{9,1... | collective-permute-start | bytes 1179656 | tf_op jit(solution)/shard_map/ppermute | solution.py:406
  30.7 9.9 %copy-start.15 = (bf16[256,640]{1,0:T(8,128)(2,1)S(1)}, bf16[256,640]{1,0:T(8,128)(2,1)}, u32[]{:S(2)}) copy-start(bf16[256,640]{1,0:T(8,128)(2,1)} %get-tuple-element.131) | copy-start | bytes 983044
  39.9 1.9 %collective-permute-start.11 = (bf16[256,640]{1,0:T(8,128)(2,1)}, bf16[256,640]{1,0:T(8,128)(2,1)S(1)}, u32[]{:S(2)}, u32[]{:S(2)}) collective-permute-start(bf16[256,640]{1,0:T(8,128)(2,1)} %collective-permute-done.7.k2a), channel_id=1, source_target_pairs={{0,1},{1,0},{2,3},{3,2},{4,5},{5,4},{6,7},{7,6},{8,9},{9,8},{10,11... | collective-permute-start | bytes 983048 | tf_op jit(solution)/shard_map/ppermute | solution.py:402
  40.0 2.3 %collective-permute-start.12 = (bf16[256,640]{1,0:T(8,128)(2,1)}, bf16[256,640]{1,0:T(8,128)(2,1)S(1)}, u32[]{:S(2)}, u32[]{:S(2)}) collective-permute-start(bf16[256,640]{1,0:T(8,128)(2,1)} %collective-permute-done.8.k2b), channel_id=1, source_target_pairs={{0,1},{1,0},{2,3},{3,2},{4,5},{5,4},{6,7},{7,6},{8,9},{9,8},{10,11... | collective-permute-start | bytes 983048 | tf_op jit(solution)/shard_map/ppermute | solution.py:402
  40.5 13.8 %collective-permute-start.2 = (bf16[256,640]{1,0:T(8,128)(2,1)S(1)}, bf16[256,640]{1,0:T(8,128)(2,1)S(1)}, u32[]{:S(2)}, u32[]{:S(2)}) collective-permute-start(bf16[256,640]{1,0:T(8,128)(2,1)S(1)} %copy-done.15), channel_id=1, source_target_pairs={{0,2},{2,0},{1,3},{3,1},{4,6},{6,4},{5,7},{7,5},{8,10},{10,8},{9,1... | collective-permute-start | bytes 983048 | tf_op jit(solution)/shard_map/ppermute | solution.py:406
  42.3 13.0 %copy-start.14 = (bf16[256,640]{1,0:T(8,128)(2,1)S(1)}, bf16[256,640]{1,0:T(8,128)(2,1)}, u32[]{:S(2)}) copy-start(bf16[256,640]{1,0:T(8,128)(2,1)} %get-tuple-element.94) | copy-start | bytes 983044
  42.3 14.2 %copy-start.13 = (bf16[256,640]{1,0:T(8,128)(2,1)S(1)}, bf16[256,640]{1,0:T(8,128)(2,1)}, u32[]{:S(2)}) copy-start(bf16[256,640]{1,0:T(8,128)(2,1)} %get-tuple-element.95) | copy-start | bytes 983044
  42.3 15.0 %copy-start.11 = (bf16[256,640]{1,0:T(8,128)(2,1)S(1)}, bf16[256,640]{1,0:T(8,128)(2,1)}, u32[]{:S(2)}) copy-start(bf16[256,640]{1,0:T(8,128)(2,1)} %copy-done.9) | copy-start | bytes 983044
  54.3 3.1 %collective-permute-start.16 = (bf16[256,768]{1,0:T(8,128)(2,1)}, bf16[256,768]{1,0:T(8,128)(2,1)S(1)}, u32[]{:S(2)}, u32[]{:S(2)}) collective-permute-start(bf16[256,768]{1,0:T(8,128)(2,1)} %collective-permute-done.1.v2a.l2), channel_id=1, source_target_pairs={{0,1},{1,0},{2,3},{3,2},{4,5},{5,4},{6,7},{7,6},{8,9},{9,8},{10,11... | collective-permute-start | bytes 1179656 | tf_op jit(solution)/shard_map/ppermute | solution.py:402
  54.3 3.1 %collective-permute-start.17 = (bf16[256,640]{1,0:T(8,128)(2,1)S(1)}, bf16[256,640]{1,0:T(8,128)(2,1)S(1)}, u32[]{:S(2)}, u32[]{:S(2)}) collective-permute-start(bf16[256,640]{1,0:T(8,128)(2,1)S(1)} %collective-permute-done.2.v2b), channel_id=1, source_target_pairs={{0,1},{1,0},{2,3},{3,2},{4,5},{5,4},{6,7},{7,6},{8,9},{9,8},{10,11... | collective-permute-start | bytes 983048 | tf_op jit(solution)/shard_map/ppermute | solution.py:402
  54.8 1.8 %collective-permute-start.18 = (bf16[256,128]{1,0:T(8,128)(2,1)S(1)}, bf16[256,128]{1,0:T(8,128)(2,1)S(1)}, u32[]{:S(2)}, u32[]{:S(2)}) collective-permute-start(bf16[256,128]{1,0:T(8,128)(2,1)S(1)} %get-tuple-element.66.l0), channel_id=1, source_target_pairs={{0,1},{1,0},{2,3},{3,2},{4,5},{5,4},{6,7},{7,6},{8,9},{9,8},{10,11... | collective-permute-start | bytes 196616 | tf_op jit(solution)/shard_map/ppermute | solution.py:402
  54.8 2.6 %collective-permute-start.19 = (bf16[2,256,128]{2,1,0:T(8,128)(2,1)S(1)}, bf16[2,256,128]{2,1,0:T(8,128)(2,1)S(1)}, u32[]{:S(2)}, u32[]{:S(2)}) collective-permute-start(bf16[2,256,128]{2,1,0:T(8,128)(2,1)S(1)} %get-tuple-element.104), channel_id=1, source_target_pairs={{0,1},{1,0},{2,3},{3,2},{4,5},{5,4},{6,7},{7,6},{8,9},{9,8},{10,11... | collective-permute-start | bytes 393224 | tf_op jit(solution)/shard_map/ppermute | solution.py:402
  55.3 12.6 %collective-permute-start.14 = (bf16[256,640]{1,0:T(8,128)(2,1)S(1)}, bf16[256,640]{1,0:T(8,128)(2,1)S(1)}, u32[]{:S(2)}, u32[]{:S(2)}) collective-permute-start(bf16[256,640]{1,0:T(8,128)(2,1)S(1)} %copy-done.14), channel_id=1, source_target_pairs={{0,2},{2,0},{1,3},{3,1},{4,6},{6,4},{5,7},{7,5},{8,10},{10,8},{9,1... | collective-permute-start | bytes 983048 | tf_op jit(solution)/shard_map/ppermute | solution.py:406
  56.6 15.5 %collective-permute-start.15 = (bf16[256,640]{1,0:T(8,128)(2,1)S(1)}, bf16[256,640]{1,0:T(8,128)(2,1)S(1)}, u32[]{:S(2)}, u32[]{:S(2)}) collective-permute-start(bf16[256,640]{1,0:T(8,128)(2,1)S(1)} %copy-done.13), channel_id=1, source_target_pairs={{0,2},{2,0},{1,3},{3,1},{4,6},{6,4},{5,7},{7,5},{8,10},{10,8},{9,1... | collective-permute-start | bytes 983048 | tf_op jit(solution)/shard_map/ppermute | solution.py:406
  67.9 5.4 %collective-permute-start.22 = (bf16[32,40,128]{2,1,0:T(8,128)(2,1)S(1)}, bf16[32,40,128]{2,1,0:T(8,128)(2,1)S(1)}, u32[]{:S(2)}, u32[]{:S(2)}) collective-permute-start(bf16[32,40,128]{2,1,0:T(8,128)(2,1)S(1)} %get-tuple-element.109), channel_id=1, source_target_pairs={{0,1},{1,0},{2,3},{3,2},{4,5},{5,4},{6,7},{7,6},{8,9},{9,8},{10,11... | collective-permute-start | bytes 983048 | tf_op jit(solution)/shard_map/ppermute | solution.py:402
  72.0 1.6 %collective-permute-start.20 = (bf16[256,640]{1,0:T(8,128)(2,1)S(1)}, bf16[256,640]{1,0:T(8,128)(2,1)S(1)}, u32[]{:S(2)}, u32[]{:S(2)}) collective-permute-start(bf16[256,640]{1,0:T(8,128)(2,1)S(1)} %collective-permute-done.14.v2a), channel_id=1, source_target_pairs={{0,1},{1,0},{2,3},{3,2},{4,5},{5,4},{6,7},{7,6},{8,9},{9,8},{10,11... | collective-permute-start | bytes 983048 | tf_op jit(solution)/shard_map/ppermute | solution.py:402
  72.0 2.1 %collective-permute-start.21 = (bf16[256,640]{1,0:T(8,128)(2,1)S(1)}, bf16[256,640]{1,0:T(8,128)(2,1)S(1)}, u32[]{:S(2)}, u32[]{:S(2)}) collective-permute-start(bf16[256,640]{1,0:T(8,128)(2,1)S(1)} %collective-permute-done.15.v2b), channel_id=1, source_target_pairs={{0,1},{1,0},{2,3},{3,2},{4,5},{5,4},{6,7},{7,6},{8,9},{9,8},{10,11... | collective-permute-start | bytes 983048 | tf_op jit(solution)/shard_map/ppermute | solution.py:402
  72.5 4.3 %collective-permute-start.23 = (bf16[256,128]{1,0:T(8,128)(2,1)S(1)}, bf16[256,128]{1,0:T(8,128)(2,1)S(1)}, u32[]{:S(2)}, u32[]{:S(2)}) collective-permute-start(bf16[256,128]{1,0:T(8,128)(2,1)S(1)} %get-tuple-element.115), channel_id=1, source_target_pairs={{0,2},{2,0},{1,3},{3,1},{4,6},{6,4},{5,7},{7,5},{8,10},{10,8},{9,1... | collective-permute-start | bytes 196616 | tf_op jit(solution)/shard_map/ppermute | solution.py:406
  88.8 3.8 %collective-permute-start.24 = (bf16[64,80,128]{2,1,0:T(8,128)(2,1)}, bf16[64,80,128]{2,1,0:T(8,128)(2,1)S(1)}, u32[]{:S(2)}, u32[]{:S(2)}) collective-permute-start(bf16[64,80,128]{2,1,0:T(8,128)(2,1)} %get-tuple-element.119), channel_id=1, source_target_pairs={{0,1},{1,0},{2,3},{3,2},{4,5},{5,4},{6,7},{7,6},{8,9},{9,8},{10,11... | collective-permute-start | bytes 3932168 | tf_op jit(solution)/shard_map/ppermute | solution.py:402
  88.9 3.1 %collective-permute-start.25 = (bf16[32,40,128]{2,1,0:T(8,128)(2,1)S(1)}, bf16[32,40,128]{2,1,0:T(8,128)(2,1)S(1)}, u32[]{:S(2)}, u32[]{:S(2)}) collective-permute-start(bf16[32,40,128]{2,1,0:T(8,128)(2,1)S(1)} %get-tuple-element.122), channel_id=1, source_target_pairs={{0,1},{1,0},{2,3},{3,2},{4,5},{5,4},{6,7},{7,6},{8,9},{9,8},{10,11... | collective-permute-start | bytes 983048 | tf_op jit(solution)/shard_map/ppermute | solution.py:402
  (12 other events, 34.9 us)

commit v5 on v4

--- a/solution.py
+++ b/solution.py
@@ -472,7 +472,7 @@
     for i, (c0, n) in enumerate(V_CHUNKS):
         which = [w for w, (a, m) in enumerate(K_CHUNKS) if a <= c0 < a + m][0]
         if i:
-            arrived, att = after((v_zs[i], att))
+            arrived, att, lgv_there = after((v_zs[i], att, over_z(lgv_there)))
         else:
             arrived, weights[-1] = after((v_zs[i], weights[-1]))
         v_zd.append(tuple(over_core(a) for a in arrived))
@@ -485,7 +485,7 @@
             c0, n, K_CHUNKS[which][0], core, att, wt, inv,
             (key_base, k_sib, *k_zs[which], *k_zd[which]), (value_base, v_sib, *v_zs[i], *v_zd[i]),
             lows, cotangent, g, up_query, up_value, low_query_p, perm, dp,
-            (near, far), downs=(hidden, lgv_here, over_z(lgv_there), lgq) if i else None,
+            (near, far), downs=(hidden, lgv_here, lgv_there, lgq) if i else None,
         )
         if not i:
             lgq, up_mine, up_other, lgv_here, lgv_there = made

time: 134 us -> 133 us (level)
  waiting for transfers between devices: 14.5 us -> 12.7 us
    ppermute x9, waiting for transfers between devices: 9.34 us -> 6.74 us  [over_z(): return lax.ppermute(a, 'zl', CORE_SWAP)]
where the time goes in v5:
time: 133 us; the launch traced here: 132 us
  Pallas kernels  42.7 us (32%)
  blocking collectives  38.9 us (29%)
  starting transfers between devices  17.1 us (13%)
  local copies, waits for them, and re-layouts  17 us (13%)
  waiting for transfers between devices  12.7 us (10%)
  other arithmetic  3 us (2%)
    all_to_all x1, blocking collectives, per_device(): landed = lax.all_to_all(payload, DP + ('zl',), 0, 0, tiled=True)  38.9 us
    pallas_call x2, Pallas kernels, grad_call(): pl.pallas_call(functools.partial(grad_kernel, att is None, bool(downs)),...  22.5 us
    pallas_call x2, Pallas kernels, weight_call(): pl.pallas_call(functools.partial(weight_kernel, c0), grid=(n,), in_specs=...  18.7 us
    unnamed x38, local copies, waits for them, and re-layouts  9.62 us
    ppermute x9, starting transfers between devices, over_z(): return lax.ppermute(a, 'zl', CORE_SWAP)  8.97 us
    ppermute x9, waiting for transfers between devices, over_z(): return lax.ppermute(a, 'zl', CORE_SWAP)  6.74 us
    ppermute x16, waiting for transfers between devices, over_core(): return lax.ppermute(a, 'core', CORE_SWAP)  5.94 us
    slice x3, local copies, waits for them, and re-layouts, columns(): return a[:, c0 * GH * HD:(c0 + n) * GH * HD]  5.46 us
  transfers between devices with their start and end apart: 26, of which 10 were waited for; matrix products, arithmetic and copies ran while one was open for 6% of the time, Pallas kernels for 23%

profile of v5, /device:TPU:0, one launch (start us, length us, event | category | flops | bytes accessed | tf_op | source)
XLA Modules:
  0.0 132.3 jit_solution(1516929320742323722)
XLA Ops:
  0.6 2.1 %fusion.9 = (bf16[256,640]{1,0:T(8,128)(2,1)}, bf16[256,640]{1,0:T(8,128)(2,1)}) fusion(bf16[256,2560]{1,0:T(8,128)(2,1)} %k0.7), kind=kLoop, calls=%fused_computation.27 | loop fusion | bytes 1310720 | tf_op jit(solution)/shard_map/slice | solution.py:423
  3.2 2.0 %collective-permute-start.3 = (bf16[256,640]{1,0:T(8,128)(2,1)}, bf16[256,640]{1,0:T(8,128)(2,1)}, u32[]{:S(2)}, u32[]{:S(2)}) collective-permute-start(bf16[256,640]{1,0:T(8,128)(2,1)} %get-tuple-element.68), channel_id=1, source_target_pairs={{0,2},{2,0},{1,3},{3,1},{4,6},{6,4},{5,7},{7,5},{8,10},{10,8},{9,1... | collective-permute-start | bytes 983048 | tf_op jit(solution)/shard_map/ppermute | solution.py:406
  5.3 2.5 %fusion.7 = (bf16[256,640]{1,0:T(8,128)(2,1)}, bf16[256,640]{1,0:T(8,128)(2,1)}, bf16[256,640]{1,0:T(8,128)(2,1)}, bf16[256,640]{1,0:T(8,128)(2,1)}) fusion(bf16[256,2560]{1,0:T(8,128)(2,1)} %v0.3), kind=kLoop, calls=%fused_computation.25 | loop fusion | bytes 2621440 | tf_op jit(solution)/shard_map/slice | solution.py:423
  7.7 1.1 copy-done.12
  9.2 4.1 %collective-permute-start.5 = (f32[5,64]{1,0:T(8,128)S(1)}, f32[5,64]{1,0:T(8,128)S(1)}, u32[]{:S(2)}, u32[]{:S(2)}) collective-permute-start(f32[5,64]{1,0:T(8,128)S(1)} %select_n.42), channel_id=1, source_target_pairs={{0,18},{2,16},{16,2},{18,0},{1,19},{3,17},{17,3},{19,1},{4,22},{6,... | collective-permute-start | bytes 3848 | tf_op jit(solution)/shard_map/ppermute | solution.py:410
  13.5 1.7 %copy-done.5 = bf16[256,5120]{1,0:T(8,128)(2,1)S(1)} copy-done((bf16[256,5120]{1,0:T(8,128)(2,1)S(1)}, bf16[256,5120]{1,0:T(8,128)(2,1)}, u32[]{:S(2)}) %copy-start.5) | copy-done | bytes 2621464
  15.3 1.3 copy-done.8
  16.6 1.5 %low_products.1 = (bf16[256,128]{1,0:T(8,128)(2,1)S(1)}, bf16[256,128]{1,0:T(8,128)(2,1)S(1)}) custom-call(bf16[256,5120]{1,0:T(8,128)(2,1)S(1)} %copy-done.5, bf16[5120,128]{1,0:T(8,128)(2,1)S(1)} %copy-done.7, bf16[5120,128]{1,0:T(8,128)(2,1)S(1)} %copy-done.8), custom_call_target="tpu_custom_call" | custom-call | flops 1000000 | bytes 1000 | tf_op jit(solution)/shard_map/low_products/pallas_call | solution.py:289
  18.3 0.9 fusion.8
  19.9 0.8 copy.25
  21.5 1.2 collective-permute-start.7
  22.7 0.8 collective-permute-start.8
  23.6 1.7 %pad_maximum_fusion.2 = bf16[256,768]{1,0:T(8,128)(2,1)} fusion(bf16[256,128]{1,0:T(8,128)(2,1)S(1)} %get-tuple-element.67.l0, bf16[256,640]{1,0:T(8,128)(2,1)} %get-tuple-element.134), kind=kLoop, calls=%fused_computation.6 | loop fusion | flops 786432 | bytes 786432 | tf_op jit(solution)/shard_map/concatenate | solution.py:440
  25.3 0.7 copy-done.9
  26.1 1.2 collective-permute-start.1
  27.3 1.1 copy-done.3
  28.4 1.3 copy-done.6
  29.7 1.0 copy-done.10
  30.7 9.3 %attention_weights.2 = (bf16[10,1024,256]{2,1,0:T(8,128)(2,1)}, f32[10,8,256]{2,1,0:T(8,128)S(1)}, bf16[256,1280]{1,0:T(8,128)(2,1)S(1)}, f32[4,256,128]{2,1,0:T(8,128)S(1)}) custom-call(s32[1,1]{1,0:T(1,128)} %bitcast.me_ref, f32[20,64]{1,0:T(8,128)S(1)} %reshape.80.bias_ref, bf16[256,2560]{1,0:T(8,128)(2,1)S(1)} %copy-done.6, ...), custom_call_target="tpu_custom_call" | custom-call | flops 1000000 | bytes 1000 | tf_op jit(solution)/shard_map/attention_weights/pallas_call | solution.py:310
  40.5 0.8 collective-permute-start.2
  42.3 9.4 %attention_weights.3 = (bf16[10,1024,256]{2,1,0:T(8,128)(2,1)}, f32[10,8,256]{2,1,0:T(8,128)S(1)}, bf16[256,1280]{1,0:T(8,128)(2,1)S(1)}, f32[2,256,128]{2,1,0:T(8,128)S(1)}, bf16[2,256,128]{2,1,0:T(8,128)(2,1)S(1)}) custom-call(s32[1,1]{1,0:T(1,128)} %bitcast.me_ref, f32[20,64]{1,0:T(8,128)S(1)} %reshape.80.bias_ref, bf16[256,2560]{1,0:T(8,128)(2,1)S(1)} %copy-done.6, ...), custom_call_target="tpu_custom_call" | custom-call | flops 1000000 | bytes 1000 | tf_op jit(solution)/shard_map/attention_weights/pallas_call | solution.py:310
  51.7 2.5 %collective-permute-done.2.v2b = bf16[256,640]{1,0:T(8,128)(2,1)S(1)} collective-permute-done((bf16[256,640]{1,0:T(8,128)(2,1)S(1)}, bf16[256,640]{1,0:T(8,128)(2,1)S(1)}, u32[]{:S(2)}, u32[]{:S(2)}) %collective-permute-start.2) | collective-permute-done | bytes 327712 | tf_op jit(solution)/shard_map/ppermute | solution.py:406
  55.3 0.8 collective-permute-start.14
  56.6 0.8 collective-permute-start.15
  57.4 10.5 %attention_grads.2 = (bf16[256,2560]{1,0:T(8,128)(2,1)}, f32[128,256]{1,0:T(8,128)S(1)}, bf16[32,40,128]{2,1,0:T(8,128)(2,1)S(1)}, bf16[32,40,128]{2,1,0:T(8,128...) custom-call(bf16[10,1024,256]{2,1,0:T(8,128)(2,1)} %get-tuple-element.97.wt_ref, ...), custom_call_target="tpu_custom_call" | custom-call | flops 1000000 | bytes 1000 | tf_op jit(solution)/shard_map/attention_grads/pallas_call | solution.py:383
  67.9 1.3 %collective-permute-start.20 = (bf16[256,128]{1,0:T(8,128)(2,1)S(1)}, bf16[256,128]{1,0:T(8,128)(2,1)S(1)}, u32[]{:S(2)}, u32[]{:S(2)}) collective-permute-start(bf16[256,128]{1,0:T(8,128)(2,1)S(1)} %get-tuple-element.107), channel_id=1, source_target_pairs={{0,2},{2,0},{1,3},{3,1},{4,6},{6,4},{5,7},{7,5},{8,10},{10,8},{9,1... | collective-permute-start | bytes 196616 | tf_op jit(solution)/shard_map/ppermute | solution.py:406
  69.2 3.5 %collective-permute-done.15.v2b = bf16[256,640]{1,0:T(8,128)(2,1)S(1)} collective-permute-done((bf16[256,640]{1,0:T(8,128)(2,1)S(1)}, bf16[256,640]{1,0:T(8,128)(2,1)S(1)}, u32[]{:S(2)}, u32[]{:S(2)}) %collective-permute-start.15) | collective-permute-done | bytes 327712 | tf_op jit(solution)/shard_map/ppermute | solution.py:406
  72.7 0.7 collective-permute-done.20.rest_4_
  74.0 1.0 collective-permute-done.21.v3a
  75.5 12.0 %attention_grads.3 = (bf16[256,2560]{1,0:T(8,128)(2,1)}, f32[128,256]{1,0:T(8,128)}, bf16[32,40,128]{2,1,0:T(8,128)(2,1)S(1)}, bf16[32,40,128]{2,1,0:T(8,128)(2,...) custom-call(bf16[10,1024,256]{2,1,0:T(8,128)(2,1)} %get-tuple-element.93., ...), custom_call_target="tpu_custom_call", output_to_operand_aliasing={{0}: (24, {})} | custom-call | flops 1000000 | bytes 1000 | tf_op jit(solution)/shard_map/attention_grads/pallas_call | solution.py:383
  88.1 2.9 %collective-permute-done.25 = bf16[32,40,128]{2,1,0:T(8,128)(2,1)S(1)} collective-permute-done((bf16[32,40,128]{2,1,0:T(8,128)(2,1)S(1)}, bf16[32,40,128]{2,1,0:T(8,128)(2,1)S(1)}, u32[]{:S(2)}, u32[]{:S(2)}) %collective-permute-start.25) | collective-permute-done | bytes 327712 | tf_op jit(solution)/shard_map/ppermute | solution.py:402
  91.8 38.9 %all_to_all.5 = bf16[64,120,128]{2,1,0:T(8,128)(2,1)S(1)} all-to-all(bf16[64,120,128]{2,1,0:T(8,128)(2,1)S(1)} %pad_maximum_fusion), channel_id=1, replica_groups=mesh['x'=4,'zh'=2,'y'=4,'zl'=2,'core'=2] {'x','zh','y','zl'}, dimensions={0} | all-to-all | bytes 3932160 | tf_op jit(solution)/shard_map/all_to_all | solution.py:498
  (93 shorter events, 9.7 us)
Async XLA Ops:
  2.7 5.0 %collective-permute-start = (bf16[256,2560]{1,0:T(8,128)(2,1)S(1)}, bf16[256,2560]{1,0:T(8,128)(2,1)S(1)}, u32[]{:S(2)}, u32[]{:S(2)}) collective-permute-start(bf16[256,2560]{1,0:T(8,128)(2,1)S(1)} %copy-done), channel_id=1, source_target_pairs={{0,1},{1,0},{2,3},{3,2},{4,5},{5,4},{6,7},{7,6},{8,9},{9,8},{10,11... | collective-permute-start | bytes 3932168 | tf_op jit(solution)/shard_map/ppermute | solution.py:402
  2.7 52.6 %collective-permute-start.13 = (bf16[256,2560]{1,0:T(8,128)(2,1)}, bf16[256,2560]{1,0:T(8,128)(2,1)}, u32[]{:S(2)}, u32[]{:S(2)}) collective-permute-start(bf16[256,2560]{1,0:T(8,128)(2,1)} %v0.3), channel_id=1, source_target_pairs={{0,1},{1,0},{2,3},{3,2},{4,5},{5,4},{6,7},{7,6},{8,9},{9,8},{10,11... | collective-permute-start | bytes 3932168 | tf_op jit(solution)/shard_map/ppermute | solution.py:402
  3.2 17.6 %collective-permute-start.3 = (bf16[256,640]{1,0:T(8,128)(2,1)}, bf16[256,640]{1,0:T(8,128)(2,1)}, u32[]{:S(2)}, u32[]{:S(2)}) collective-permute-start(bf16[256,640]{1,0:T(8,128)(2,1)} %get-tuple-element.68), channel_id=1, source_target_pairs={{0,2},{2,0},{1,3},{3,1},{4,6},{6,4},{5,7},{7,5},{8,10},{10,8},{9,1... | collective-permute-start | bytes 983048 | tf_op jit(solution)/shard_map/ppermute | solution.py:406
  5.2 15.6 %collective-permute-start.4 = (bf16[256,640]{1,0:T(8,128)(2,1)}, bf16[256,640]{1,0:T(8,128)(2,1)}, u32[]{:S(2)}, u32[]{:S(2)}) collective-permute-start(bf16[256,640]{1,0:T(8,128)(2,1)} %get-tuple-element.69), channel_id=1, source_target_pairs={{0,2},{2,0},{1,3},{3,1},{4,6},{6,4},{5,7},{7,5},{8,10},{10,8},{9,1... | collective-permute-start | bytes 983048 | tf_op jit(solution)/shard_map/ppermute | solution.py:406
  9.2 8.9 %collective-permute-start.5 = (f32[5,64]{1,0:T(8,128)S(1)}, f32[5,64]{1,0:T(8,128)S(1)}, u32[]{:S(2)}, u32[]{:S(2)}) collective-permute-start(f32[5,64]{1,0:T(8,128)S(1)} %select_n.42), channel_id=1, source_target_pairs={{0,18},{2,16},{16,2},{18,0},{1,19},{3,17},{17,3},{19,1},{4,22},{6,... | collective-permute-start | bytes 3848 | tf_op jit(solution)/shard_map/ppermute | solution.py:410
  18.1 9.1 %copy-start.1 = (bf16[256,2560]{1,0:T(8,128)(2,1)S(1)}, bf16[256,2560]{1,0:T(8,128)(2,1)}, u32[]{:S(2)}) copy-start(bf16[256,2560]{1,0:T(8,128)(2,1)} %cot_ref.7) | copy-start | bytes 3932164
  18.2 9.1 %copy-start.2 = (bf16[128,2560]{1,0:T(8,128)(2,1)S(1)}, bf16[128,2560]{1,0:T(8,128)(2,1)}, u32[]{:S(2)}) copy-start(bf16[128,2560]{1,0:T(8,128)(2,1)} %upq_ref.7) | copy-start | bytes 1966084
  18.2 2.6 %collective-permute-start.6 = (f32[2,5,64]{2,1,0:T(8,128)S(1)}, f32[2,5,64]{2,1,0:T(8,128)S(1)}, u32[]{:S(2)}, u32[]{:S(2)}) collective-permute-start(f32[2,5,64]{2,1,0:T(8,128)S(1)} %get-tuple-element.140), channel_id=1, source_target_pairs={{0,1},{1,0},{2,3},{3,2},{4,5},{5,4},{6,7},{7,6},{8,9},{9,8},{10,11... | collective-permute-start | bytes 7688 | tf_op jit(solution)/shard_map/ppermute | solution.py:402
  20.9 4.4 %collective-permute-start.9 = (bf16[256,640]{1,0:T(8,128)(2,1)}, bf16[256,640]{1,0:T(8,128)(2,1)S(1)}, u32[]{:S(2)}, u32[]{:S(2)}) collective-permute-start(bf16[256,640]{1,0:T(8,128)(2,1)} %collective-permute-done.3.k2a), channel_id=1, source_target_pairs={{0,1},{1,0},{2,3},{3,2},{4,5},{5,4},{6,7},{7,6},{8,9},{9,8},{10,11... | collective-permute-start | bytes 983048 | tf_op jit(solution)/shard_map/ppermute | solution.py:402
  21.4 5.8 %collective-permute-start.10 = (bf16[256,640]{1,0:T(8,128)(2,1)}, bf16[256,640]{1,0:T(8,128)(2,1)}, u32[]{:S(2)}, u32[]{:S(2)}) collective-permute-start(bf16[256,640]{1,0:T(8,128)(2,1)} %collective-permute-done.4.k2b), channel_id=1, source_target_pairs={{0,1},{1,0},{2,3},{3,2},{4,5},{5,4},{6,7},{7,6},{8,9},{9,8},{10,11... | collective-permute-start | bytes 983048 | tf_op jit(solution)/shard_map/ppermute | solution.py:402
  21.5 18.4 %collective-permute-start.7 = (bf16[256,640]{1,0:T(8,128)(2,1)}, bf16[256,640]{1,0:T(8,128)(2,1)}, u32[]{:S(2)}, u32[]{:S(2)}) collective-permute-start(bf16[256,640]{1,0:T(8,128)(2,1)} %get-tuple-element.78), channel_id=1, source_target_pairs={{0,2},{2,0},{1,3},{3,1},{4,6},{6,4},{5,7},{7,5},{8,10},{10,8},{9,1... | collective-permute-start | bytes 983048 | tf_op jit(solution)/shard_map/ppermute | solution.py:406
  22.7 17.2 %collective-permute-start.8 = (bf16[256,640]{1,0:T(8,128)(2,1)}, bf16[256,640]{1,0:T(8,128)(2,1)}, u32[]{:S(2)}, u32[]{:S(2)}) collective-permute-start(bf16[256,640]{1,0:T(8,128)(2,1)} %get-tuple-element.79), channel_id=1, source_target_pairs={{0,2},{2,0},{1,3},{3,1},{4,6},{6,4},{5,7},{7,5},{8,10},{10,8},{9,1... | collective-permute-start | bytes 983048 | tf_op jit(solution)/shard_map/ppermute | solution.py:406
  26.1 28.2 %collective-permute-start.1 = (bf16[256,768]{1,0:T(8,128)(2,1)}, bf16[256,768]{1,0:T(8,128)(2,1)}, u32[]{:S(2)}, u32[]{:S(2)}) collective-permute-start(bf16[256,768]{1,0:T(8,128)(2,1)} %pad_maximum_fusion.2), channel_id=1, source_target_pairs={{0,2},{2,0},{1,3},{3,1},{4,6},{6,4},{5,7},{7,5},{8,10},{10,8},{9,1... | collective-permute-start | bytes 1179656 | tf_op jit(solution)/shard_map/ppermute | solution.py:406
  30.7 9.9 %copy-start.15 = (bf16[256,640]{1,0:T(8,128)(2,1)S(1)}, bf16[256,640]{1,0:T(8,128)(2,1)}, u32[]{:S(2)}) copy-start(bf16[256,640]{1,0:T(8,128)(2,1)} %get-tuple-element.133) | copy-start | bytes 983044
  39.9 1.9 %collective-permute-start.11 = (bf16[256,640]{1,0:T(8,128)(2,1)}, bf16[256,640]{1,0:T(8,128)(2,1)S(1)}, u32[]{:S(2)}, u32[]{:S(2)}) collective-permute-start(bf16[256,640]{1,0:T(8,128)(2,1)} %collective-permute-done.7.k2a), channel_id=1, source_target_pairs={{0,1},{1,0},{2,3},{3,2},{4,5},{5,4},{6,7},{7,6},{8,9},{9,8},{10,11... | collective-permute-start | bytes 983048 | tf_op jit(solution)/shard_map/ppermute | solution.py:402
  40.0 2.3 %collective-permute-start.12 = (bf16[256,640]{1,0:T(8,128)(2,1)}, bf16[256,640]{1,0:T(8,128)(2,1)S(1)}, u32[]{:S(2)}, u32[]{:S(2)}) collective-permute-start(bf16[256,640]{1,0:T(8,128)(2,1)} %collective-permute-done.8.k2b), channel_id=1, source_target_pairs={{0,1},{1,0},{2,3},{3,2},{4,5},{5,4},{6,7},{7,6},{8,9},{9,8},{10,11... | collective-permute-start | bytes 983048 | tf_op jit(solution)/shard_map/ppermute | solution.py:402
  40.5 13.8 %collective-permute-start.2 = (bf16[256,640]{1,0:T(8,128)(2,1)S(1)}, bf16[256,640]{1,0:T(8,128)(2,1)S(1)}, u32[]{:S(2)}, u32[]{:S(2)}) collective-permute-start(bf16[256,640]{1,0:T(8,128)(2,1)S(1)} %copy-done.15), channel_id=1, source_target_pairs={{0,2},{2,0},{1,3},{3,1},{4,6},{6,4},{5,7},{7,5},{8,10},{10,8},{9,1... | collective-permute-start | bytes 983048 | tf_op jit(solution)/shard_map/ppermute | solution.py:406
  42.3 13.0 %copy-start.14 = (bf16[256,640]{1,0:T(8,128)(2,1)S(1)}, bf16[256,640]{1,0:T(8,128)(2,1)}, u32[]{:S(2)}) copy-start(bf16[256,640]{1,0:T(8,128)(2,1)} %get-tuple-element.95) | copy-start | bytes 983044
  42.3 14.2 %copy-start.13 = (bf16[256,640]{1,0:T(8,128)(2,1)S(1)}, bf16[256,640]{1,0:T(8,128)(2,1)}, u32[]{:S(2)}) copy-start(bf16[256,640]{1,0:T(8,128)(2,1)} %get-tuple-element.96) | copy-start | bytes 983044
  42.3 15.0 %copy-start.11 = (bf16[256,640]{1,0:T(8,128)(2,1)S(1)}, bf16[256,640]{1,0:T(8,128)(2,1)}, u32[]{:S(2)}) copy-start(bf16[256,640]{1,0:T(8,128)(2,1)} %copy-done.9) | copy-start | bytes 983044
  54.3 3.1 %collective-permute-start.16 = (bf16[256,768]{1,0:T(8,128)(2,1)}, bf16[256,768]{1,0:T(8,128)(2,1)S(1)}, u32[]{:S(2)}, u32[]{:S(2)}) collective-permute-start(bf16[256,768]{1,0:T(8,128)(2,1)} %collective-permute-done.1.v2a.l2), channel_id=1, source_target_pairs={{0,1},{1,0},{2,3},{3,2},{4,5},{5,4},{6,7},{7,6},{8,9},{9,8},{10,11... | collective-permute-start | bytes 1179656 | tf_op jit(solution)/shard_map/ppermute | solution.py:402
  54.3 3.1 %collective-permute-start.17 = (bf16[256,640]{1,0:T(8,128)(2,1)S(1)}, bf16[256,640]{1,0:T(8,128)(2,1)S(1)}, u32[]{:S(2)}, u32[]{:S(2)}) collective-permute-start(bf16[256,640]{1,0:T(8,128)(2,1)S(1)} %collective-permute-done.2.v2b), channel_id=1, source_target_pairs={{0,1},{1,0},{2,3},{3,2},{4,5},{5,4},{6,7},{7,6},{8,9},{9,8},{10,11... | collective-permute-start | bytes 983048 | tf_op jit(solution)/shard_map/ppermute | solution.py:402
  54.8 1.8 %collective-permute-start.18 = (bf16[256,128]{1,0:T(8,128)(2,1)S(1)}, bf16[256,128]{1,0:T(8,128)(2,1)S(1)}, u32[]{:S(2)}, u32[]{:S(2)}) collective-permute-start(bf16[256,128]{1,0:T(8,128)(2,1)S(1)} %get-tuple-element.67.l0), channel_id=1, source_target_pairs={{0,1},{1,0},{2,3},{3,2},{4,5},{5,4},{6,7},{7,6},{8,9},{9,8},{10,11... | collective-permute-start | bytes 196616 | tf_op jit(solution)/shard_map/ppermute | solution.py:402
  54.8 2.6 %collective-permute-start.19 = (bf16[2,256,128]{2,1,0:T(8,128)(2,1)S(1)}, bf16[2,256,128]{2,1,0:T(8,128)(2,1)S(1)}, u32[]{:S(2)}, u32[]{:S(2)}) collective-permute-start(bf16[2,256,128]{2,1,0:T(8,128)(2,1)S(1)} %get-tuple-element.105), channel_id=1, source_target_pairs={{0,1},{1,0},{2,3},{3,2},{4,5},{5,4},{6,7},{7,6},{8,9},{9,8},{10,11... | collective-permute-start | bytes 393224 | tf_op jit(solution)/shard_map/ppermute | solution.py:402
  55.3 13.9 %collective-permute-start.14 = (bf16[256,640]{1,0:T(8,128)(2,1)S(1)}, bf16[256,640]{1,0:T(8,128)(2,1)S(1)}, u32[]{:S(2)}, u32[]{:S(2)}) collective-permute-start(bf16[256,640]{1,0:T(8,128)(2,1)S(1)} %copy-done.14), channel_id=1, source_target_pairs={{0,2},{2,0},{1,3},{3,1},{4,6},{6,4},{5,7},{7,5},{8,10},{10,8},{9,1... | collective-permute-start | bytes 983048 | tf_op jit(solution)/shard_map/ppermute | solution.py:406
  56.6 16.2 %collective-permute-start.15 = (bf16[256,640]{1,0:T(8,128)(2,1)S(1)}, bf16[256,640]{1,0:T(8,128)(2,1)S(1)}, u32[]{:S(2)}, u32[]{:S(2)}) collective-permute-start(bf16[256,640]{1,0:T(8,128)(2,1)S(1)} %copy-done.13), channel_id=1, source_target_pairs={{0,2},{2,0},{1,3},{3,1},{4,6},{6,4},{5,7},{7,5},{8,10},{10,8},{9,1... | collective-permute-start | bytes 983048 | tf_op jit(solution)/shard_map/ppermute | solution.py:406
  67.9 6.0 %collective-permute-start.23 = (bf16[32,40,128]{2,1,0:T(8,128)(2,1)S(1)}, bf16[32,40,128]{2,1,0:T(8,128)(2,1)S(1)}, u32[]{:S(2)}, u32[]{:S(2)}) collective-permute-start(bf16[32,40,128]{2,1,0:T(8,128)(2,1)S(1)} %get-tuple-element.111), channel_id=1, source_target_pairs={{0,1},{1,0},{2,3},{3,2},{4,5},{5,4},{6,7},{7,6},{8,9},{9,8},{10,11... | collective-permute-start | bytes 983048 | tf_op jit(solution)/shard_map/ppermute | solution.py:402
  67.9 5.5 %collective-permute-start.20 = (bf16[256,128]{1,0:T(8,128)(2,1)S(1)}, bf16[256,128]{1,0:T(8,128)(2,1)S(1)}, u32[]{:S(2)}, u32[]{:S(2)}) collective-permute-start(bf16[256,128]{1,0:T(8,128)(2,1)S(1)} %get-tuple-element.107), channel_id=1, source_target_pairs={{0,2},{2,0},{1,3},{3,1},{4,6},{6,4},{5,7},{7,5},{8,10},{10,8},{9,1... | collective-permute-start | bytes 196616 | tf_op jit(solution)/shard_map/ppermute | solution.py:406
  73.4 1.6 %collective-permute-start.21 = (bf16[256,640]{1,0:T(8,128)(2,1)S(1)}, bf16[256,640]{1,0:T(8,128)(2,1)S(1)}, u32[]{:S(2)}, u32[]{:S(2)}) collective-permute-start(bf16[256,640]{1,0:T(8,128)(2,1)S(1)} %collective-permute-done.14.v2a), channel_id=1, source_target_pairs={{0,1},{1,0},{2,3},{3,2},{4,5},{5,4},{6,7},{7,6},{8,9},{9,8},{10,11... | collective-permute-start | bytes 983048 | tf_op jit(solution)/shard_map/ppermute | solution.py:402
  73.4 2.1 %collective-permute-start.22 = (bf16[256,640]{1,0:T(8,128)(2,1)S(1)}, bf16[256,640]{1,0:T(8,128)(2,1)S(1)}, u32[]{:S(2)}, u32[]{:S(2)}) collective-permute-start(bf16[256,640]{1,0:T(8,128)(2,1)S(1)} %collective-permute-done.15.v2b), channel_id=1, source_target_pairs={{0,1},{1,0},{2,3},{3,2},{4,5},{5,4},{6,7},{7,6},{8,9},{9,8},{10,11... | collective-permute-start | bytes 983048 | tf_op jit(solution)/shard_map/ppermute | solution.py:402
  87.5 3.8 %collective-permute-start.24 = (bf16[64,80,128]{2,1,0:T(8,128)(2,1)}, bf16[64,80,128]{2,1,0:T(8,128)(2,1)S(1)}, u32[]{:S(2)}, u32[]{:S(2)}) collective-permute-start(bf16[64,80,128]{2,1,0:T(8,128)(2,1)} %get-tuple-element.121), channel_id=1, source_target_pairs={{0,1},{1,0},{2,3},{3,2},{4,5},{5,4},{6,7},{7,6},{8,9},{9,8},{10,11... | collective-permute-start | bytes 3932168 | tf_op jit(solution)/shard_map/ppermute | solution.py:402
  87.7 3.3 %collective-permute-start.25 = (bf16[32,40,128]{2,1,0:T(8,128)(2,1)S(1)}, bf16[32,40,128]{2,1,0:T(8,128)(2,1)S(1)}, u32[]{:S(2)}, u32[]{:S(2)}) collective-permute-start(bf16[32,40,128]{2,1,0:T(8,128)(2,1)S(1)} %get-tuple-element.124), channel_id=1, source_target_pairs={{0,1},{1,0},{2,3},{3,2},{4,5},{5,4},{6,7},{7,6},{8,9},{9,8},{10,11... | collective-permute-start | bytes 983048 | tf_op jit(solution)/shard_map/ppermute | solution.py:402
  (12 other events, 33.6 us)

commit v6 on v5

--- a/solution.py
+++ b/solution.py
@@ -443,14 +443,14 @@
     turn = jnp.arange(R)
     turn = turn % dp * (R // dp) + turn // dp
     perm = (turn[:, None] == jnp.arange(R)[None, :]).astype(BF16)
-    k_zs[0], low_query, low_query_p, perm, bias, k_second, v_second = after(
-        (k_zs[0], low_query, low_query_p, perm, bias, k_second, v_second)
+    low_sib = over_core(low_value)
+    k_zs[0], low_query, low_query_p, perm, bias, k_second, v_second, low_sib = after(
+        (k_zs[0], low_query, low_query_p, perm, bias, k_second, v_second, low_sib)
     )
     k_zs.append(tuple(over_z(a) for a in k_second))
     k_zd = [tuple(over_core(a) for a in k_zs[0])]
     v_zs = [tuple(over_z(a) for a in v_first)]
     v_sib = over_core(value_base)
-    low_sib = over_core(low_value)
 
     weights, lgv = [], [None]
     for i, (c0, n) in enumerate(K_CHUNKS):

time: 133 us -> 133 us (level)
  transfers between devices with their start and end apart: 26 -> 26, of which waited for: 10 -> 8; matrix products, arithmetic and copies ran while one was open for 6% -> 6% of each run, Pallas kernels for 23% -> 23%
where the time goes in v6:
time: 133 us; the launch traced here: 132 us
  Pallas kernels  42.7 us (32%)
  blocking collectives  38.7 us (29%)
  local copies, waits for them, and re-layouts  17 us (13%)
  starting transfers between devices  17 us (13%)
  waiting for transfers between devices  12.8 us (10%)
  other arithmetic  3.04 us (2%)
    all_to_all x1, blocking collectives, per_device(): landed = lax.all_to_all(payload, DP + ('zl',), 0, 0, tiled=True)  38.7 us
    pallas_call x2, Pallas kernels, grad_call(): pl.pallas_call(functools.partial(grad_kernel, att is None, bool(downs)),...  22.5 us
    pallas_call x2, Pallas kernels, weight_call(): pl.pallas_call(functools.partial(weight_kernel, c0), grid=(n,), in_specs=...  18.7 us
    unnamed x38, local copies, waits for them, and re-layouts  9.62 us
    ppermute x9, starting transfers between devices, over_z(): return lax.ppermute(a, 'zl', CORE_SWAP)  8.81 us
    ppermute x9, waiting for transfers between devices, over_z(): return lax.ppermute(a, 'zl', CORE_SWAP)  7.86 us
    slice x3, local copies, waits for them, and re-layouts, columns(): return a[:, c0 * GH * HD:(c0 + n) * GH * HD]  5.46 us
    ppermute x16, waiting for transfers between devices, over_core(): return lax.ppermute(a, 'core', CORE_SWAP)  4.95 us
  transfers between devices with their start and end apart: 26, of which 8 were waited for; matrix products, arithmetic and copies ran while one was open for 6% of the time, Pallas kernels for 23%

profile of v6, /device:TPU:0, one launch (start us, length us, event | category | flops | bytes accessed | tf_op | source)
XLA Modules:
  0.0 132.2 jit_solution(15272444837830399878)
XLA Ops:
  0.6 2.1 %fusion.9 = (bf16[256,640]{1,0:T(8,128)(2,1)}, bf16[256,640]{1,0:T(8,128)(2,1)}) fusion(bf16[256,2560]{1,0:T(8,128)(2,1)} %k0.7), kind=kLoop, calls=%fused_computation.27 | loop fusion | bytes 1310720 | tf_op jit(solution)/shard_map/slice | solution.py:423
  3.2 2.0 %collective-permute-start.3 = (bf16[256,640]{1,0:T(8,128)(2,1)}, bf16[256,640]{1,0:T(8,128)(2,1)}, u32[]{:S(2)}, u32[]{:S(2)}) collective-permute-start(bf16[256,640]{1,0:T(8,128)(2,1)} %get-tuple-element.69), channel_id=1, source_target_pairs={{0,2},{2,0},{1,3},{3,1},{4,6},{6,4},{5,7},{7,5},{8,10},{10,8},{9,1... | collective-permute-start | bytes 983048 | tf_op jit(solution)/shard_map/ppermute | solution.py:406
  5.3 2.5 %fusion.7 = (bf16[256,640]{1,0:T(8,128)(2,1)}, bf16[256,640]{1,0:T(8,128)(2,1)}, bf16[256,640]{1,0:T(8,128)(2,1)}, bf16[256,640]{1,0:T(8,128)(2,1)}) fusion(bf16[256,2560]{1,0:T(8,128)(2,1)} %v0.3), kind=kLoop, calls=%fused_computation.25 | loop fusion | bytes 2621440 | tf_op jit(solution)/shard_map/slice | solution.py:423
  7.7 1.1 copy-done.12
  9.2 4.1 %collective-permute-start.5 = (f32[5,64]{1,0:T(8,128)S(1)}, f32[5,64]{1,0:T(8,128)S(1)}, u32[]{:S(2)}, u32[]{:S(2)}) collective-permute-start(f32[5,64]{1,0:T(8,128)S(1)} %select_n.42), channel_id=1, source_target_pairs={{0,18},{2,16},{16,2},{18,0},{1,19},{3,17},{17,3},{19,1},{4,22},{6,... | collective-permute-start | bytes 3848 | tf_op jit(solution)/shard_map/ppermute | solution.py:410
  13.5 1.7 %copy-done.5 = bf16[256,5120]{1,0:T(8,128)(2,1)S(1)} copy-done((bf16[256,5120]{1,0:T(8,128)(2,1)S(1)}, bf16[256,5120]{1,0:T(8,128)(2,1)}, u32[]{:S(2)}) %copy-start.5) | copy-done | bytes 2621464
  15.3 1.3 copy-done.8
  16.6 1.5 %low_products.1 = (bf16[256,128]{1,0:T(8,128)(2,1)S(1)}, bf16[256,128]{1,0:T(8,128)(2,1)S(1)}) custom-call(bf16[256,5120]{1,0:T(8,128)(2,1)S(1)} %copy-done.5, bf16[5120,128]{1,0:T(8,128)(2,1)S(1)} %copy-done.7, bf16[5120,128]{1,0:T(8,128)(2,1)S(1)} %copy-done.8), custom_call_target="tpu_custom_call" | custom-call | flops 1000000 | bytes 1000 | tf_op jit(solution)/shard_map/low_products/pallas_call | solution.py:289
  18.8 0.9 fusion.8
  19.9 0.6 reshape.78
  20.5 0.8 copy.25
  22.0 0.7 collective-permute-start.8
  22.7 1.3 collective-permute-start.9
  24.1 1.7 %pad_maximum_fusion.2 = bf16[256,768]{1,0:T(8,128)(2,1)} fusion(bf16[256,128]{1,0:T(8,128)(2,1)S(1)} %get-tuple-element.68.l0, bf16[256,640]{1,0:T(8,128)(2,1)} %get-tuple-element.136), kind=kLoop, calls=%fused_computation.6 | loop fusion | flops 786432 | bytes 786432 | tf_op jit(solution)/shard_map/concatenate | solution.py:440
  25.8 0.7 copy-done.9
  26.6 0.7 collective-permute-start.1
  27.3 1.1 copy-done.3
  28.4 1.3 copy-done.6
  29.7 1.0 copy-done.10
  30.7 9.3 %attention_weights.2 = (bf16[10,1024,256]{2,1,0:T(8,128)(2,1)}, f32[10,8,256]{2,1,0:T(8,128)S(1)}, bf16[256,1280]{1,0:T(8,128)(2,1)S(1)}, f32[4,256,128]{2,1,0:T(8,128)S(1)}) custom-call(s32[1,1]{1,0:T(1,128)} %bitcast.me_ref, f32[20,64]{1,0:T(8,128)S(1)} %reshape.80.bias_ref, bf16[256,2560]{1,0:T(8,128)(2,1)S(1)} %copy-done.6, ...), custom_call_target="tpu_custom_call" | custom-call | flops 1000000 | bytes 1000 | tf_op jit(solution)/shard_map/attention_weights/pallas_call | solution.py:310
  40.5 1.3 collective-permute-start.2
  42.3 9.4 %attention_weights.3 = (bf16[10,1024,256]{2,1,0:T(8,128)(2,1)}, f32[10,8,256]{2,1,0:T(8,128)S(1)}, bf16[256,1280]{1,0:T(8,128)(2,1)S(1)}, f32[2,256,128]{2,1,0:T(8,128)S(1)}, bf16[2,256,128]{2,1,0:T(8,128)(2,1)S(1)}) custom-call(s32[1,1]{1,0:T(1,128)} %bitcast.me_ref, f32[20,64]{1,0:T(8,128)S(1)} %reshape.80.bias_ref, bf16[256,2560]{1,0:T(8,128)(2,1)S(1)} %copy-done.6, ...), custom_call_target="tpu_custom_call" | custom-call | flops 1000000 | bytes 1000 | tf_op jit(solution)/shard_map/attention_weights/pallas_call | solution.py:310
  51.7 2.7 %collective-permute-done.2.v2b = bf16[256,640]{1,0:T(8,128)(2,1)S(1)} collective-permute-done((bf16[256,640]{1,0:T(8,128)(2,1)S(1)}, bf16[256,640]{1,0:T(8,128)(2,1)S(1)}, u32[]{:S(2)}, u32[]{:S(2)}) %collective-permute-start.2) | collective-permute-done | bytes 327712 | tf_op jit(solution)/shard_map/ppermute | solution.py:406
  55.6 1.4 %collective-permute-start.16 = (bf16[256,640]{1,0:T(8,128)(2,1)S(1)}, bf16[256,640]{1,0:T(8,128)(2,1)S(1)}, u32[]{:S(2)}, u32[]{:S(2)}) collective-permute-start(bf16[256,640]{1,0:T(8,128)(2,1)S(1)} %copy-done.13), channel_id=1, source_target_pairs={{0,2},{2,0},{1,3},{3,1},{4,6},{6,4},{5,7},{7,5},{8,10},{10,8},{9,1... | collective-permute-start | bytes 983048 | tf_op jit(solution)/shard_map/ppermute | solution.py:406
  57.0 10.6 %attention_grads.2 = (bf16[256,2560]{1,0:T(8,128)(2,1)}, f32[128,256]{1,0:T(8,128)S(1)}, bf16[32,40,128]{2,1,0:T(8,128)(2,1)S(1)}, bf16[32,40,128]{2,1,0:T(8,128...) custom-call(bf16[10,1024,256]{2,1,0:T(8,128)(2,1)} %get-tuple-element.98.wt_ref, ...), custom_call_target="tpu_custom_call" | custom-call | flops 1000000 | bytes 1000 | tf_op jit(solution)/shard_map/attention_grads/pallas_call | solution.py:383
  67.6 0.7 collective-permute-start.20
  68.3 4.1 %collective-permute-done.16.v2b = bf16[256,640]{1,0:T(8,128)(2,1)S(1)} collective-permute-done((bf16[256,640]{1,0:T(8,128)(2,1)S(1)}, bf16[256,640]{1,0:T(8,128)(2,1)S(1)}, u32[]{:S(2)}, u32[]{:S(2)}) %collective-permute-start.16) | collective-permute-done | bytes 327712 | tf_op jit(solution)/shard_map/ppermute | solution.py:406
  72.5 1.0 collective-permute-done.20.rest_4_
  74.1 1.0 collective-permute-done.21.v3a
  75.6 12.0 %attention_grads.3 = (bf16[256,2560]{1,0:T(8,128)(2,1)}, f32[128,256]{1,0:T(8,128)}, bf16[32,40,128]{2,1,0:T(8,128)(2,1)S(1)}, bf16[32,40,128]{2,1,0:T(8,128)(2,...) custom-call(bf16[10,1024,256]{2,1,0:T(8,128)(2,1)} %get-tuple-element.94., ...), custom_call_target="tpu_custom_call", output_to_operand_aliasing={{0}: (24, {})} | custom-call | flops 1000000 | bytes 1000 | tf_op jit(solution)/shard_map/attention_grads/pallas_call | solution.py:383
  88.2 2.9 %collective-permute-done.25 = bf16[32,40,128]{2,1,0:T(8,128)(2,1)S(1)} collective-permute-done((bf16[32,40,128]{2,1,0:T(8,128)(2,1)S(1)}, bf16[32,40,128]{2,1,0:T(8,128)(2,1)S(1)}, u32[]{:S(2)}, u32[]{:S(2)}) %collective-permute-start.25) | collective-permute-done | bytes 327712 | tf_op jit(solution)/shard_map/ppermute | solution.py:402
  91.9 38.7 %all_to_all.5 = bf16[64,120,128]{2,1,0:T(8,128)(2,1)S(1)} all-to-all(bf16[64,120,128]{2,1,0:T(8,128)(2,1)S(1)} %pad_maximum_fusion), channel_id=1, replica_groups=mesh['x'=4,'zh'=2,'y'=4,'zl'=2,'core'=2] {'x','zh','y','zl'}, dimensions={0} | all-to-all | bytes 3932160 | tf_op jit(solution)/shard_map/all_to_all | solution.py:498
  (93 shorter events, 8.8 us)
Async XLA Ops:
  2.7 5.0 %collective-permute-start = (bf16[256,2560]{1,0:T(8,128)(2,1)S(1)}, bf16[256,2560]{1,0:T(8,128)(2,1)S(1)}, u32[]{:S(2)}, u32[]{:S(2)}) collective-permute-start(bf16[256,2560]{1,0:T(8,128)(2,1)S(1)} %copy-done), channel_id=1, source_target_pairs={{0,1},{1,0},{2,3},{3,2},{4,5},{5,4},{6,7},{7,6},{8,9},{9,8},{10,11... | collective-permute-start | bytes 3932168 | tf_op jit(solution)/shard_map/ppermute | solution.py:402
  2.7 52.9 %collective-permute-start.14 = (bf16[256,2560]{1,0:T(8,128)(2,1)}, bf16[256,2560]{1,0:T(8,128)(2,1)}, u32[]{:S(2)}, u32[]{:S(2)}) collective-permute-start(bf16[256,2560]{1,0:T(8,128)(2,1)} %v0.3), channel_id=1, source_target_pairs={{0,1},{1,0},{2,3},{3,2},{4,5},{5,4},{6,7},{7,6},{8,9},{9,8},{10,11... | collective-permute-start | bytes 3932168 | tf_op jit(solution)/shard_map/ppermute | solution.py:402
  3.2 18.2 %collective-permute-start.3 = (bf16[256,640]{1,0:T(8,128)(2,1)}, bf16[256,640]{1,0:T(8,128)(2,1)}, u32[]{:S(2)}, u32[]{:S(2)}) collective-permute-start(bf16[256,640]{1,0:T(8,128)(2,1)} %get-tuple-element.69), channel_id=1, source_target_pairs={{0,2},{2,0},{1,3},{3,1},{4,6},{6,4},{5,7},{7,5},{8,10},{10,8},{9,1... | collective-permute-start | bytes 983048 | tf_op jit(solution)/shard_map/ppermute | solution.py:406
  5.2 16.2 %collective-permute-start.4 = (bf16[256,640]{1,0:T(8,128)(2,1)}, bf16[256,640]{1,0:T(8,128)(2,1)}, u32[]{:S(2)}, u32[]{:S(2)}) collective-permute-start(bf16[256,640]{1,0:T(8,128)(2,1)} %get-tuple-element.70), channel_id=1, source_target_pairs={{0,2},{2,0},{1,3},{3,1},{4,6},{6,4},{5,7},{7,5},{8,10},{10,8},{9,1... | collective-permute-start | bytes 983048 | tf_op jit(solution)/shard_map/ppermute | solution.py:406
  9.2 9.0 %collective-permute-start.5 = (f32[5,64]{1,0:T(8,128)S(1)}, f32[5,64]{1,0:T(8,128)S(1)}, u32[]{:S(2)}, u32[]{:S(2)}) collective-permute-start(f32[5,64]{1,0:T(8,128)S(1)} %select_n.42), channel_id=1, source_target_pairs={{0,18},{2,16},{16,2},{18,0},{1,19},{3,17},{17,3},{19,1},{4,22},{6,... | collective-permute-start | bytes 3848 | tf_op jit(solution)/shard_map/ppermute | solution.py:410
  18.1 3.3 %collective-permute-start.7 = (bf16[256,128]{1,0:T(8,128)(2,1)S(1)}, bf16[256,128]{1,0:T(8,128)(2,1)}, u32[]{:S(2)}, u32[]{:S(2)}) collective-permute-start(bf16[256,128]{1,0:T(8,128)(2,1)S(1)} %get-tuple-element.68.l0), channel_id=1, source_target_pairs={{0,1},{1,0},{2,3},{3,2},{4,5},{5,4},{6,7},{7,6},{8,9},{9,8},{10,11... | collective-permute-start | bytes 196616 | tf_op jit(solution)/shard_map/ppermute | solution.py:402
  18.2 9.0 %copy-start.1 = (bf16[256,2560]{1,0:T(8,128)(2,1)S(1)}, bf16[256,2560]{1,0:T(8,128)(2,1)}, u32[]{:S(2)}) copy-start(bf16[256,2560]{1,0:T(8,128)(2,1)} %cot_ref.7) | copy-start | bytes 3932164
  18.2 9.0 %copy-start.2 = (bf16[128,2560]{1,0:T(8,128)(2,1)S(1)}, bf16[128,2560]{1,0:T(8,128)(2,1)}, u32[]{:S(2)}) copy-start(bf16[128,2560]{1,0:T(8,128)(2,1)} %upq_ref.7) | copy-start | bytes 1966084
  18.3 3.1 %collective-permute-start.6 = (f32[2,5,64]{2,1,0:T(8,128)S(1)}, f32[2,5,64]{2,1,0:T(8,128)S(1)}, u32[]{:S(2)}, u32[]{:S(2)}) collective-permute-start(f32[2,5,64]{2,1,0:T(8,128)S(1)} %get-tuple-element.142), channel_id=1, source_target_pairs={{0,1},{1,0},{2,3},{3,2},{4,5},{5,4},{6,7},{7,6},{8,9},{9,8},{10,11... | collective-permute-start | bytes 7688 | tf_op jit(solution)/shard_map/ppermute | solution.py:402
  21.4 4.4 %collective-permute-start.10 = (bf16[256,640]{1,0:T(8,128)(2,1)}, bf16[256,640]{1,0:T(8,128)(2,1)S(1)}, u32[]{:S(2)}, u32[]{:S(2)}) collective-permute-start(bf16[256,640]{1,0:T(8,128)(2,1)} %collective-permute-done.3.k2a), channel_id=1, source_target_pairs={{0,1},{1,0},{2,3},{3,2},{4,5},{5,4},{6,7},{7,6},{8,9},{9,8},{10,11... | collective-permute-start | bytes 983048 | tf_op jit(solution)/shard_map/ppermute | solution.py:402
  21.5 5.7 %collective-permute-start.11 = (bf16[256,640]{1,0:T(8,128)(2,1)}, bf16[256,640]{1,0:T(8,128)(2,1)}, u32[]{:S(2)}, u32[]{:S(2)}) collective-permute-start(bf16[256,640]{1,0:T(8,128)(2,1)} %collective-permute-done.4.k2b), channel_id=1, source_target_pairs={{0,1},{1,0},{2,3},{3,2},{4,5},{5,4},{6,7},{7,6},{8,9},{9,8},{10,11... | collective-permute-start | bytes 983048 | tf_op jit(solution)/shard_map/ppermute | solution.py:402
  22.0 17.9 %collective-permute-start.8 = (bf16[256,640]{1,0:T(8,128)(2,1)}, bf16[256,640]{1,0:T(8,128)(2,1)}, u32[]{:S(2)}, u32[]{:S(2)}) collective-permute-start(bf16[256,640]{1,0:T(8,128)(2,1)} %get-tuple-element.79), channel_id=1, source_target_pairs={{0,2},{2,0},{1,3},{3,1},{4,6},{6,4},{5,7},{7,5},{8,10},{10,8},{9,1... | collective-permute-start | bytes 983048 | tf_op jit(solution)/shard_map/ppermute | solution.py:406
  22.7 17.2 %collective-permute-start.9 = (bf16[256,640]{1,0:T(8,128)(2,1)}, bf16[256,640]{1,0:T(8,128)(2,1)}, u32[]{:S(2)}, u32[]{:S(2)}) collective-permute-start(bf16[256,640]{1,0:T(8,128)(2,1)} %get-tuple-element.80), channel_id=1, source_target_pairs={{0,2},{2,0},{1,3},{3,1},{4,6},{6,4},{5,7},{7,5},{8,10},{10,8},{9,1... | collective-permute-start | bytes 983048 | tf_op jit(solution)/shard_map/ppermute | solution.py:406
  26.6 27.9 %collective-permute-start.1 = (bf16[256,768]{1,0:T(8,128)(2,1)}, bf16[256,768]{1,0:T(8,128)(2,1)}, u32[]{:S(2)}, u32[]{:S(2)}) collective-permute-start(bf16[256,768]{1,0:T(8,128)(2,1)} %pad_maximum_fusion.2), channel_id=1, source_target_pairs={{0,2},{2,0},{1,3},{3,1},{4,6},{6,4},{5,7},{7,5},{8,10},{10,8},{9,1... | collective-permute-start | bytes 1179656 | tf_op jit(solution)/shard_map/ppermute | solution.py:406
  30.7 9.9 %copy-start.15 = (bf16[256,640]{1,0:T(8,128)(2,1)S(1)}, bf16[256,640]{1,0:T(8,128)(2,1)}, u32[]{:S(2)}) copy-start(bf16[256,640]{1,0:T(8,128)(2,1)} %get-tuple-element.135) | copy-start | bytes 983044
  39.9 1.9 %collective-permute-start.12 = (bf16[256,640]{1,0:T(8,128)(2,1)}, bf16[256,640]{1,0:T(8,128)(2,1)S(1)}, u32[]{:S(2)}, u32[]{:S(2)}) collective-permute-start(bf16[256,640]{1,0:T(8,128)(2,1)} %collective-permute-done.8.k2a), channel_id=1, source_target_pairs={{0,1},{1,0},{2,3},{3,2},{4,5},{5,4},{6,7},{7,6},{8,9},{9,8},{10,11... | collective-permute-start | bytes 983048 | tf_op jit(solution)/shard_map/ppermute | solution.py:402
  40.0 2.3 %collective-permute-start.13 = (bf16[256,640]{1,0:T(8,128)(2,1)}, bf16[256,640]{1,0:T(8,128)(2,1)S(1)}, u32[]{:S(2)}, u32[]{:S(2)}) collective-permute-start(bf16[256,640]{1,0:T(8,128)(2,1)} %collective-permute-done.9.k2b), channel_id=1, source_target_pairs={{0,1},{1,0},{2,3},{3,2},{4,5},{5,4},{6,7},{7,6},{8,9},{9,8},{10,11... | collective-permute-start | bytes 983048 | tf_op jit(solution)/shard_map/ppermute | solution.py:402
  40.5 13.9 %collective-permute-start.2 = (bf16[256,640]{1,0:T(8,128)(2,1)S(1)}, bf16[256,640]{1,0:T(8,128)(2,1)S(1)}, u32[]{:S(2)}, u32[]{:S(2)}) collective-permute-start(bf16[256,640]{1,0:T(8,128)(2,1)S(1)} %copy-done.15), channel_id=1, source_target_pairs={{0,2},{2,0},{1,3},{3,1},{4,6},{6,4},{5,7},{7,5},{8,10},{10,8},{9,1... | collective-permute-start | bytes 983048 | tf_op jit(solution)/shard_map/ppermute | solution.py:406
  42.3 12.6 %copy-start.14 = (bf16[256,640]{1,0:T(8,128)(2,1)S(1)}, bf16[256,640]{1,0:T(8,128)(2,1)}, u32[]{:S(2)}) copy-start(bf16[256,640]{1,0:T(8,128)(2,1)} %get-tuple-element.96) | copy-start | bytes 983044
  42.3 13.2 %copy-start.13 = (bf16[256,640]{1,0:T(8,128)(2,1)S(1)}, bf16[256,640]{1,0:T(8,128)(2,1)}, u32[]{:S(2)}) copy-start(bf16[256,640]{1,0:T(8,128)(2,1)} %get-tuple-element.97) | copy-start | bytes 983044
  42.3 14.7 %copy-start.11 = (bf16[256,640]{1,0:T(8,128)(2,1)S(1)}, bf16[256,640]{1,0:T(8,128)(2,1)}, u32[]{:S(2)}) copy-start(bf16[256,640]{1,0:T(8,128)(2,1)} %copy-done.9) | copy-start | bytes 983044
  54.4 2.6 %collective-permute-start.17 = (bf16[256,768]{1,0:T(8,128)(2,1)}, bf16[256,768]{1,0:T(8,128)(2,1)S(1)}, u32[]{:S(2)}, u32[]{:S(2)}) collective-permute-start(bf16[256,768]{1,0:T(8,128)(2,1)} %collective-permute-done.1.v2a.l2), channel_id=1, source_target_pairs={{0,1},{1,0},{2,3},{3,2},{4,5},{5,4},{6,7},{7,6},{8,9},{9,8},{10,11... | collective-permute-start | bytes 1179656 | tf_op jit(solution)/shard_map/ppermute | solution.py:402
  54.4 2.6 %collective-permute-start.18 = (bf16[256,640]{1,0:T(8,128)(2,1)S(1)}, bf16[256,640]{1,0:T(8,128)(2,1)S(1)}, u32[]{:S(2)}, u32[]{:S(2)}) collective-permute-start(bf16[256,640]{1,0:T(8,128)(2,1)S(1)} %collective-permute-done.2.v2b), channel_id=1, source_target_pairs={{0,1},{1,0},{2,3},{3,2},{4,5},{5,4},{6,7},{7,6},{8,9},{9,8},{10,11... | collective-permute-start | bytes 983048 | tf_op jit(solution)/shard_map/ppermute | solution.py:402
  54.9 2.0 %collective-permute-start.19 = (bf16[2,256,128]{2,1,0:T(8,128)(2,1)S(1)}, bf16[2,256,128]{2,1,0:T(8,128)(2,1)S(1)}, u32[]{:S(2)}, u32[]{:S(2)}) collective-permute-start(bf16[2,256,128]{2,1,0:T(8,128)(2,1)S(1)} %get-tuple-element.107), channel_id=1, source_target_pairs={{0,1},{1,0},{2,3},{3,2},{4,5},{5,4},{6,7},{7,6},{8,9},{9,8},{10,11... | collective-permute-start | bytes 393224 | tf_op jit(solution)/shard_map/ppermute | solution.py:402
  54.9 13.4 %collective-permute-start.15 = (bf16[256,640]{1,0:T(8,128)(2,1)S(1)}, bf16[256,640]{1,0:T(8,128)(2,1)S(1)}, u32[]{:S(2)}, u32[]{:S(2)}) collective-permute-start(bf16[256,640]{1,0:T(8,128)(2,1)S(1)} %copy-done.14), channel_id=1, source_target_pairs={{0,2},{2,0},{1,3},{3,1},{4,6},{6,4},{5,7},{7,5},{8,10},{10,8},{9,1... | collective-permute-start | bytes 983048 | tf_op jit(solution)/shard_map/ppermute | solution.py:406
  55.6 16.9 %collective-permute-start.16 = (bf16[256,640]{1,0:T(8,128)(2,1)S(1)}, bf16[256,640]{1,0:T(8,128)(2,1)S(1)}, u32[]{:S(2)}, u32[]{:S(2)}) collective-permute-start(bf16[256,640]{1,0:T(8,128)(2,1)S(1)} %copy-done.13), channel_id=1, source_target_pairs={{0,2},{2,0},{1,3},{3,1},{4,6},{6,4},{5,7},{7,5},{8,10},{10,8},{9,1... | collective-permute-start | bytes 983048 | tf_op jit(solution)/shard_map/ppermute | solution.py:406
  67.6 6.4 %collective-permute-start.23 = (bf16[32,40,128]{2,1,0:T(8,128)(2,1)S(1)}, bf16[32,40,128]{2,1,0:T(8,128)(2,1)S(1)}, u32[]{:S(2)}, u32[]{:S(2)}) collective-permute-start(bf16[32,40,128]{2,1,0:T(8,128)(2,1)S(1)} %get-tuple-element.113), channel_id=1, source_target_pairs={{0,1},{1,0},{2,3},{3,2},{4,5},{5,4},{6,7},{7,6},{8,9},{9,8},{10,11... | collective-permute-start | bytes 983048 | tf_op jit(solution)/shard_map/ppermute | solution.py:402
  67.6 5.8 %collective-permute-start.20 = (bf16[256,128]{1,0:T(8,128)(2,1)S(1)}, bf16[256,128]{1,0:T(8,128)(2,1)S(1)}, u32[]{:S(2)}, u32[]{:S(2)}) collective-permute-start(bf16[256,128]{1,0:T(8,128)(2,1)S(1)} %get-tuple-element.109), channel_id=1, source_target_pairs={{0,2},{2,0},{1,3},{3,1},{4,6},{6,4},{5,7},{7,5},{8,10},{10,8},{9,1... | collective-permute-start | bytes 196616 | tf_op jit(solution)/shard_map/ppermute | solution.py:406
  73.5 1.6 %collective-permute-start.21 = (bf16[256,640]{1,0:T(8,128)(2,1)S(1)}, bf16[256,640]{1,0:T(8,128)(2,1)S(1)}, u32[]{:S(2)}, u32[]{:S(2)}) collective-permute-start(bf16[256,640]{1,0:T(8,128)(2,1)S(1)} %collective-permute-done.15.v2a), channel_id=1, source_target_pairs={{0,1},{1,0},{2,3},{3,2},{4,5},{5,4},{6,7},{7,6},{8,9},{9,8},{10,11... | collective-permute-start | bytes 983048 | tf_op jit(solution)/shard_map/ppermute | solution.py:402
  73.5 2.1 %collective-permute-start.22 = (bf16[256,640]{1,0:T(8,128)(2,1)S(1)}, bf16[256,640]{1,0:T(8,128)(2,1)S(1)}, u32[]{:S(2)}, u32[]{:S(2)}) collective-permute-start(bf16[256,640]{1,0:T(8,128)(2,1)S(1)} %collective-permute-done.16.v2b), channel_id=1, source_target_pairs={{0,1},{1,0},{2,3},{3,2},{4,5},{5,4},{6,7},{7,6},{8,9},{9,8},{10,11... | collective-permute-start | bytes 983048 | tf_op jit(solution)/shard_map/ppermute | solution.py:402
  87.6 3.8 %collective-permute-start.24 = (bf16[64,80,128]{2,1,0:T(8,128)(2,1)}, bf16[64,80,128]{2,1,0:T(8,128)(2,1)S(1)}, u32[]{:S(2)}, u32[]{:S(2)}) collective-permute-start(bf16[64,80,128]{2,1,0:T(8,128)(2,1)} %get-tuple-element.123), channel_id=1, source_target_pairs={{0,1},{1,0},{2,3},{3,2},{4,5},{5,4},{6,7},{7,6},{8,9},{9,8},{10,11... | collective-permute-start | bytes 3932168 | tf_op jit(solution)/shard_map/ppermute | solution.py:402
  87.8 3.3 %collective-permute-start.25 = (bf16[32,40,128]{2,1,0:T(8,128)(2,1)S(1)}, bf16[32,40,128]{2,1,0:T(8,128)(2,1)S(1)}, u32[]{:S(2)}, u32[]{:S(2)}) collective-permute-start(bf16[32,40,128]{2,1,0:T(8,128)(2,1)S(1)} %get-tuple-element.126), channel_id=1, source_target_pairs={{0,1},{1,0},{2,3},{3,2},{4,5},{5,4},{6,7},{7,6},{8,9},{9,8},{10,11... | collective-permute-start | bytes 983048 | tf_op jit(solution)/shard_map/ppermute | solution.py:402
  (12 other events, 34.0 us)
